TPU v7x, 128 devices: a whole 4x4x4 slice. The times are simulated.
128 devices in a mesh: user: 16 (over x, y_lo, core), cand: 8 (over z, y_hi).
Axes of the slice: x: 4, y: 4 (y_hi: 2, y_lo: 2; y = y_hi * 2 + y_lo), z: 4, core: 2. Of those that a mesh axis runs over, the one named last changes fastest.
Arguments:
- pooled: bfloat16 [16, 32, 1024, 1024], P('user', None, 'cand'), may hold values from -6 to 6
- cand_feats: bfloat16 [65536, 1024], P(('user', 'cand')), may hold values from -6 to 6
- hist_len: int32 [32], P('user'), may hold values from 1 to 1024, 16384 in all
- cand_user: int32 [65536], P(('user', 'cand')), may hold values from 0 to 31, as said below
- w_in: bfloat16 [1024, 4096], replicated, may hold values from -0.1875 to 0.1875
- w_out: bfloat16 [1024, 1024], replicated, may hold values from -0.1875 to 0.1875
Outputs:
- hist_out: bfloat16 [32, 1024, 1024], P('user', 'cand')
- cand_out: bfloat16 [65536, 1024], P(('user', 'cand'))
Inputs may be any that keep to these rules, and one draw needn't show every extreme that they name: `hist_len`: the lengths sum to 16384, and the longest is 1024. `cand_user`: candidate row r belongs to one of the 2 users numbered from (r // 4096) * 2 on.
All inputs are finite; a program needn't handle non-finite values. No bound on the sum of `hist_len` on one device may be relied on, other than what follows from the above.
Results may differ from a plain program's by a relative error of at most 0.022.
Values may be sent and summed in bfloat16 or wider, within the bound.
No kernel may reach another device: no remote copies, remote signals or barrier semaphores. Data moves between devices by JAX's collectives and lax.ppermute only.
A program may use at most 128 MiB of HBM per device.

v0:
```python
import functools

import jax
import jax.numpy as jnp
from jax import lax
from jax.experimental import pallas as pl
from jax.experimental.pallas import tpu as pltpu
from jax.sharding import PartitionSpec as P

F32 = jnp.float32
BF16 = jnp.bfloat16
HEADS = 8
HD = 128
D = 1024
SLOTS = 128
ROWS = 512
NX, NZ = 4, 4
WINDOW = 320
HALF_SCALE = 0.5 / (HD**0.5)
VMEM = 20 * 1024 * 1024
GROUP = 512
SHIFTS = (0, -1, 1, 2)


def silu(v):
    half = v * 0.5
    return half + half * jnp.tanh(half)


def layer_norm(rows):
    mean = jnp.mean(rows, axis=-1, keepdims=True)
    centered = rows - mean
    var = jnp.mean(centered * centered, axis=-1, keepdims=True)
    return centered * lax.rsqrt(var + 1e-05)


def mm(a, b):
    return jnp.dot(a, b, preferred_element_type=F32)


def weights_of(queries, keys):
    s = lax.dot_general(queries, keys, (((1,), (1,)), ((), ())), preferred_element_type=F32)
    half = s * HALF_SCALE
    return half + half * jnp.tanh(half)


def in_vmem(array):
    return pltpu.with_memory_space_constraint(array, pltpu.VMEM)


def kernel_call(body, name, arrays, out_shape, scratch, scalars=None, aliases=None):
    vmem = pl.BlockSpec(memory_space=pltpu.VMEM)
    in_specs, args = [vmem] * len(arrays), [in_vmem(array) for array in arrays]
    if scalars is not None:
        in_specs = [pl.BlockSpec(memory_space=pltpu.SMEM)] + in_specs
        args = [scalars] + args
    return pl.pallas_call(
        body,
        in_specs=in_specs,
        out_specs=[vmem] * len(out_shape),
        out_shape=out_shape,
        scratch_shapes=scratch,
        input_output_aliases=aliases or {},
        compiler_params=pltpu.CompilerParams(vmem_limit_bytes=VMEM),
        cost_estimate=pl.CostEstimate(flops=10**6, bytes_accessed=1 << 16, transcendentals=0),
        name=name,
    )(*args)


def cand_kernel(owner_ref, feats_ref, w_ref, xs_ref, u_ref, q_ref, a_ref):
    second = owner_ref[...].astype(F32)
    r_from = lax.broadcasted_iota(jnp.int32, (ROWS, ROWS), 0)
    r_to = lax.broadcasted_iota(jnp.int32, (ROWS, ROWS), 1)
    upper = jnp.where(r_from <= r_to, 1.0, 0.0).astype(BF16)
    ones_before = mm(jnp.broadcast_to(second, (8, ROWS)).astype(BF16), upper)[:1]
    index = lax.broadcasted_iota(jnp.int32, (1, ROWS), 1).astype(F32)
    n_first = ROWS - jnp.sum(second, axis=1, keepdims=True)
    place = jnp.where(second > 0.5, n_first + ones_before - 1.0, index - ones_before)
    onehot = jnp.where(r_from == place.astype(jnp.int32), 1.0, 0.0).astype(BF16)
    x = layer_norm(feats_ref[...].astype(F32)).astype(BF16)
    xs_ref[...] = mm(onehot, x).astype(BF16)

    @pl.loop(0, D // GROUP)
    def _(g):
        cols = lambda n: pl.ds(pl.multiple_of(n * D + g * GROUP, GROUP), GROUP)
        u, v, q, k = (silu(mm(xs_ref[...], w_ref[:, cols(n)])).astype(BF16) for n in range(4))
        u_ref[:, cols(0)] = u
        q_ref[:, cols(0)] = q
        prod = q.astype(F32) * k.astype(F32)
        for h in range(GROUP // HD):
            hc = slice(h * HD, (h + 1) * HD)
            half = jnp.sum(prod[:, hc], axis=-1, keepdims=True) * HALF_SCALE
            own = (half + half * jnp.tanh(half)).astype(BF16).astype(F32)
            out_cols = pl.ds(pl.multiple_of(g * GROUP + h * HD, HD), HD)
            a_ref[:, out_cols] = own * v[:, hc].astype(F32)


def cand_project(owner_row, feats, w_in):
    rows = jax.ShapeDtypeStruct((ROWS, D), BF16)
    out_shape = [rows, rows, rows, jax.ShapeDtypeStruct((ROWS, D), F32)]
    return kernel_call(cand_kernel, "cand_project", [owner_row, feats, w_in], out_shape, [])


def absorb_kernel(plan, scal_ref, *refs):
    users, first, final = plan["users"], plan["first"], plan["final"]
    refs = list(refs)
    take = lambda n: [refs.pop(0) for _ in range(n)]
    keys = [(user, shift, e, ref) for (user, shift, es), ref in zip(plan["items"], take(len(plan["items"]))) for e in es]
    w_ref, q_ref, a_ref = take(3)
    if first:
        own_ref = dict(zip(users, take(len(users))))
    else:
        qh_ref = dict(zip(users, take(len(users))))
        ah_ref = dict(zip(users, take(len(users))))
    if final:
        uh_ref = dict(zip(users, take(len(users))))
        xh_ref = dict(zip(users, take(len(users))))
        u_ref, xs_ref, owner_ref, wo_ref = take(4)
        hist_ref, cand_ref = take(2)
    else:
        take(1)
        if first:
            ah_ref = dict(zip(users, take(len(users))))
            qh_ref = dict(zip(users, take(len(users))))
            uh_ref = dict(zip(users, take(len(users))))
        else:
            take(len(users))
    k_scr, v_scr = take(2)
    if final:
        (y_scr,) = take(1)
    row_iota = lax.broadcasted_iota(jnp.int32, (SLOTS, 1), 0)
    ahead = lax.broadcasted_iota(jnp.int32, (SLOTS, SLOTS), 0) - lax.broadcasted_iota(
        jnp.int32, (SLOTS, SLOTS), 1
    )
    for user in users:
        length = scal_ref[user, 0]
        row_lo = scal_ref[user, 1]
        row_hi = scal_ref[user, 2]
        my_off = scal_ref[user, 3]
        mine_keys = [(shift, e, ref) for (u, shift, e, ref) in keys if u == user]
        offs = [scal_ref[user, 4 + 2 * SHIFTS.index(shift) + e] for shift, e, _ in mine_keys]
        n_keys = SLOTS * len(offs)

        @pl.loop(0, D // GROUP)
        def _(g):
            cols = lambda n: pl.ds(pl.multiple_of(n * D + g * GROUP, GROUP), GROUP)
            if first:
                x_own = own_ref[user][...]
                qh_ref[user][:, cols(0)] = silu(mm(x_own, w_ref[:, cols(2)])).astype(BF16)
                uh_ref[user][:, cols(0)] = silu(mm(x_own, w_ref[:, cols(0)])).astype(BF16)
                ah_ref[user][:, cols(0)] = jnp.zeros((SLOTS, GROUP), F32)
            x = jnp.concatenate([ref[min(e, ref.shape[0] - 1)] for _, e, ref in mine_keys], axis=0)
            k_scr[:n_keys, :] = silu(mm(x, w_ref[:, cols(3)])).astype(BF16)
            v = silu(mm(x, w_ref[:, cols(1)])).astype(BF16)
            for i, off in enumerate(offs):
                piece = v[i * SLOTS : (i + 1) * SLOTS]
                piece = jnp.where(row_iota < length - off, piece, jnp.zeros_like(piece))
                v_scr[i * SLOTS : (i + 1) * SLOTS, :] = piece

            def attend(start, count):
                rows = pl.ds(start, count)
                index = start + lax.broadcasted_iota(jnp.int32, (count, 1), 0)
                mine = (index >= row_lo) & (index < row_hi)
                for h in range(GROUP // HD):
                    hc = slice(h * HD, (h + 1) * HD)
                    oc = pl.ds(pl.multiple_of(g * GROUP + h * HD, HD), HD)
                    q = jnp.concatenate([q_ref[rows, oc], qh_ref[user][:, oc]], axis=0)
                    total = None
                    for n in range(0, n_keys, 2 * SLOTS):
                        w = weights_of(q, k_scr[n : n + 2 * SLOTS, hc])
                        parts = []
                        for i in range(2):
                            part = w[count:, i * SLOTS : (i + 1) * SLOTS]
                            seen = ahead >= offs[n // SLOTS + i] - my_off
                            parts.append(jnp.where(seen, part, 0.0).astype(BF16))
                        w = jnp.concatenate([w[:count].astype(BF16), jnp.concatenate(parts, axis=1)], axis=0)
                        pv = mm(w, v_scr[n : n + 2 * SLOTS, hc])
                        total = pv if total is None else total + pv
                    a_ref[rows, oc] += jnp.where(mine, total[:count], 0.0)
                    ah_ref[user][:, oc] += total[count:]

            start = jnp.minimum((row_lo // 16) * 16, ROWS - WINDOW)
            narrow = row_hi <= start + WINDOW

            @pl.when(narrow)
            def _():
                attend(pl.multiple_of(start, 16), WINDOW)

            @pl.when(jnp.logical_not(narrow))
            def _():
                attend(0, ROWS)

    if final:
        n_hist = SLOTS * len(users)
        for i, user in enumerate(users):
            y = layer_norm(ah_ref[user][...]) * uh_ref[user][...].astype(F32)
            y_scr[i * SLOTS : (i + 1) * SLOTS, :] = y.astype(BF16)

        @pl.loop(0, ROWS // SLOTS)
        def _(n):
            rows = pl.ds(pl.multiple_of(n * SLOTS, SLOTS), SLOTS)
            y = layer_norm(a_ref[rows, :]) * u_ref[rows, :].astype(F32)
            y_scr[pl.ds(pl.multiple_of(n_hist + n * SLOTS, SLOTS), SLOTS), :] = y.astype(BF16)

        r_row = lax.broadcasted_iota(jnp.int32, (ROWS, ROWS), 0)
        r_col = lax.broadcasted_iota(jnp.int32, (ROWS, ROWS), 1)
        second = owner_ref[...].astype(F32)
        lower = jnp.where(r_col <= r_row, 1.0, 0.0).astype(BF16)
        ones_before = mm(lower, jnp.broadcast_to(second, (ROWS, HD)).astype(BF16))[:, :1]
        index = lax.broadcasted_iota(jnp.int32, (ROWS, 1), 0).astype(F32)
        n_first = ROWS - jnp.sum(second, axis=0, keepdims=True)
        place = jnp.where(second > 0.5, n_first + ones_before - 1.0, index - ones_before)
        back = jnp.where(r_col == place.astype(jnp.int32), 1.0, 0.0).astype(BF16)

        @pl.loop(0, D // GROUP)
        def _(g):
            cols = pl.ds(pl.multiple_of(g * GROUP, GROUP), GROUP)
            res = mm(y_scr[...], wo_ref[:, cols])
            for i, user in enumerate(users):
                out = res[i * SLOTS : (i + 1) * SLOTS] + xh_ref[user][:, cols].astype(F32)
                keep = scal_ref[user, 3] + row_iota < scal_ref[user, 0]
                hist_ref[user, :, cols] = jnp.where(keep, out, 0.0).astype(BF16)
            done = (res[n_hist:] + xs_ref[:, cols].astype(F32)).astype(BF16)
            cand_ref[:, cols] = mm(back, done).astype(BF16)


def absorb(name, scal, items, w_in, q_cand, a_cand, first=None, state=None, final=None):
    users = tuple(sorted({item[0] for item in items}))
    plan = dict(items=tuple(item[:3] for item in items), users=users, first=first is not None, final=final is not None)
    arrays = [item[3] for item in items] + [w_in, q_cand, a_cand]
    n = len(users)
    a_at = len(arrays)
    sums = jax.ShapeDtypeStruct((SLOTS, D), F32)
    rows = jax.ShapeDtypeStruct((SLOTS, D), BF16)
    most = max(sum(len(item[2]) for item in items if item[0] == user) for user in users)
    scratch = [pltpu.VMEM((most * SLOTS, GROUP), BF16)] * 2
    out_shape = [jax.ShapeDtypeStruct((ROWS, D), F32)]
    aliases = {a_at: 0}
    if first is not None:
        arrays += [first[user] for user in users]
        out_shape += [sums] * n + [rows] * (2 * n)
    else:
        arrays += [state[user][0] for user in users]
        aliases.update({len(arrays) + 1 + i: 1 + i for i in range(n)})
        arrays += [state[user][2] for user in users]
        out_shape += [sums] * n
    if final is not None:
        arrays += [state[user][1] for user in users]
        arrays += [final["own"][user] for user in users]
        arrays += [final["u"], final["xs"], final["owner"], final["w_out"]]
        out_shape = [jax.ShapeDtypeStruct((n, SLOTS, D), BF16), jax.ShapeDtypeStruct((ROWS, D), BF16)]
        aliases = {}
        scratch.append(pltpu.VMEM((n * SLOTS + ROWS, D), BF16))
    outs = kernel_call(
        functools.partial(absorb_kernel, plan), name, arrays, out_shape, scratch, scal, aliases
    )
    if final is not None:
        return outs
    new = {}
    for i, user in enumerate(users):
        if first is not None:
            new[user] = (outs[1 + n + i], outs[1 + 2 * n + i], outs[1 + i])
        else:
            new[user] = (state[user][0], state[user][1], outs[1 + i])
    return outs[0], new


def user_perm(dx, dy, dcore):
    pairs = []
    for u in range(4 * NX):
        x, y, core = u >> 2, (u >> 1) & 1, u & 1
        pairs.append((u, (((x + dx) % NX) * 2 + (y ^ dy)) * 2 + (core ^ dcore)))
    return pairs


def cand_perm(dz, dy):
    return [(c, (((c >> 1) + dz) % NZ) * 2 + ((c & 1) ^ dy)) for c in range(2 * NZ)]


def to_user(array, dx, dy, dcore):
    return lax.ppermute(array, "user", user_perm(dx, dy, dcore))


def to_cand(array, dz, dy):
    return lax.ppermute(array, "cand", cand_perm(dz, dy))


def after(value, *others):
    return lax.optimization_barrier((value, others))[0]


def local(pooled, cand_feats, hist_len, cand_user, w_in, w_out):
    user = lax.axis_index("user")
    cand = lax.axis_index("cand")
    x, y, core = user >> 2, (user >> 1) & 1, user & 1
    z, y_hi = cand >> 1, cand & 1
    owner = cand_user - 2 * user
    n_first = ROWS - jnp.sum(owner)
    offsets = [SLOTS * (((z + dz + NZ) % NZ) * 2 + (y_hi ^ e)) for dz in SHIFTS for e in range(2)]
    scal = jnp.stack(
        [
            jnp.stack([hist_len[0], 0 * user, n_first, cand * SLOTS] + offsets),
            jnp.stack([hist_len[1], n_first, 0 * user + ROWS, cand * SLOTS] + offsets),
        ]
    ).astype(jnp.int32)

    tables = pooled.reshape(NX, 2, 2, 2, SLOTS, D)

    def block(j, core_at, x_at=None, y_at=None):
        at = (0 if x_at is None else x_at, 0 if y_at is None else y_at, core_at, j, 0, 0)
        size = (NX if x_at is None else 1, 2 if y_at is None else 1, 1, 1, SLOTS, D)
        return lax.dynamic_slice(tables, at, size).reshape(size[0], size[1], SLOTS, D)

    def share(got, x_at=None, y_at=None):
        at = (0 if x_at is None else x_at, 0 if y_at is None else y_at, 0, 0)
        size = (NX if x_at is None else 1, 2 if y_at is None else 1, SLOTS, D)
        return lax.dynamic_slice(got, at, size)

    hop = [lax.rem(x + d, NX) for d in range(NX)]
    with jax.named_scope("sum_core"):
        pack0 = block(0, 1 - core)
        got0 = to_user(pack0, 0, 0, 1)
        tables = after(tables, pack0)
        got1 = to_user(block(1, 1 - core), 0, 0, 1)
    with jax.named_scope("sum_x_first"):
        away = [
            (block(0, core, x_at=hop[d]).astype(F32) + share(got0, x_at=hop[d]).astype(F32)).astype(BF16)[0]
            for d in range(NX)
        ]
        x0 = [to_user(away[d], d, 0, 0) for d in (1, 3, 2)]
    with jax.named_scope("sum_y_second"):
        got1 = after(got1, away)
        over = (block(1, core, y_at=1 - y).astype(F32) + share(got1, y_at=1 - y).astype(F32)).astype(BF16)
        y1 = to_user(over, 0, 1, 0)
    owner_row = after(owner.reshape(1, ROWS), over)
    xs, u_cand, q_cand, a_cand = cand_project(owner_row, cand_feats, w_in)
    with jax.named_scope("sum_x_first"):
        x0 = after(x0, xs)
        total0 = away[0].astype(F32)
        for got in x0:
            total0 = total0 + got.astype(F32)
        y0 = to_user(lax.dynamic_index_in_dim(total0, 1 - y, 0, False).astype(BF16), 0, 1, 0)
        mine0 = lax.dynamic_index_in_dim(total0, y, 0, False)
    with jax.named_scope("sum_y_second"):
        y1 = after(y1, mine0)
        away1 = []
        for d in range(NX):
            part = (
                block(1, core, x_at=hop[d], y_at=y).astype(F32)
                + share(got1, x_at=hop[d], y_at=y).astype(F32)
            )[0, 0]
            part = part + share(y1, x_at=hop[d], y_at=0).astype(F32)[0, 0]
            away1.append(part if d == 0 else part.astype(BF16))
        x1 = [to_user(away1[d], d, 0, 0) for d in (1, 3, 2)]
    with jax.named_scope("gather"):
        y0 = after(y0, away1)
        own0 = layer_norm(mine0 + y0.astype(F32)).astype(BF16)
        pair0 = jnp.stack([own0, to_cand(own0, 0, 1)])
        z0 = {-1: to_cand(pair0, 1, 0), 1: to_cand(pair0, -1, 0)}
    both = (0, 1)
    put = functools.partial(absorb, scal=scal, w_in=w_in, q_cand=q_cand)
    a_cand, state0 = put("own_first", items=[(0, 0, both, pair0)], a_cand=a_cand, first={0: own0})
    with jax.named_scope("gather"):
        x1 = after(x1, a_cand)
        total1 = away1[0]
        for got in x1:
            total1 = total1 + got.astype(F32)
        own1 = layer_norm(total1).astype(BF16)
        near1 = to_cand(own1, 0, 1)
        z0 = after(z0, own1)
        ends0 = [z0[-1][:1], z0[1][1:]]
        far0 = [to_cand(ends0[0], 1, 0), to_cand(ends0[1], -1, 0)]
        pair1 = jnp.stack([own1, after(near1, ends0)])
        z1 = {-1: to_cand(pair1, 1, 0), 1: to_cand(pair1, -1, 0)}
    a_cand, state0 = put(
        "side_first",
        items=[(0, -1, both, z0[-1]), (0, 1, both, z0[1])],
        a_cand=after(a_cand, pair1),
        state=state0,
    )
    a_cand, state1 = put("own_second", items=[(1, 0, both, pair1)], a_cand=a_cand, first={1: own1})
    with jax.named_scope("gather"):
        z1 = after(z1, a_cand)
        ends1 = [z1[-1][:1], z1[1][1:]]
        far1 = [to_cand(ends1[0], 1, 0), to_cand(ends1[1], -1, 0)]
    a_cand, state1 = put(
        "side_second",
        items=[(1, -1, both, z1[-1]), (1, 1, both, z1[1])],
        a_cand=after(a_cand, ends1),
        state=state1,
    )
    return put(
        "far_finish",
        items=[(0, 2, (0,), far0[0]), (0, 2, (1,), far0[1]), (1, 2, (0,), far1[0]), (1, 2, (1,), far1[1])],
        a_cand=a_cand,
        state={**state0, **state1},
        final=dict(
            own={0: own0, 1: own1}, u=u_cand, xs=xs, owner=owner.reshape(ROWS, 1), w_out=w_out
        ),
    )


def solution(mesh):
    placed = (
        P("user", None, "cand", None),
        P(("user", "cand"), None),
        P("user"),
        P(("user", "cand")),
        P(),
        P(),
    )
    return jax.shard_map(
        local,
        mesh=mesh,
        in_specs=placed,
        out_specs=(P("user", "cand", None), P(("user", "cand"), None)),
        check_vma=False,
    )
```

profile of v0, /device:TPU:0, one launch (start us, length us, event | category | flops | bytes accessed | tf_op | source)
XLA Modules:
  0.0 137.5 jit_solution(11119006559722014144)
XLA Ops:
  0.6 3.1 %dynamic-slice_bitcast_fusion.1 = bf16[4,2,128,1024]{3,2,1,0:T(8,128)(2,1)} fusion(bf16[4,2,2,2,128,1024]{5,4,3,2,1,0:T(8,128)(2,1)} %bitcast.81, s32[]{:T(128)S(6)} %select_n.91), kind=kLoop, calls=%fused_computation.3 | loop fusion | bytes 4194308 | tf_op jit(solution)/shard_map/sum_core/reshape | solution.py:312
  3.8 3.1 %dynamic-slice_bitcast_fusion = bf16[4,2,128,1024]{3,2,1,0:T(8,128)(2,1)} fusion(bf16[4,2,2,2,128,1024]{5,4,3,2,1,0:T(8,128)(2,1)} %bitcast.82, s32[]{:T(128)S(6)} %select_n.91), kind=kLoop, calls=%fused_computation.2 | loop fusion | bytes 4194308 | tf_op jit(solution)/shard_map/sum_core/reshape | solution.py:312
  6.9 0.5 collective-permute-start.4
  7.4 0.9 collective-permute-done
  8.3 4.2 %fusion.5 = (bf16[2,128,1024]{2,1,0:T(8,128)(2,1)}, bf16[2,128,1024]{2,1,0:T(8,128)(2,1)}, bf16[2,128,1024]{2,1,0:T(8,128)(2,1)}, bf16[2,128,1024]{2,1,0:T(8,128)(2,1)}) fusion(bf16[4,2,128,1024]{3,2,1,0:T(8,128)(2,1)} %collective-permute-done, s32[]{:T(128)S(6)} %select_n.92, s32[]{:T(128)S(6)} %select_n.93, s32[]{:T(128)S(6)} %select_n.95, ...), kind=kLoop, calls=%fused_computation.13 | loop fusion | flops 4194304 | bytes 6291476 | tf_op jit(solution)/shard_map/sum_x_first/squeeze | solution.py:327
  12.5 1.6 %collective-permute-start.1 = (bf16[2,128,1024]{2,1,0:T(8,128)(2,1)}, bf16[2,128,1024]{2,1,0:T(8,128)(2,1)}, u32[]{:S(2)}, u32[]{:S(2)}) collective-permute-start(bf16[2,128,1024]{2,1,0:T(8,128)(2,1)} %get-tuple-element.80), channel_id=1, source_target_pairs={{0,32},{8,40},{16,48},{24,56},{32,64},{40,72},{48,80},{56,88},{64,... | collective-permute-start | bytes 1572872 | tf_op jit(solution)/shard_map/sum_x_first/ppermute | solution.py:281
  14.1 1.7 %collective-permute-start.2 = (bf16[2,128,1024]{2,1,0:T(8,128)(2,1)}, bf16[2,128,1024]{2,1,0:T(8,128)(2,1)}, u32[]{:S(2)}, u32[]{:S(2)}) collective-permute-start(bf16[2,128,1024]{2,1,0:T(8,128)(2,1)} %get-tuple-element.79), channel_id=1, source_target_pairs={{0,96},{8,104},{16,112},{24,120},{32,0},{40,8},{48,16},{56,24},{64... | collective-permute-start | bytes 1572872 | tf_op jit(solution)/shard_map/sum_x_first/ppermute | solution.py:281
  15.7 1.9 %collective-permute-start.3 = (bf16[2,128,1024]{2,1,0:T(8,128)(2,1)}, bf16[2,128,1024]{2,1,0:T(8,128)(2,1)}, u32[]{:S(2)}, u32[]{:S(2)}) collective-permute-start(bf16[2,128,1024]{2,1,0:T(8,128)(2,1)} %get-tuple-element.81), channel_id=1, source_target_pairs={{0,64},{8,72},{16,80},{24,88},{32,96},{40,104},{48,112},{56,120},{... | collective-permute-start | bytes 1572872 | tf_op jit(solution)/shard_map/sum_x_first/ppermute | solution.py:281
  17.6 3.3 %fusion = bf16[4,1,128,1024]{3,2,0,1:T(8,128)(2,1)} fusion(s32[]{:T(128)S(6)} %select_n.97, bf16[4,2,2,2,128,1024]{5,4,3,2,1,0:T(8,128)(2,1)} %bitcast.84, s32[]{:T(128)S(6)} %select_n.93, bf16[4,2,128,1024]{3,2,1,0:T(8,128)(2,1)S(1)} %collective-permute-done.4), kind=kLoop, calls=%fused_computation.1 | loop fusion | flops 2097152 | bytes 3145736 | tf_op jit(solution)/shard_map/sum_y_second/convert_element_type | solution.py:333
  20.9 1.6 %collective-permute-start.6 = (bf16[4,1,128,1024]{3,2,1,0:T(8,128)(2,1)}, bf16[4,1,128,1024]{3,2,1,0:T(8,128)(2,1)}, u32[]{:S(2)}, u32[]{:S(2)}) collective-permute-start(bf16[4,1,128,1024]{3,2,1,0:T(8,128)(2,1)} %bitcast.28), channel_id=1, source_target_pairs={{0,16},{8,24},{16,0},{24,8},{32,48},{40,56},{48,32},{56,40},{64,80... | collective-permute-start | bytes 3145736 | tf_op jit(solution)/shard_map/sum_y_second/ppermute | solution.py:281
  22.5 0.7 fusion.23
  23.2 3.4 %copy-done = bf16[1024,4096]{1,0:T(8,128)(2,1)S(1)} copy-done((bf16[1024,4096]{1,0:T(8,128)(2,1)S(1)}, bf16[1024,4096]{1,0:T(8,128)(2,1)}, u32[]{:S(2)}) %copy-start) | copy-done | bytes 8388632
  26.6 1.2 copy-done.19
  27.8 7.6 %cand_project.1 = (bf16[512,1024]{1,0:T(8,128)(2,1)S(1)}, bf16[512,1024]{1,0:T(8,128)(2,1)S(1)}, bf16[512,1024]{1,0:T(8,128)(2,1)S(1)}, f32[512,1024]{1,0:T(8,128)S(1)}) custom-call(s32[1,512]{1,0:T(1,128)S(1)} %bitcast.79, bf16[512,1024]{1,0:T(8,128)(2,1)S(1)} %copy-done.19, bf16[1024,4096]{1,0:T(8,128)(2,1)S(1)} %copy-done), custom_call_target="tpu_custom_call" | custom-call | flops 1000000 | bytes 65536 | tf_op jit(solution)/shard_map/cand_project/pallas_call | solution.py:57
  35.5 4.8 %collective-permute-done.3 = bf16[2,128,1024]{2,1,0:T(8,128)(2,1)} collective-permute-done((bf16[2,128,1024]{2,1,0:T(8,128)(2,1)}, bf16[2,128,1024]{2,1,0:T(8,128)(2,1)}, u32[]{:S(2)}, u32[]{:S(2)}) %collective-permute-start.3) | collective-permute-done | bytes 524320 | tf_op jit(solution)/shard_map/sum_x_first/ppermute | solution.py:281
  40.3 1.7 %convert_add_fusion.5 = f32[2,128,1024]{2,1,0:T(8,128)S(1)} fusion(bf16[2,128,1024]{2,1,0:T(8,128)(2,1)} %collective-permute-done.3, bf16[2,128,1024]{2,1,0:T(8,128)(2,1)} %collective-permute-done.2, bf16[2,128,1024]{2,1,0:T(8,128)(2,1)} %collective-permute-done.1, bf16[2,128,1024]{2,1,0:T(8,128)(2,1)S(1)} %copy-done.31), kind=kLoop, calls=%fused_computation.12 | loop fusion | flops 1835008 | bytes 3145728 | tf_op jit(solution)/shard_map/sum_x_first/add | solution.py:341
  42.0 1.7 %collective-permute-start.5 = (bf16[128,1024]{1,0:T(8,128)(2,1)S(1)}, bf16[128,1024]{1,0:T(8,128)(2,1)S(1)}, u32[]{:S(2)}, u32[]{:S(2)}) collective-permute-start(bf16[128,1024]{1,0:T(8,128)(2,1)S(1)} %fusion.17), channel_id=1, source_target_pairs={{0,16},{8,24},{16,0},{24,8},{32,48},{40,56},{48,32},{56,40},{64,80... | collective-permute-start | bytes 786440 | tf_op jit(solution)/shard_map/sum_x_first/ppermute | solution.py:281
  43.7 3.3 %collective-permute-done.6 = bf16[4,1,128,1024]{3,2,1,0:T(8,128)(2,1)} collective-permute-done((bf16[4,1,128,1024]{3,2,1,0:T(8,128)(2,1)}, bf16[4,1,128,1024]{3,2,1,0:T(8,128)(2,1)}, u32[]{:S(2)}, u32[]{:S(2)}) %collective-permute-start.6) | collective-permute-done | bytes 1048608 | tf_op jit(solution)/shard_map/sum_y_second/ppermute | solution.py:281
  47.0 3.0 %fusion.20 = (bf16[128,1024]{1,0:T(8,128)(2,1)}, bf16[128,1024]{1,0:T(8,128)(2,1)}, bf16[128,1024]{1,0:T(8,128)(2,1)}, f32[128,1024]{1,0:T(8,128)}) fusion(bf16[4,1,128,1024]{3,2,1,0:T(8,128)(2,1)} %collective-permute-done.6, s32[]{:T(128)S(6)} %select_n.95, bf16[4,2,128,1024]{3,2,1,0:T(8,128)(2,1)S(1)} %copy-done.29, s32[]{:T(128)S(6)} %select_n.98, ...), kind=kLoop, calls=%fused_computation.42 | loop fusion | flops 3014656 | bytes 4456472 | tf_op jit(solution)/shard_map/sum_y_second/convert_element_type | solution.py:353
  50.0 1.1 collective-permute-done.5
  51.1 0.1 fusion.21
  51.2 0.2 multiply_reduce_fusion.1
  51.4 0.1 multiply_convert_fusion.1.refs_4_.refs_13_
  51.6 3.3 %collective-permute-start.7 = (bf16[128,1024]{1,0:T(8,128)(2,1)S(1)}, bf16[128,1024]{1,0:T(8,128)(2,1)}, u32[]{:S(2)}, u32[]{:S(2)}) collective-permute-start(bf16[128,1024]{1,0:T(8,128)(2,1)S(1)} %multiply_convert_fusion.1.refs_4_.refs_13_), channel_id=1, source_target_pairs={{0,1},{1,0},{2,3},{3,2},{4,5},{5,4},{6,7},{7,6},{8,9},{9,8},{10,11... | collective-permute-start | bytes 786440 | tf_op jit(solution)/shard_map/gather/ppermute | solution.py:285
  54.9 0.6 collective-permute-start.10
  55.4 2.6 %collective-permute-start.11 = (bf16[128,1024]{1,0:T(8,128)(2,1)}, bf16[128,1024]{1,0:T(8,128)(2,1)}, u32[]{:S(2)}, u32[]{:S(2)}) collective-permute-start(bf16[128,1024]{1,0:T(8,128)(2,1)} %get-tuple-element.74), channel_id=1, source_target_pairs={{0,96},{8,104},{16,112},{24,120},{32,0},{40,8},{48,16},{56,24},{64... | collective-permute-start | bytes 786440 | tf_op jit(solution)/shard_map/sum_y_second/ppermute | solution.py:281
  58.1 0.5 collective-permute-start.12
  58.6 0.6 fusion.24
  59.9 0.8 stack.83
  60.7 0.6 stack.85
  61.3 1.0 pad_maximum_fusion.refs_0_
  62.3 2.0 %collective-permute-start.8 = (bf16[2,128,1024]{2,1,0:T(8,128)(2,1)S(1)}, bf16[2,128,1024]{2,1,0:T(8,128)(2,1)S(1)}, u32[]{:S(2)}, u32[]{:S(2)}) collective-permute-start(bf16[2,128,1024]{2,1,0:T(8,128)(2,1)S(1)} %pad_maximum_fusion.refs_0_), channel_id=1, source_target_pairs={{0,2},{1,3},{2,4},{3,5},{4,6},{5,7},{6,0},{7,1},{8,10},{9,11},{10,... | collective-permute-start | bytes 1572872 | tf_op jit(solution)/shard_map/gather/ppermute | solution.py:285
  64.3 2.4 %collective-permute-start.9 = (bf16[2,128,1024]{2,1,0:T(8,128)(2,1)S(1)}, bf16[2,128,1024]{2,1,0:T(8,128)(2,1)S(1)}, u32[]{:S(2)}, u32[]{:S(2)}) collective-permute-start(bf16[2,128,1024]{2,1,0:T(8,128)(2,1)S(1)} %pad_maximum_fusion.refs_0_), channel_id=1, source_target_pairs={{0,6},{1,7},{2,0},{3,1},{4,2},{5,3},{6,4},{7,5},{8,14},{9,15},{10,... | collective-permute-start | bytes 1572872 | tf_op jit(solution)/shard_map/gather/ppermute | solution.py:285
  66.7 3.4 %copy-done.1 = bf16[1024,4096]{1,0:T(8,128)(2,1)S(1)} copy-done((bf16[1024,4096]{1,0:T(8,128)(2,1)S(1)}, bf16[1024,4096]{1,0:T(8,128)(2,1)}, u32[]{:S(2)}) %copy-start.1) | copy-done | bytes 8388632
  70.1 4.4 %own_first.1 = (f32[512,1024]{1,0:T(8,128)S(1)}, f32[128,1024]{1,0:T(8,128)S(1)}, bf16[128,1024]{1,0:T(8,128)(2,1)S(1)}, bf16[128,1024]{1,0:T(8,128)(2,1)S(1)}) custom-call(s32[2,12]{1,0:T(2,128)S(1)} %pad_add_fusion.scal_ref, bf16[2,128,1024]{2,1,0:T(8,128)(2,1)S(1)} %pad_maximum_fusion.refs_0_, ...), custom_call_target="tpu_custom_call", output_to_operand_aliasing={{0}: (4, {})} | custom-call | flops 1000000 | bytes 65536 | tf_op jit(solution)/shard_map/own_first/pallas_call | solution.py:57
  74.6 1.5 %fusion.22 = (f32[128]{0:T(128)S(1)}, f32[128,1024]{1,0:T(8,128)S(1)}) fusion(bf16[128,1024]{1,0:T(8,128)(2,1)} %collective-permute-done.12, bf16[128,1024]{1,0:T(8,128)(2,1)} %collective-permute-done.11, f32[128,1024]{1,0:T(8,128)S(1)} %copy-done.30, bf16[128,1024]{1,0:T(8,128)(2,1)} %collective-permute-done.10), kind=kLoop, calls=%fused_computation.50 | loop fusion | flops 917376 | bytes 1835520 | tf_op jit(solution)/shard_map/gather/reduce_sum | solution.py:31
  76.1 0.2 multiply_reduce_fusion
  76.3 0.1 multiply_convert_fusion.refs_4_.refs_14_
  76.4 2.1 %collective-permute-start.15 = (bf16[128,1024]{1,0:T(8,128)(2,1)S(1)}, bf16[128,1024]{1,0:T(8,128)(2,1)S(1)}, u32[]{:S(2)}, u32[]{:S(2)}) collective-permute-start(bf16[128,1024]{1,0:T(8,128)(2,1)S(1)} %multiply_convert_fusion.refs_4_.refs_14_), channel_id=1, source_target_pairs={{0,1},{1,0},{2,3},{3,2},{4,5},{5,4},{6,7},{7,6},{8,9},{9,8},{10,11... | collective-permute-start | bytes 786440 | tf_op jit(solution)/shard_map/gather/ppermute | solution.py:285
  78.6 0.1 fusion.25
  78.7 0.7 slice.20
  79.4 0.7 slice.21
  80.2 4.2 %collective-permute-done.15 = bf16[128,1024]{1,0:T(8,128)(2,1)S(1)} collective-permute-done((bf16[128,1024]{1,0:T(8,128)(2,1)S(1)}, bf16[128,1024]{1,0:T(8,128)(2,1)S(1)}, u32[]{:S(2)}, u32[]{:S(2)}) %collective-permute-start.15) | collective-permute-done | bytes 262176 | tf_op jit(solution)/shard_map/gather/ppermute | solution.py:285
  84.4 0.1 collective-permute-start.16
  84.5 3.2 %collective-permute-start.17 = (bf16[2,128,1024]{2,1,0:T(8,128)(2,1)S(1)}, bf16[2,128,1024]{2,1,0:T(8,128)(2,1)S(1)}, u32[]{:S(2)}, u32[]{:S(2)}) collective-permute-start(bf16[2,128,1024]{2,1,0:T(8,128)(2,1)S(1)} %pad_maximum_fusion.1.refs_0_), channel_id=1, source_target_pairs={{0,6},{1,7},{2,0},{3,1},{4,2},{5,3},{6,4},{7,5},{8,14},{9,15},{10,... | collective-permute-start | bytes 1572872 | tf_op jit(solution)/shard_map/gather/ppermute | solution.py:285
  87.7 3.2 %collective-permute-start.14 = (bf16[1,128,1024]{2,1,0:T(8,128)(2,1)}, bf16[1,128,1024]{2,1,0:T(8,128)(2,1)}, u32[]{:S(2)}, u32[]{:S(2)}) collective-permute-start(bf16[1,128,1024]{2,1,0:T(8,128)(2,1)} %slice.21), channel_id=1, source_target_pairs={{0,6},{1,7},{2,0},{3,1},{4,2},{5,3},{6,4},{7,5},{8,14},{9,15},{10,... | collective-permute-start | bytes 786440 | tf_op jit(solution)/shard_map/gather/ppermute | solution.py:285
  91.0 6.3 %side_first.1 = (f32[512,1024]{1,0:T(8,128)S(1)}, f32[128,1024]{1,0:T(8,128)S(1)}) custom-call(s32[2,12]{1,0:T(2,128)S(1)} %pad_add_fusion.scal_ref, bf16[2,128,1024]{2,1,0:T(8,128)(2,1)S(1)} %collective-permute-done.8.refs_0_, bf16[2,128,1024]{2,1,0:T(8,128)(2,1)S(1)} %collective-permute-done.9.refs_1_, ...), custom_call_target="tpu_custom_call", output_to_operand_aliasing={{0}: (5, {}), {1}: (7, {})} | custom-call | flops 1000000 | bytes 65536 | tf_op jit(solution)/shard_map/side_first/pallas_call | solution.py:57
  97.3 4.4 %own_second.1 = (f32[512,1024]{1,0:T(8,128)S(1)}, f32[128,1024]{1,0:T(8,128)S(1)}, bf16[128,1024]{1,0:T(8,128)(2,1)S(1)}, bf16[128,1024]{1,0:T(8,128)(2,1)S(1)}) custom-call(s32[2,12]{1,0:T(2,128)S(1)} %pad_add_fusion.scal_ref, bf16[2,128,1024]{2,1,0:T(8,128)(2,1)S(1)} %pad_maximum_fusion.1.refs_0_, ...), custom_call_target="tpu_custom_call", output_to_operand_aliasing={{0}: (4, {})} | custom-call | flops 1000000 | bytes 65536 | tf_op jit(solution)/shard_map/own_second/pallas_call | solution.py:57
  101.8 0.8 copy-done.8
  102.6 0.7 copy-done.16
  103.3 0.7 copy-done.26
  104.0 0.8 slice.22
  104.8 0.1 copy-done.12
  104.9 0.8 copy-done.10
  105.7 0.7 slice.23
  106.4 3.2 %collective-permute-start.19 = (bf16[1,128,1024]{2,1,0:T(8,128)(2,1)}, bf16[1,128,1024]{2,1,0:T(8,128)(2,1)}, u32[]{:S(2)}, u32[]{:S(2)}) collective-permute-start(bf16[1,128,1024]{2,1,0:T(8,128)(2,1)} %slice.23), channel_id=1, source_target_pairs={{0,6},{1,7},{2,0},{3,1},{4,2},{5,3},{6,4},{7,5},{8,14},{9,15},{10,... | collective-permute-start | bytes 786440 | tf_op jit(solution)/shard_map/gather/ppermute | solution.py:285
  109.6 0.9 copy.24.refs_17_
  110.5 3.4 %copy-done.2 = bf16[1024,4096]{1,0:T(8,128)(2,1)S(1)} copy-done((bf16[1024,4096]{1,0:T(8,128)(2,1)S(1)}, bf16[1024,4096]{1,0:T(8,128)(2,1)}, u32[]{:S(2)}) %copy-start.2) | copy-done | bytes 8388632
  113.9 1.0 copy-done.9
  114.9 1.0 copy-done.11
  116.0 1.0 copy-done.13
  117.0 0.9 copy-done.17
  118.0 6.3 %side_second.1 = (f32[512,1024]{1,0:T(8,128)S(1)}, f32[128,1024]{1,0:T(8,128)S(1)}) custom-call(s32[2,12]{1,0:T(2,128)S(1)} %pad_add_fusion.scal_ref, bf16[2,128,1024]{2,1,0:T(8,128)(2,1)S(1)} %copy-done.11, bf16[2,128,1024]{2,1,0:T(8,128)(2,1)S(1)} %copy-done.13, bf16[1024,4096]{1,0:T(8,128)(2,1)S(1)} %copy-done.2, ...), custom_call_target="tpu_custom_call", output_to_operand_aliasing={{0}: (5, {}), {1}: (7, {})} | custom-call | flops 1000000 | bytes 65536 | tf_op jit(solution)/shard_map/side_second/pallas_call | solution.py:57
  124.5 13.1 %far_finish.1 = (bf16[2,128,1024]{2,1,0:T(8,128)(2,1)}, bf16[512,1024]{1,0:T(8,128)(2,1)}) custom-call(s32[2,12]{1,0:T(2,128)S(1)} %pad_add_fusion.scal_ref, bf16[1,128,1024]{2,1,0:T(8,128)(2,1)} %collective-permute-done.13.refs_0_, bf16[1,128,1024]{2,1,0:T(8,128)(2,1)} %collective-permute-done.14.refs_1_, ...), custom_call_target="tpu_custom_call" | custom-call | flops 1000000 | bytes 65536 | tf_op jit(solution)/shard_map/far_finish/pallas_call | solution.py:57
  (80 shorter events, 0.3 us)
Async XLA Ops:
  3.8 4.5 %collective-permute-start = (bf16[4,2,128,1024]{3,2,1,0:T(8,128)(2,1)}, bf16[4,2,128,1024]{3,2,1,0:T(8,128)(2,1)}, u32[]{:S(2)}, u32[]{:S(2)}) collective-permute-start(bf16[4,2,128,1024]{3,2,1,0:T(8,128)(2,1)} %dynamic-slice_bitcast_fusion.1), channel_id=1, source_target_pairs={{0,8},{8,0},{16,24},{24,16},{32,40},{40,32},{48,56},{56,48},{64,72... | collective-permute-start | bytes 6291464 | tf_op jit(solution)/shard_map/sum_core/ppermute | solution.py:281
  6.9 10.8 %collective-permute-start.4 = (bf16[4,2,128,1024]{3,2,1,0:T(8,128)(2,1)}, bf16[4,2,128,1024]{3,2,1,0:T(8,128)(2,1)S(1)}, u32[]{:S(2)}, u32[]{:S(2)}) collective-permute-start(bf16[4,2,128,1024]{3,2,1,0:T(8,128)(2,1)} %dynamic-slice_bitcast_fusion), channel_id=1, source_target_pairs={{0,8},{8,0},{16,24},{24,16},{32,40},{40,32},{48,56},{56,48},{64,72... | collective-permute-start | bytes 6291464 | tf_op jit(solution)/shard_map/sum_core/ppermute | solution.py:281
  12.5 10.0 %copy-start.32 = (s32[512]{0:T(512)S(1)}, s32[512]{0:T(512)}, u32[]{:S(2)}) copy-start(s32[512]{0:T(512)} %param.9) | copy-start | bytes 6148
  12.5 23.0 %collective-permute-start.1 = (bf16[2,128,1024]{2,1,0:T(8,128)(2,1)}, bf16[2,128,1024]{2,1,0:T(8,128)(2,1)}, u32[]{:S(2)}, u32[]{:S(2)}) collective-permute-start(bf16[2,128,1024]{2,1,0:T(8,128)(2,1)} %get-tuple-element.80), channel_id=1, source_target_pairs={{0,32},{8,40},{16,48},{24,56},{32,64},{40,72},{48,80},{56,88},{64,... | collective-permute-start | bytes 1572872 | tf_op jit(solution)/shard_map/sum_x_first/ppermute | solution.py:281
  14.1 21.4 %collective-permute-start.2 = (bf16[2,128,1024]{2,1,0:T(8,128)(2,1)}, bf16[2,128,1024]{2,1,0:T(8,128)(2,1)}, u32[]{:S(2)}, u32[]{:S(2)}) collective-permute-start(bf16[2,128,1024]{2,1,0:T(8,128)(2,1)} %get-tuple-element.79), channel_id=1, source_target_pairs={{0,96},{8,104},{16,112},{24,120},{32,0},{40,8},{48,16},{56,24},{64... | collective-permute-start | bytes 1572872 | tf_op jit(solution)/shard_map/sum_x_first/ppermute | solution.py:281
  15.7 24.6 %collective-permute-start.3 = (bf16[2,128,1024]{2,1,0:T(8,128)(2,1)}, bf16[2,128,1024]{2,1,0:T(8,128)(2,1)}, u32[]{:S(2)}, u32[]{:S(2)}) collective-permute-start(bf16[2,128,1024]{2,1,0:T(8,128)(2,1)} %get-tuple-element.81), channel_id=1, source_target_pairs={{0,64},{8,72},{16,80},{24,88},{32,96},{40,104},{48,112},{56,120},{... | collective-permute-start | bytes 1572872 | tf_op jit(solution)/shard_map/sum_x_first/ppermute | solution.py:281
  17.6 5.6 %copy-start.28 = (bf16[4,2,128,1024]{3,2,1,0:T(8,128)(2,1)}, bf16[4,2,128,1024]{3,2,1,0:T(8,128)(2,1)S(1)}, u32[]{:S(2)}) copy-start(bf16[4,2,128,1024]{3,2,1,0:T(8,128)(2,1)S(1)} %collective-permute-done.4) | copy-start | bytes 6291460
  20.9 26.1 %collective-permute-start.6 = (bf16[4,1,128,1024]{3,2,1,0:T(8,128)(2,1)}, bf16[4,1,128,1024]{3,2,1,0:T(8,128)(2,1)}, u32[]{:S(2)}, u32[]{:S(2)}) collective-permute-start(bf16[4,1,128,1024]{3,2,1,0:T(8,128)(2,1)} %bitcast.28), channel_id=1, source_target_pairs={{0,16},{8,24},{16,0},{24,8},{32,48},{40,56},{48,32},{56,40},{64,80... | collective-permute-start | bytes 3145736 | tf_op jit(solution)/shard_map/sum_y_second/ppermute | solution.py:281
  23.2 3.4 %copy-start = (bf16[1024,4096]{1,0:T(8,128)(2,1)S(1)}, bf16[1024,4096]{1,0:T(8,128)(2,1)}, u32[]{:S(2)}) copy-start(bf16[1024,4096]{1,0:T(8,128)(2,1)} %refs_4_.1) | copy-start | bytes 25165828
  26.6 1.2 copy-start.19
  27.8 12.5 %copy-start.31 = (bf16[2,128,1024]{2,1,0:T(8,128)(2,1)S(1)}, bf16[2,128,1024]{2,1,0:T(8,128)(2,1)}, u32[]{:S(2)}) copy-start(bf16[2,128,1024]{2,1,0:T(8,128)(2,1)} %get-tuple-element.78) | copy-start | bytes 1572868
  35.4 14.5 %copy-start.20 = (bf16[512,1024]{1,0:T(8,128)(2,1)}, bf16[512,1024]{1,0:T(8,128)(2,1)S(1)}, u32[]{:S(2)}) copy-start(bf16[512,1024]{1,0:T(8,128)(2,1)S(1)} %get-tuple-element.39.refs_16_) | copy-start | bytes 3145732
  35.4 14.5 %copy-start.22 = (bf16[512,1024]{1,0:T(8,128)(2,1)}, bf16[512,1024]{1,0:T(8,128)(2,1)S(1)}, u32[]{:S(2)}) copy-start(bf16[512,1024]{1,0:T(8,128)(2,1)S(1)} %get-tuple-element.69.refs_15_) | copy-start | bytes 3145732
  35.4 11.5 %copy-start.29 = (bf16[4,2,128,1024]{3,2,1,0:T(8,128)(2,1)S(1)}, bf16[4,2,128,1024]{3,2,1,0:T(8,128)(2,1)}, u32[]{:S(2)}) copy-start(bf16[4,2,128,1024]{3,2,1,0:T(8,128)(2,1)} %copy-done.28) | copy-start | bytes 6291460
  42.0 9.1 %collective-permute-start.5 = (bf16[128,1024]{1,0:T(8,128)(2,1)S(1)}, bf16[128,1024]{1,0:T(8,128)(2,1)S(1)}, u32[]{:S(2)}, u32[]{:S(2)}) collective-permute-start(bf16[128,1024]{1,0:T(8,128)(2,1)S(1)} %fusion.17), channel_id=1, source_target_pairs={{0,16},{8,24},{16,0},{24,8},{32,48},{40,56},{48,32},{56,40},{64,80... | collective-permute-start | bytes 786440 | tf_op jit(solution)/shard_map/sum_x_first/ppermute | solution.py:281
  50.0 8.6 %copy-start.33 = (s32[2]{0:T(128)S(1)}, s32[2]{0:T(128)}, u32[]{:S(2)}) copy-start(s32[2]{0:T(128)} %param.8) | copy-start | bytes 28
  51.6 9.8 %collective-permute-start.7 = (bf16[128,1024]{1,0:T(8,128)(2,1)S(1)}, bf16[128,1024]{1,0:T(8,128)(2,1)}, u32[]{:S(2)}, u32[]{:S(2)}) collective-permute-start(bf16[128,1024]{1,0:T(8,128)(2,1)S(1)} %multiply_convert_fusion.1.refs_4_.refs_13_), channel_id=1, source_target_pairs={{0,1},{1,0},{2,3},{3,2},{4,5},{5,4},{6,7},{7,6},{8,9},{9,8},{10,11... | collective-permute-start | bytes 786440 | tf_op jit(solution)/shard_map/gather/ppermute | solution.py:285
  54.9 19.7 %collective-permute-start.10 = (bf16[128,1024]{1,0:T(8,128)(2,1)}, bf16[128,1024]{1,0:T(8,128)(2,1)}, u32[]{:S(2)}, u32[]{:S(2)}) collective-permute-start(bf16[128,1024]{1,0:T(8,128)(2,1)} %get-tuple-element.76), channel_id=1, source_target_pairs={{0,32},{8,40},{16,48},{24,56},{32,64},{40,72},{48,80},{56,88},{64,... | collective-permute-start | bytes 786440 | tf_op jit(solution)/shard_map/sum_y_second/ppermute | solution.py:281
  55.4 19.1 %collective-permute-start.11 = (bf16[128,1024]{1,0:T(8,128)(2,1)}, bf16[128,1024]{1,0:T(8,128)(2,1)}, u32[]{:S(2)}, u32[]{:S(2)}) collective-permute-start(bf16[128,1024]{1,0:T(8,128)(2,1)} %get-tuple-element.74), channel_id=1, source_target_pairs={{0,96},{8,104},{16,112},{24,120},{32,0},{40,8},{48,16},{56,24},{64... | collective-permute-start | bytes 786440 | tf_op jit(solution)/shard_map/sum_y_second/ppermute | solution.py:281
  58.1 16.5 %collective-permute-start.12 = (bf16[128,1024]{1,0:T(8,128)(2,1)}, bf16[128,1024]{1,0:T(8,128)(2,1)}, u32[]{:S(2)}, u32[]{:S(2)}) collective-permute-start(bf16[128,1024]{1,0:T(8,128)(2,1)} %get-tuple-element.75), channel_id=1, source_target_pairs={{0,64},{8,72},{16,80},{24,88},{32,96},{40,104},{48,112},{56,120},{... | collective-permute-start | bytes 786440 | tf_op jit(solution)/shard_map/sum_y_second/ppermute | solution.py:281
  62.3 16.4 %collective-permute-start.8 = (bf16[2,128,1024]{2,1,0:T(8,128)(2,1)S(1)}, bf16[2,128,1024]{2,1,0:T(8,128)(2,1)S(1)}, u32[]{:S(2)}, u32[]{:S(2)}) collective-permute-start(bf16[2,128,1024]{2,1,0:T(8,128)(2,1)S(1)} %pad_maximum_fusion.refs_0_), channel_id=1, source_target_pairs={{0,2},{1,3},{2,4},{3,5},{4,6},{5,7},{6,0},{7,1},{8,10},{9,11},{10,... | collective-permute-start | bytes 1572872 | tf_op jit(solution)/shard_map/gather/ppermute | solution.py:285
  64.3 14.4 %collective-permute-start.9 = (bf16[2,128,1024]{2,1,0:T(8,128)(2,1)S(1)}, bf16[2,128,1024]{2,1,0:T(8,128)(2,1)S(1)}, u32[]{:S(2)}, u32[]{:S(2)}) collective-permute-start(bf16[2,128,1024]{2,1,0:T(8,128)(2,1)S(1)} %pad_maximum_fusion.refs_0_), channel_id=1, source_target_pairs={{0,6},{1,7},{2,0},{3,1},{4,2},{5,3},{6,4},{7,5},{8,14},{9,15},{10,... | collective-permute-start | bytes 1572872 | tf_op jit(solution)/shard_map/gather/ppermute | solution.py:285
  66.7 3.4 %copy-start.1 = (bf16[1024,4096]{1,0:T(8,128)(2,1)S(1)}, bf16[1024,4096]{1,0:T(8,128)(2,1)}, u32[]{:S(2)}) copy-start(bf16[1024,4096]{1,0:T(8,128)(2,1)} %refs_4_.1) | copy-start | bytes 25165828
  70.1 4.5 %copy-start.30 = (f32[128,1024]{1,0:T(8,128)S(1)}, f32[128,1024]{1,0:T(8,128)}, u32[]{:S(2)}) copy-start(f32[128,1024]{1,0:T(8,128)} %get-tuple-element.77) | copy-start | bytes 1572868
  74.5 1.7 %copy-start.24 = (bf16[128,1024]{1,0:T(8,128)(2,1)}, bf16[128,1024]{1,0:T(8,128)(2,1)S(1)}, u32[]{:S(2)}) copy-start(bf16[128,1024]{1,0:T(8,128)(2,1)S(1)} %get-tuple-element.67.refs_11_) | copy-start | bytes 786436
  74.5 16.4 %copy-start.14 = (bf16[128,1024]{1,0:T(8,128)(2,1)}, bf16[128,1024]{1,0:T(8,128)(2,1)S(1)}, u32[]{:S(2)}) copy-start(bf16[128,1024]{1,0:T(8,128)(2,1)S(1)} %get-tuple-element.55.refs_5_.refs_7_) | copy-start | bytes 786436
  76.4 20.9 %copy-start.3 = (bf16[128,1024]{1,0:T(8,128)(2,1)}, bf16[128,1024]{1,0:T(8,128)(2,1)S(1)}, u32[]{:S(2)}) copy-start(bf16[128,1024]{1,0:T(8,128)(2,1)S(1)} %multiply_convert_fusion.refs_4_.refs_14_) | copy-start | bytes 786436
  76.4 8.0 %collective-permute-start.15 = (bf16[128,1024]{1,0:T(8,128)(2,1)S(1)}, bf16[128,1024]{1,0:T(8,128)(2,1)S(1)}, u32[]{:S(2)}, u32[]{:S(2)}) collective-permute-start(bf16[128,1024]{1,0:T(8,128)(2,1)S(1)} %multiply_convert_fusion.refs_4_.refs_14_), channel_id=1, source_target_pairs={{0,1},{1,0},{2,3},{3,2},{4,5},{5,4},{6,7},{7,6},{8,9},{9,8},{10,11... | collective-permute-start | bytes 786440 | tf_op jit(solution)/shard_map/gather/ppermute | solution.py:285
  84.4 19.6 %collective-permute-start.16 = (bf16[2,128,1024]{2,1,0:T(8,128)(2,1)S(1)}, bf16[2,128,1024]{2,1,0:T(8,128)(2,1)S(1)}, u32[]{:S(2)}, u32[]{:S(2)}) collective-permute-start(bf16[2,128,1024]{2,1,0:T(8,128)(2,1)S(1)} %pad_maximum_fusion.1.refs_0_), channel_id=1, source_target_pairs={{0,2},{1,3},{2,4},{3,5},{4,6},{5,7},{6,0},{7,1},{8,10},{9,11},{10,... | collective-permute-start | bytes 1572872 | tf_op jit(solution)/shard_map/gather/ppermute | solution.py:285
  84.5 19.5 %collective-permute-start.17 = (bf16[2,128,1024]{2,1,0:T(8,128)(2,1)S(1)}, bf16[2,128,1024]{2,1,0:T(8,128)(2,1)S(1)}, u32[]{:S(2)}, u32[]{:S(2)}) collective-permute-start(bf16[2,128,1024]{2,1,0:T(8,128)(2,1)S(1)} %pad_maximum_fusion.1.refs_0_), channel_id=1, source_target_pairs={{0,6},{1,7},{2,0},{3,1},{4,2},{5,3},{6,4},{7,5},{8,14},{9,15},{10,... | collective-permute-start | bytes 1572872 | tf_op jit(solution)/shard_map/gather/ppermute | solution.py:285
  87.7 36.6 %collective-permute-start.13 = (bf16[1,128,1024]{2,1,0:T(8,128)(2,1)}, bf16[1,128,1024]{2,1,0:T(8,128)(2,1)}, u32[]{:S(2)}, u32[]{:S(2)}) collective-permute-start(bf16[1,128,1024]{2,1,0:T(8,128)(2,1)} %slice.20), channel_id=1, source_target_pairs={{0,2},{1,3},{2,4},{3,5},{4,6},{5,7},{6,0},{7,1},{8,10},{9,11},{10,... | collective-permute-start | bytes 786440 | tf_op jit(solution)/shard_map/gather/ppermute | solution.py:285
  87.7 36.6 %collective-permute-start.14 = (bf16[1,128,1024]{2,1,0:T(8,128)(2,1)}, bf16[1,128,1024]{2,1,0:T(8,128)(2,1)}, u32[]{:S(2)}, u32[]{:S(2)}) collective-permute-start(bf16[1,128,1024]{2,1,0:T(8,128)(2,1)} %slice.21), channel_id=1, source_target_pairs={{0,6},{1,7},{2,0},{3,1},{4,2},{5,3},{6,4},{7,5},{8,14},{9,15},{10,... | collective-permute-start | bytes 786440 | tf_op jit(solution)/shard_map/gather/ppermute | solution.py:285
  97.3 4.5 %copy-start.6 = (f32[128,1024]{1,0:T(8,128)}, f32[128,1024]{1,0:T(8,128)S(1)}, u32[]{:S(2)}) copy-start(f32[128,1024]{1,0:T(8,128)S(1)} %get-tuple-element.65.refs_9_) | copy-start | bytes 1572868
  101.8 0.8 copy-start.8
  102.6 0.7 copy-start.16
  103.3 0.7 copy-start.26
  104.0 0.9 copy-start.12
  104.9 0.8 copy-start.10
  106.4 17.9 %collective-permute-start.18 = (bf16[1,128,1024]{2,1,0:T(8,128)(2,1)}, bf16[1,128,1024]{2,1,0:T(8,128)(2,1)}, u32[]{:S(2)}, u32[]{:S(2)}) collective-permute-start(bf16[1,128,1024]{2,1,0:T(8,128)(2,1)} %slice.22), channel_id=1, source_target_pairs={{0,2},{1,3},{2,4},{3,5},{4,6},{5,7},{6,0},{7,1},{8,10},{9,11},{10,... | collective-permute-start | bytes 786440 | tf_op jit(solution)/shard_map/gather/ppermute | solution.py:285
  106.4 18.0 %collective-permute-start.19 = (bf16[1,128,1024]{2,1,0:T(8,128)(2,1)}, bf16[1,128,1024]{2,1,0:T(8,128)(2,1)}, u32[]{:S(2)}, u32[]{:S(2)}) collective-permute-start(bf16[1,128,1024]{2,1,0:T(8,128)(2,1)} %slice.23), channel_id=1, source_target_pairs={{0,6},{1,7},{2,0},{3,1},{4,2},{5,3},{6,4},{7,5},{8,14},{9,15},{10,... | collective-permute-start | bytes 786440 | tf_op jit(solution)/shard_map/gather/ppermute | solution.py:285
  110.5 3.4 %copy-start.2 = (bf16[1024,4096]{1,0:T(8,128)(2,1)S(1)}, bf16[1024,4096]{1,0:T(8,128)(2,1)}, u32[]{:S(2)}) copy-start(bf16[1024,4096]{1,0:T(8,128)(2,1)} %refs_4_.1) | copy-start | bytes 25165828
  113.9 1.0 copy-start.9
  114.9 1.0 copy-start.11
  116.0 1.0 copy-start.13
  117.0 0.9 copy-start.17
  118.0 6.4 %copy-start.4 = (bf16[128,1024]{1,0:T(8,128)(2,1)S(1)}, bf16[128,1024]{1,0:T(8,128)(2,1)}, u32[]{:S(2)}) copy-start(bf16[128,1024]{1,0:T(8,128)(2,1)} %copy-done.3) | copy-start | bytes 786436
  118.0 6.4 %copy-start.5 = (bf16[1024,1024]{1,0:T(8,128)(2,1)S(1)}, bf16[1024,1024]{1,0:T(8,128)(2,1)}, u32[]{:S(2)}) copy-start(bf16[1024,1024]{1,0:T(8,128)(2,1)} %refs_18_.1) | copy-start | bytes 6291460
  118.0 6.4 %copy-start.7 = (f32[128,1024]{1,0:T(8,128)S(1)}, f32[128,1024]{1,0:T(8,128)}, u32[]{:S(2)}) copy-start(f32[128,1024]{1,0:T(8,128)} %copy-done.6) | copy-start | bytes 1572868
  118.0 6.4 %copy-start.15 = (bf16[128,1024]{1,0:T(8,128)(2,1)S(1)}, bf16[128,1024]{1,0:T(8,128)(2,1)}, u32[]{:S(2)}) copy-start(bf16[128,1024]{1,0:T(8,128)(2,1)} %copy-done.14) | copy-start | bytes 786436
  118.0 6.4 %copy-start.18 = (s32[512,1]{1,0:T(8,128)S(1)}, s32[512,1]{1,0:T(8,128)}, u32[]{:S(2)}) copy-start(s32[512,1]{1,0:T(8,128)} %copy.24.refs_17_) | copy-start | bytes 6148
  118.0 6.4 %copy-start.21 = (bf16[512,1024]{1,0:T(8,128)(2,1)S(1)}, bf16[512,1024]{1,0:T(8,128)(2,1)}, u32[]{:S(2)}) copy-start(bf16[512,1024]{1,0:T(8,128)(2,1)} %copy-done.20) | copy-start | bytes 3145732
  118.0 6.4 %copy-start.23 = (bf16[512,1024]{1,0:T(8,128)(2,1)S(1)}, bf16[512,1024]{1,0:T(8,128)(2,1)}, u32[]{:S(2)}) copy-start(bf16[512,1024]{1,0:T(8,128)(2,1)} %copy-done.22) | copy-start | bytes 3145732
  118.0 6.4 %copy-start.25 = (bf16[128,1024]{1,0:T(8,128)(2,1)S(1)}, bf16[128,1024]{1,0:T(8,128)(2,1)}, u32[]{:S(2)}) copy-start(bf16[128,1024]{1,0:T(8,128)(2,1)} %copy-done.24) | copy-start | bytes 786436
  118.0 6.4 %copy-start.27 = (bf16[128,1024]{1,0:T(8,128)(2,1)S(1)}, bf16[128,1024]{1,0:T(8,128)(2,1)}, u32[]{:S(2)}) copy-start(bf16[128,1024]{1,0:T(8,128)(2,1)} %copy-done.26) | copy-start | bytes 786436
where the time goes:
time: 138 us
  Pallas kernels  42.1 us (31%)
  starting transfers between devices  32.2 us (23%)
  local copies, waits for them, and re-layouts  30.8 us (22%)
  other arithmetic  16.3 us (12%)
  waiting for transfers between devices  14.3 us (10%)
  between operations  1.8 us (1%)
    pallas_call x6, Pallas kernels, kernel_call(): pl.pallas_call(body, in_specs=in_specs, out_specs=[vmem] * len(out_shape)...  42.1 us
    ppermute x10, starting transfers between devices, to_cand(): return lax.ppermute(array, 'cand', cand_perm(dz, dy))  19.6 us
    unnamed x68, local copies, waits for them, and re-layouts  18.6 us
    ppermute x10, starting transfers between devices, to_user(): return lax.ppermute(array, 'user', user_perm(dx, dy, dcore))  12.6 us
    ppermute x10, waiting for transfers between devices, to_user(): return lax.ppermute(array, 'user', user_perm(dx, dy, dcore))  10.1 us
    reshape x2, local copies, waits for them, and re-layouts, block(): lax.dynamic_slice(tables, at, size).reshape(size[0], size[1], SLOTS, D)  6.22 us
    squeeze x1, other arithmetic, local(): (block(0, core, x_at=hop[d]).astype(F32) + share(got0, x_at=hop[d]).astyp...  4.23 us
    ppermute x10, waiting for transfers between devices, to_cand(): return lax.ppermute(array, 'cand', cand_perm(dz, dy))  4.22 us
  transfers between devices with their start and end apart: 20, of which 5 were waited for; matrix products, arithmetic and copies ran while one was open for 18% of the time, Pallas kernels for 21%

commit v1 on v0

v1 whole, which is shorter than its diff:
```python
import functools

import jax
import jax.numpy as jnp
from jax import lax
from jax.experimental import pallas as pl
from jax.experimental.pallas import tpu as pltpu
from jax.sharding import PartitionSpec as P

F32 = jnp.float32
BF16 = jnp.bfloat16
HEADS = 8
HD = 128
D = 1024
SLOTS = 128
ROWS = 512
NX, NZ = 4, 4
WINDOW = 320
HALF_SCALE = 0.5 / (HD**0.5)
VMEM = 40 * 1024 * 1024
GROUP = 512
STEPS = D // GROUP
SHIFTS = (0, -1, 1, 2)


def silu(v):
    half = v * 0.5
    return half + half * jnp.tanh(half)


def layer_norm(rows):
    mean = jnp.mean(rows, axis=-1, keepdims=True)
    centered = rows - mean
    var = jnp.mean(centered * centered, axis=-1, keepdims=True)
    return centered * lax.rsqrt(var + 1e-05)


def mm(a, b):
    return jnp.dot(a, b, preferred_element_type=F32)


def weights_of(queries, keys):
    s = lax.dot_general(queries, keys, (((1,), (1,)), ((), ())), preferred_element_type=F32)
    half = s * HALF_SCALE
    return half + half * jnp.tanh(half)


def after(value, *others):
    return lax.optimization_barrier((value, others))[0]


def in_hbm(array):
    return pltpu.with_memory_space_constraint(array, pltpu.HBM)


def cost():
    return pl.CostEstimate(flops=10**6, bytes_accessed=1 << 16, transcendentals=0)


def pack_kernel(scal_ref, tables_ref, out_ref, sems):
    copies = []
    for x in range(NX):
        for y in range(2):
            n = 2 * x + y
            copies.append(
                pltpu.make_async_copy(
                    tables_ref.at[x, y, scal_ref[0], scal_ref[1]], out_ref.at[x, y], sems.at[n]
                )
            )
    for copy in copies:
        copy.start()
    for copy in copies:
        copy.wait()


def pack(tables, core_at, j):
    return pl.pallas_call(
        pack_kernel,
        in_specs=[pl.BlockSpec(memory_space=pltpu.SMEM), pl.BlockSpec(memory_space=pltpu.HBM)],
        out_specs=pl.BlockSpec(memory_space=pltpu.HBM),
        out_shape=jax.ShapeDtypeStruct((NX, 2, SLOTS, D), BF16),
        scratch_shapes=[pltpu.SemaphoreType.DMA((2 * NX,))],
        compiler_params=pltpu.CompilerParams(vmem_limit_bytes=VMEM),
        cost_estimate=cost(),
        name="pack",
    )(jnp.stack([core_at, jnp.int32(j)]).astype(jnp.int32), in_hbm(tables))


def add_up(name, scal, grid, parts, outs):
    def body(scal_ref, *refs):
        ins, out_refs = refs[: len(parts)], refs[len(parts) :]
        for (_, dtype, _, _, members), out_ref in zip(outs, out_refs):
            total = None
            for n in members:
                value = ins[n][...].astype(F32)
                value = value.reshape(value.shape[-2:])
                total = value if total is None else total + value
            if dtype == "norm":
                total, dtype = layer_norm(total), BF16
            out_ref[...] = total.astype(dtype).reshape(out_ref.shape)

    return pl.pallas_call(
        body,
        grid_spec=pltpu.PrefetchScalarGridSpec(
            num_scalar_prefetch=1,
            grid=grid,
            in_specs=[pl.BlockSpec(block, index) for _, block, index in parts],
            out_specs=[pl.BlockSpec(block, index) for _, _, block, index, _ in outs],
        ),
        out_shape=[
            jax.ShapeDtypeStruct(shape, BF16 if dtype == "norm" else dtype)
            for shape, dtype, _, _, _ in outs
        ],
        compiler_params=pltpu.CompilerParams(vmem_limit_bytes=VMEM),
        cost_estimate=cost(),
        name=name,
    )(scal, *(in_hbm(array) if array.ndim == 6 else array for array, _, _ in parts))


def over_y(scal, tables, got):
    block = (1, 1, 1, 1, SLOTS, D)
    return add_up(
        "over_y",
        scal,
        (NX,),
        [
            (tables, block, lambda i, s: (i, 1 - s[1], s[2], 1, 0, 0)),
            (got, (1, 1, SLOTS, D), lambda i, s: (i, 1 - s[1], 0, 0)),
        ],
        [((NX, SLOTS, D), BF16, (1, SLOTS, D), lambda i, s: (i, 0, 0), (0, 1))],
    )[0]


def away_x(scal, tables, got):
    half = SLOTS // 2
    parts, outs = [], []
    for d in range(NX):
        parts.append(
            (
                tables,
                (1, 1, 1, 1, half, D),
                lambda i, s, d=d: ((s[0] + d) % NX, i // 2, s[2], 0, i % 2, 0),
            )
        )
        parts.append((got, (1, 1, half, D), lambda i, s, d=d: ((s[0] + d) % NX, i // 2, i % 2, 0)))
        outs.append(
            ((2, SLOTS, D), BF16, (1, half, D), lambda i, s: (i // 2, i % 2, 0), (2 * d, 2 * d + 1))
        )
    return add_up("away_x", scal, (4,), parts, outs)


def join_x(scal, away, arrived):
    half = SLOTS // 2
    arrays = [away] + list(arrived)
    parts = [(a, (1, half, D), lambda i, s: (s[1], i, 0)) for a in arrays]
    parts += [(a, (1, half, D), lambda i, s: (1 - s[1], i, 0)) for a in arrays]
    out = lambda dtype, members: ((SLOTS, D), dtype, (half, D), lambda i, s: (i, 0), members)
    return add_up("join_x", scal, (2,), parts, [out(F32, (0, 1, 2, 3)), out(BF16, (4, 5, 6, 7))])


def join_y(scal, tables, got, arrived):
    half = SLOTS // 2
    parts, outs = [], []
    for d in range(NX):
        at = lambda s, d=d: (s[0] + d) % NX
        parts.append(
            (tables, (1, 1, 1, 1, half, D), lambda i, s, at=at: (at(s), s[1], s[2], 1, i, 0))
        )
        parts.append((got, (1, 1, half, D), lambda i, s, at=at: (at(s), s[1], i, 0)))
        parts.append((arrived, (1, half, D), lambda i, s, at=at: (at(s), i, 0)))
        outs.append(
            (
                (SLOTS, D),
                F32 if d == 0 else BF16,
                (half, D),
                lambda i, s: (i, 0),
                (3 * d, 3 * d + 1, 3 * d + 2),
            )
        )
    return add_up("join_y", scal, (2,), parts, outs)


def norm_sum(scal, arrays):
    half = SLOTS // 2
    parts = [(a, (half, D), lambda i, s: (i, 0)) for a in arrays]
    return add_up(
        "norm_sum",
        scal,
        (2,),
        parts,
        [((SLOTS, D), "norm", (half, D), lambda i, s: (i, 0), tuple(range(len(arrays))))],
    )[0]


class Fetch:
    def __init__(self, sems):
        self.sems, self.count, self.pending = sems, 0, {}

    def start(self, key, src, dst):
        copy = pltpu.make_async_copy(src, dst, self.sems.at[self.count])
        copy.start()
        self.count += 1
        self.pending.setdefault(key, []).append(copy)

    def wait(self, *keys):
        for key in keys:
            for copy in self.pending.pop(key, ()):
                copy.wait()


def cand_kernel(owner_ref, feats_hbm, w_hbm, *refs):
    outs, (xs_ref, u_ref, q_ref, a_ref), (feats_ref, w_ref, sems, out_sems) = refs[:4], refs[4:8], refs[8:]
    stores = []
    for g in range(STEPS):
        cols = slice(g * GROUP, (g + 1) * GROUP)
        for n, ref in enumerate((u_ref, q_ref, a_ref)):
            stores.append(
                pltpu.make_async_copy(
                    ref.at[:, cols], outs[1 + n].at[:, cols], out_sems.at[3 * g + n]
                )
            )
    stores.append(pltpu.make_async_copy(xs_ref, outs[0], out_sems.at[3 * STEPS]))
    fetch = Fetch(sems)
    fetch.start("feats", feats_hbm, feats_ref)
    for g in range(STEPS):
        for n in range(4):
            at = n * D + g * GROUP
            fetch.start(g, w_hbm.at[:, at : at + GROUP], w_ref.at[4 * g + n])
    second = owner_ref[...].astype(F32)
    r_from = lax.broadcasted_iota(jnp.int32, (ROWS, ROWS), 0)
    r_to = lax.broadcasted_iota(jnp.int32, (ROWS, ROWS), 1)
    upper = jnp.where(r_from <= r_to, 1.0, 0.0).astype(BF16)
    ones_before = mm(jnp.broadcast_to(second, (8, ROWS)).astype(BF16), upper)[:1]
    index = lax.broadcasted_iota(jnp.int32, (1, ROWS), 1).astype(F32)
    n_first = ROWS - jnp.sum(second, axis=1, keepdims=True)
    place = jnp.where(second > 0.5, n_first + ones_before - 1.0, index - ones_before)
    onehot = jnp.where(r_from == place.astype(jnp.int32), 1.0, 0.0).astype(BF16)
    fetch.wait("feats")
    x = layer_norm(feats_ref[...].astype(F32)).astype(BF16)
    xs_ref[...] = mm(onehot, x).astype(BF16)
    stores[-1].start()
    fetch.wait(0)

    @pl.loop(0, STEPS)
    def _(g):
        @pl.when(g == STEPS - 1)
        def _():
            fetch.wait(*range(1, STEPS))
            for copy in stores[: 3 * (STEPS - 1)]:
                copy.start()

        cols = pl.ds(pl.multiple_of(g * GROUP, GROUP), GROUP)
        u, v, q, k = (silu(mm(xs_ref[...], w_ref[4 * g + n])).astype(BF16) for n in range(4))
        u_ref[:, cols] = u
        q_ref[:, cols] = q
        prod = q.astype(F32) * k.astype(F32)
        for h in range(GROUP // HD):
            hc = slice(h * HD, (h + 1) * HD)
            half = jnp.sum(prod[:, hc], axis=-1, keepdims=True) * HALF_SCALE
            own = (half + half * jnp.tanh(half)).astype(BF16).astype(F32)
            out_cols = pl.ds(pl.multiple_of(g * GROUP + h * HD, HD), HD)
            a_ref[:, out_cols] = own * v[:, hc].astype(F32)

    for copy in stores[3 * (STEPS - 1) : -1]:
        copy.start()
    for copy in stores:
        copy.wait()


def cand_project(owner_row, feats, w_in):
    rows = pltpu.HBM((ROWS, D), BF16)
    vmem, hbm = pl.BlockSpec(memory_space=pltpu.VMEM), pl.BlockSpec(memory_space=pltpu.HBM)
    return pl.pallas_call(
        cand_kernel,
        in_specs=[vmem, hbm, hbm],
        out_specs=[hbm] * 4,
        out_shape=[rows, rows, rows, pltpu.HBM((ROWS, D), F32)],
        scratch_shapes=[pltpu.VMEM((ROWS, D), BF16)] * 3
        + [
            pltpu.VMEM((ROWS, D), F32),
            pltpu.VMEM((ROWS, D), BF16),
            pltpu.VMEM((4 * STEPS, D, GROUP), BF16),
            pltpu.SemaphoreType.DMA((1 + 4 * STEPS,)),
            pltpu.SemaphoreType.DMA((1 + 3 * STEPS,)),
        ],
        compiler_params=pltpu.CompilerParams(vmem_limit_bytes=VMEM),
        cost_estimate=cost(),
        name="cand_project",
    )(owner_row, in_hbm(feats), in_hbm(w_in))


def absorb_kernel(plan, scal_ref, *refs):
    items, first, final = plan["items"], plan["first"], plan["final"]
    users = sorted({user for user, _ in items})
    refs = list(refs)
    names = plan["names"]
    hbm = dict(zip(names, refs[: len(names)]))
    refs = refs[len(names) :]
    outs = dict(zip(plan["outs"], refs[: len(plan["outs"])]))
    refs = refs[len(plan["outs"]) :]
    vm = dict(zip(plan["held"], refs[: len(plan["held"])]))
    refs = refs[len(plan["held"]) :]
    made = dict(zip(plan["made"], refs[: len(plan["made"])]))
    refs = refs[len(plan["made"]) :]
    w_ref, k_scr, v_scr = refs[:3]
    sems, out_sems = refs[-2:]
    fetch = Fetch(sems)
    kinds = (3, 1, 2, 0) if first else (3, 1)
    fetch.start("x", hbm["x0"], vm["x0"])
    for g in range(STEPS):
        for n in kinds:
            at = n * D + g * GROUP
            fetch.start(("w", g), hbm["w_in"].at[:, at : at + GROUP], w_ref.at[4 * g + n])
        if g == 0:
            for name in names:
                if name not in ("x0", "w_in") and name in vm:
                    key = "late" if name in ("w_out", "u", "xs", "uh0", "uh1", "xh0", "xh1") else "x"
                    fetch.start(key, hbm[name], vm[name])
    if first:
        ah = {user: made["ah%d" % user] for user in users}
        qh = {user: made["qh%d" % user] for user in users}
        uh = {user: made["uh%d" % user] for user in users}
    else:
        ah = {user: vm["ah%d" % user] for user in (0, 1) if "ah%d" % user in vm}
        qh = {user: vm["qh%d" % user] for user in users}
    a_ref, q_ref = vm["a"], vm["q"]
    row_iota = lax.broadcasted_iota(jnp.int32, (SLOTS, 1), 0)
    ahead = lax.broadcasted_iota(jnp.int32, (SLOTS, SLOTS), 0) - lax.broadcasted_iota(
        jnp.int32, (SLOTS, SLOTS), 1
    )
    fetch.wait("x", ("w", 0))
    halves, wholes = [], []
    for name, out in outs.items():
        src = made[name] if name in made else vm[name]
        if name in ("a", "cand"):
            for g in range(STEPS):
                cols = slice(g * GROUP, (g + 1) * GROUP)
                halves.append(pltpu.make_async_copy(src.at[:, cols], out.at[:, cols], out_sems.at[g]))
        else:
            wholes.append(pltpu.make_async_copy(src, out, out_sems.at[STEPS + len(wholes)]))

    @pl.loop(0, STEPS)
    def _(g):
        @pl.when(g == STEPS - 1)
        def _():
            fetch.wait(*(("w", n) for n in range(1, STEPS)))
            if not final:
                for copy in halves[: STEPS - 1]:
                    copy.start()

        cols = pl.ds(pl.multiple_of(g * GROUP, GROUP), GROUP)
        wk, wv = w_ref[4 * g + 3], w_ref[4 * g + 1]
        for user in users:
            length = scal_ref[user, 0]
            row_lo = scal_ref[user, 1]
            row_hi = scal_ref[user, 2]
            my_off = scal_ref[user, 3]
            mine_items = [(n, shift) for n, (u, shift) in enumerate(items) if u == user]
            offs = [scal_ref[user, 4 + 2 * SHIFTS.index(shift) + e] for _, shift in mine_items for e in (0, 1)]
            n_keys = SLOTS * len(offs)
            if first:
                x_own = vm["x%d" % mine_items[0][0]][0]
                qh[user][:, cols] = silu(mm(x_own, w_ref[4 * g + 2])).astype(BF16)
                uh[user][:, cols] = silu(mm(x_own, w_ref[4 * g])).astype(BF16)
                ah[user][:, cols] = jnp.zeros((SLOTS, GROUP), F32)
            x = jnp.concatenate([vm["x%d" % n][...].reshape(2 * SLOTS, D) for n, _ in mine_items], axis=0)
            k_scr[:n_keys, :] = silu(mm(x, wk)).astype(BF16)
            v = silu(mm(x, wv)).astype(BF16)
            for i, off in enumerate(offs):
                piece = v[i * SLOTS : (i + 1) * SLOTS]
                piece = jnp.where(row_iota < length - off, piece, jnp.zeros_like(piece))
                v_scr[i * SLOTS : (i + 1) * SLOTS, :] = piece

            def attend(start, count):
                rows = pl.ds(start, count)
                index = start + lax.broadcasted_iota(jnp.int32, (count, 1), 0)
                mine = (index >= row_lo) & (index < row_hi)
                for h in range(GROUP // HD):
                    hc = slice(h * HD, (h + 1) * HD)
                    oc = pl.ds(pl.multiple_of(g * GROUP + h * HD, HD), HD)
                    q = jnp.concatenate([q_ref[rows, oc], qh[user][:, oc]], axis=0)
                    total = None
                    for n in range(0, n_keys, 2 * SLOTS):
                        w = weights_of(q, k_scr[n : n + 2 * SLOTS, hc])
                        parts = []
                        for i in range(2):
                            part = w[count:, i * SLOTS : (i + 1) * SLOTS]
                            seen = ahead >= offs[n // SLOTS + i] - my_off
                            parts.append(jnp.where(seen, part, 0.0).astype(BF16))
                        w = jnp.concatenate([w[:count].astype(BF16), jnp.concatenate(parts, axis=1)], axis=0)
                        pv = mm(w, v_scr[n : n + 2 * SLOTS, hc])
                        total = pv if total is None else total + pv
                    a_ref[rows, oc] += jnp.where(mine, total[:count], 0.0)
                    ah[user][:, oc] += total[count:]

            start = jnp.minimum((row_lo // 16) * 16, ROWS - WINDOW)
            narrow = row_hi <= start + WINDOW

            @pl.when(narrow)
            def _():
                attend(pl.multiple_of(start, 16), WINDOW)

            @pl.when(jnp.logical_not(narrow))
            def _():
                attend(0, ROWS)

    if not final:
        for copy in halves[STEPS - 1 :] + wholes:
            copy.start()
        for copy in halves + wholes:
            copy.wait()
        return
    y_scr = refs[3]
    owner_ref = vm["owner"]
    r_row = lax.broadcasted_iota(jnp.int32, (ROWS, ROWS), 0)
    r_col = lax.broadcasted_iota(jnp.int32, (ROWS, ROWS), 1)
    second = owner_ref[...].astype(F32)
    lower = jnp.where(r_col <= r_row, 1.0, 0.0).astype(BF16)
    ones_before = mm(lower, jnp.broadcast_to(second, (ROWS, HD)).astype(BF16))[:, :1]
    index = lax.broadcasted_iota(jnp.int32, (ROWS, 1), 0).astype(F32)
    n_first = ROWS - jnp.sum(second, axis=0, keepdims=True)
    place = jnp.where(second > 0.5, n_first + ones_before - 1.0, index - ones_before)
    back = jnp.where(r_col == place.astype(jnp.int32), 1.0, 0.0).astype(BF16)
    fetch.wait("late")
    for user in (0, 1):
        y = layer_norm(ah[user][...]) * vm["uh%d" % user][...].astype(F32)
        y_scr[user * SLOTS : (user + 1) * SLOTS, :] = y.astype(BF16)
    for n in range(0, ROWS, SLOTS):
        rows = slice(n, n + SLOTS)
        y = layer_norm(a_ref[rows, :]) * vm["u"][rows, :].astype(F32)
        y_scr[2 * SLOTS + n : 3 * SLOTS + n, :] = y.astype(BF16)

    @pl.loop(0, STEPS)
    def _(g):
        @pl.when(g == STEPS - 1)
        def _():
            for copy in halves[: STEPS - 1]:
                copy.start()

        cols = pl.ds(pl.multiple_of(g * GROUP, GROUP), GROUP)
        res = mm(y_scr[...], vm["w_out"][:, cols])
        for user in (0, 1):
            out = res[user * SLOTS : (user + 1) * SLOTS] + vm["xh%d" % user][:, cols].astype(F32)
            keep = scal_ref[user, 3] + row_iota < scal_ref[user, 0]
            made["hist"][user, :, cols] = jnp.where(keep, out, 0.0).astype(BF16)
        done = (res[2 * SLOTS :] + vm["xs"][:, cols].astype(F32)).astype(BF16)
        made["cand"][:, cols] = mm(back, done).astype(BF16)

    for copy in halves[STEPS - 1 :] + wholes:
        copy.start()
    for copy in halves + wholes:
        copy.wait()


def absorb(name, scal, items, w_in, q_cand, a_cand, first=False, state=None, final=None):
    users = sorted({item[0] for item in items})
    args = {"x%d" % n: item[2] for n, item in enumerate(items)}
    args.update(w_in=w_in, q=q_cand, a=a_cand)
    outs = {}
    sums, rows = pltpu.HBM((SLOTS, D), F32), pltpu.HBM((SLOTS, D), BF16)
    hbm, anywhere = pl.BlockSpec(memory_space=pltpu.HBM), pl.BlockSpec(memory_space=pl.ANY)
    if not first:
        for user in users:
            args["qh%d" % user] = state[user][0]
        for user in (0, 1) if final else users:
            args["ah%d" % user] = state[user][2]
    extra = []
    if final is not None:
        for user in (0, 1):
            args["uh%d" % user] = state[user][1]
            args["xh%d" % user] = final["own"][user]
        args.update({n: final[n] for n in ("u", "xs", "w_out", "owner")})
        outs = dict(
            hist=jax.ShapeDtypeStruct((2, SLOTS, D), BF16), cand=jax.ShapeDtypeStruct((ROWS, D), BF16)
        )
        extra = [pltpu.VMEM((2 * SLOTS + ROWS, D), BF16)]
    else:
        outs["a"] = pltpu.HBM((ROWS, D), F32)
        for user in users:
            outs["ah%d" % user] = sums
            if first:
                outs["qh%d" % user] = rows
                outs["uh%d" % user] = rows
    names = list(args)
    held = [n for n in names if n != "w_in"]
    most = max(sum(1 for item in items if item[0] == user) for user in users)
    plan = dict(
        items=tuple(item[:2] for item in items),
        first=first,
        final=final is not None,
        names=names,
        outs=list(outs),
        held=held,
        made=[n for n in outs if n not in held],
    )
    results = pl.pallas_call(
        functools.partial(absorb_kernel, plan),
        in_specs=[pl.BlockSpec(memory_space=pltpu.SMEM)]
        + [anywhere if n.startswith("x") and n != "xs" else hbm for n in names],
        out_specs=[hbm] * len(outs),
        out_shape=list(outs.values()),
        scratch_shapes=[pltpu.VMEM(args[n].shape, args[n].dtype) for n in held]
        + [pltpu.VMEM(outs[n].shape, outs[n].dtype) for n in plan["made"]]
        + [pltpu.VMEM((4 * STEPS, D, GROUP), BF16)]
        + [pltpu.VMEM((2 * most * SLOTS, GROUP), BF16)] * 2
        + extra
        + [pltpu.SemaphoreType.DMA((len(names) + 4 * STEPS,)), pltpu.SemaphoreType.DMA((STEPS + len(outs),))],
        compiler_params=pltpu.CompilerParams(vmem_limit_bytes=VMEM),
        cost_estimate=cost(),
        name=name,
    )(scal, *(args[n] if n.startswith("x") and n != "xs" else in_hbm(args[n]) for n in names))
    if final is not None:
        return results
    results = dict(zip(outs, results))
    new = dict(state or {})
    for user in users:
        if first:
            new[user] = tuple(results[n + str(user)] for n in ("qh", "uh", "ah"))
        else:
            new[user] = (state[user][0], state[user][1], results["ah%d" % user])
    return results["a"], new


def user_perm(dx, dy, dcore):
    pairs = []
    for u in range(4 * NX):
        x, y, core = u >> 2, (u >> 1) & 1, u & 1
        pairs.append((u, (((x + dx) % NX) * 2 + (y ^ dy)) * 2 + (core ^ dcore)))
    return pairs


def cand_perm(dz, dy):
    return [(c, (((c >> 1) + dz) % NZ) * 2 + ((c & 1) ^ dy)) for c in range(2 * NZ)]


def to_user(array, dx, dy, dcore):
    return lax.ppermute(array, "user", user_perm(dx, dy, dcore))


def to_cand(array, dz, dy):
    return lax.ppermute(array, "cand", cand_perm(dz, dy))


def local(pooled, cand_feats, hist_len, cand_user, w_in, w_out):
    user = lax.axis_index("user")
    cand = lax.axis_index("cand")
    x, y, core = user >> 2, (user >> 1) & 1, user & 1
    z, y_hi = cand >> 1, cand & 1
    owner = cand_user - 2 * user
    n_first = ROWS - jnp.sum(owner)
    offsets = [SLOTS * (((z + dz + NZ) % NZ) * 2 + (y_hi ^ e)) for dz in SHIFTS for e in range(2)]
    scal = jnp.stack(
        [
            jnp.stack([hist_len[0], 0 * user, n_first, cand * SLOTS] + offsets),
            jnp.stack([hist_len[1], n_first, 0 * user + ROWS, cand * SLOTS] + offsets),
        ]
    ).astype(jnp.int32)

    tables = pooled.reshape(NX, 2, 2, 2, SLOTS, D)
    place = jnp.stack([x, y, core]).astype(jnp.int32)
    with jax.named_scope("sum_core"):
        pack1 = pack(tables, 1 - core, 1)
        got1 = to_user(pack1, 0, 0, 1)
        pack0 = pack(after(tables, pack1), 1 - core, 0)
        got0 = to_user(pack0, 0, 0, 1)
    with jax.named_scope("sum_y_second"):
        over1 = over_y(place, tables, after(got1, pack0))
        y1 = to_user(over1, 0, 1, 0)
    with jax.named_scope("sum_x_first"):
        away0 = away_x(place, tables, after(got0, over1))
        x0 = [to_user(away0[d], d, 0, 0) for d in (1, 3, 2)]
    xs, u_cand, q_cand, a_cand = cand_project(after(owner.reshape(1, ROWS), away0), cand_feats, w_in)
    with jax.named_scope("sum_y_second"):
        away1 = join_y(place, tables, got1, after(y1, xs))
        x1 = [to_user(away1[d], d, 0, 0) for d in (1, 3, 2)]
    with jax.named_scope("sum_x_first"):
        mine0, over0 = join_x(place, away0[0], after(x0, away1))
        y0 = to_user(over0, 0, 1, 0)
    with jax.named_scope("gather"):
        own0 = norm_sum(place, [mine0, y0])
        near0 = to_cand(own0, 0, 1)
        own1 = norm_sum(place, [away1[0]] + after(x1, own0))
        near1 = to_cand(own1, 0, 1)
        pair0 = jnp.stack([own0, after(near0, own1)])
        z0 = {-1: to_cand(pair0, 1, 0), 1: to_cand(pair0, -1, 0)}
        pair1 = jnp.stack([own1, after(near1, pair0)])
        z1 = {-1: to_cand(pair1, 1, 0), 1: to_cand(pair1, -1, 0)}
    put = functools.partial(absorb, scal=scal, w_in=w_in, q_cand=q_cand)
    a_cand, state = put("own_pairs", items=[(0, 0, pair0), (1, 0, pair1)], a_cand=a_cand, first=True)
    with jax.named_scope("gather"):
        z0 = after(z0, a_cand)
        far0 = to_cand(z0[-1], 1, 0)
    a_cand, state = put(
        "side_first", items=[(0, -1, z0[-1]), (0, 1, z0[1])], a_cand=a_cand, state=state
    )
    with jax.named_scope("gather"):
        z1 = after(z1, a_cand)
        far1 = to_cand(z1[1], -1, 0)
    a_cand, state = put(
        "side_second",
        items=[(1, -1, z1[-1]), (1, 1, z1[1]), (0, 2, far0)],
        a_cand=a_cand,
        state=state,
    )
    return put(
        "far_finish",
        items=[(1, 2, far1)],
        a_cand=a_cand,
        state=state,
        final=dict(
            own={0: own0, 1: own1}, u=u_cand, xs=xs, owner=owner.reshape(ROWS, 1), w_out=w_out
        ),
    )


def solution(mesh):
    placed = (
        P("user", None, "cand", None),
        P(("user", "cand"), None),
        P("user"),
        P(("user", "cand")),
        P(),
        P(),
    )
    return jax.shard_map(
        local,
        mesh=mesh,
        in_specs=placed,
        out_specs=(P("user", "cand", None), P(("user", "cand"), None)),
        check_vma=False,
    )
```

time: 138 us -> 260 us (1.88)
  Pallas kernels: 42.1 us -> 207 us
  local copies, waits for them, and re-layouts: 30.8 us -> 3.75 us
  other arithmetic: 16.3 us -> 1.04 us
  starting transfers between devices: 32.2 us -> 29.5 us
    pallas_call x6 -> x13, Pallas kernels: 42.1 us -> 207 us  [the longest x2 130 us: pack(): pl.pallas_call(pack_kernel, in_specs=[pl.BlockSpec(memory_space=pltpu.SME...]
    unnamed x68 -> x8, local copies, waits for them, and re-layouts: 18.6 us -> 0.82 us
    convert_element_type x4 -> x0, other arithmetic: 6.52 us -> none  [the longest x1 3.26 us: local(): (block(1, core, y_at=1 - y).astype(F32) + share(got1, y_at=1 - y).astype(...]
    reshape x2 -> x0, local copies, waits for them, and re-layouts: 6.22 us -> none  [block(): lax.dynamic_slice(tables, at, size).reshape(size[0], size[1], SLOTS, D)]
    ppermute x10, waiting for transfers between devices: 10.1 us -> 15.9 us  [to_user(): return lax.ppermute(array, 'user', user_perm(dx, dy, dcore))]
    squeeze x1 -> x0, other arithmetic: 4.23 us -> none  [local(): (block(0, core, x_at=hop[d]).astype(F32) + share(got0, x_at=hop[d]).astyp...]
    ppermute x10 -> x8, waiting for transfers between devices: 4.22 us -> 0.93 us  [to_cand(): return lax.ppermute(array, 'cand', cand_perm(dz, dy))]
    slice x4 -> x0, local copies, waits for them, and re-layouts: 3.01 us -> none  [the longest x2 1.54 us: local(): ends1 = [z1[-1][:1], z1[1][1:]]]
  transfers between devices with their start and end apart: 20 -> 18, of which waited for: 5 -> 6; matrix products, arithmetic and copies ran while one was open for 18% -> 2% of each run, Pallas kernels for 21% -> 49%
where the time goes in v1:
time: 260 us; the launch traced here: 259 us
  Pallas kernels  207 us (80%)
  starting transfers between devices  29.5 us (11%)
  waiting for transfers between devices  16.9 us (6%)
  local copies, waits for them, and re-layouts  3.75 us (1%)
    pallas_call x2, Pallas kernels, pack(): pl.pallas_call(pack_kernel, in_specs=[pl.BlockSpec(memory_space=pltpu.SME...  130 us
    pallas_call x4, Pallas kernels, absorb(): pl.pallas_call(functools.partial(absorb_kernel, plan), in_specs=[pl.Block...  51.2 us
    ppermute x8, starting transfers between devices, to_cand(): return lax.ppermute(array, 'cand', cand_perm(dz, dy))  17.9 us
    ppermute x10, waiting for transfers between devices, to_user(): return lax.ppermute(array, 'user', user_perm(dx, dy, dcore))  15.9 us
    pallas_call x6, Pallas kernels, add_up(): pl.pallas_call(body, grid_spec=pltpu.PrefetchScalarGridSpec(num_scalar_pr...  15.1 us
    ppermute x10, starting transfers between devices, to_user(): return lax.ppermute(array, 'user', user_perm(dx, dy, dcore))  11.6 us
    pallas_call x1, Pallas kernels, cand_project(): pl.pallas_call(cand_kernel, in_specs=[vmem, hbm, hbm], out_specs=[hbm] *...  9.89 us
  transfers between devices with their start and end apart: 18, of which 6 were waited for; matrix products, arithmetic and copies ran while one was open for 2% of the time, Pallas kernels for 49%

profile of v1, /device:TPU:0, one launch (start us, length us, event | category | flops | bytes accessed | tf_op | source)
XLA Modules:
  0.0 259.5 jit_solution(9476902128984808918)
XLA Ops:
  0.6 0.1 pad_add_fusion.2.scal_ref
  0.7 65.2 %pack.2 = bf16[4,2,128,1024]{3,2,1,0:T(8,128)(2,1)} custom-call(s32[2]{0:T(128)S(1)} %pad_add_fusion.2.scal_ref, bf16[4,2,2,2,128,1024]{5,4,3,2,1,0:T(8,128)(2,1)} %bitcast.27), custom_call_target="tpu_custom_call" | custom-call | flops 1000000 | bytes 65536 | tf_op jit(solution)/shard_map/sum_core/pack/pallas_call | solution.py:77
  66.0 0.1 collective-permute-start
  66.1 0.1 pad_add_fusion.3.scal_ref
  66.1 65.2 %pack.3 = bf16[4,2,128,1024]{3,2,1,0:T(8,128)(2,1)} custom-call(s32[2]{0:T(128)S(1)} %pad_add_fusion.3.scal_ref, bf16[4,2,2,2,128,1024]{5,4,3,2,1,0:T(8,128)(2,1)} %bitcast.28), custom_call_target="tpu_custom_call" | custom-call | flops 1000000 | bytes 65536 | tf_op jit(solution)/shard_map/sum_core/pack/pallas_call | solution.py:77
  131.4 0.6 collective-permute-start.2
  132.0 0.1 pad_add_fusion.1.scal_ref
  132.0 0.0 collective-permute-done.refs_1_.refs_4_.refs_7_.refs_10_
  132.0 4.0 %over_y.1 = bf16[4,128,1024]{2,1,0:T(8,128)(2,1)} custom-call(s32[3]{0:T(128)S(1)} %pad_add_fusion.1.scal_ref, bf16[4,2,2,2,128,1024]{5,4,3,2,1,0:T(8,128)(2,1)} %bitcast.29, bf16[4,2,128,1024]{3,2,1,0:T(8,128)(2,1)S(1)} %collective-permute-done.refs_1_.refs_4_.refs_7_.refs_10_), custom_call_target="tpu_custom_call" | custom-call | flops 1000000 | bytes 65536 | tf_op jit(solution)/shard_map/sum_y_second/over_y/pallas_call | solution.py:102
  136.0 1.7 collective-permute-start.1
  137.7 0.0 collective-permute-done.2.refs_1_.refs_3_.refs_5_.refs_7_
  137.7 4.7 %away_x.1 = (bf16[2,128,1024]{2,1,0:T(8,128)(2,1)S(1)}, bf16[2,128,1024]{2,1,0:T(8,128)(2,1)}, bf16[2,128,1024]{2,1,0:T(8,128)(2,1)}, bf16[2,128,1024]{2,1,0:T(8,128)(2,1)}) custom-call(s32[3]{0:T(128)S(1)} %pad_add_fusion.1.scal_ref, bf16[4,2,2,2,128,1024]{5,4,3,2,1,0:T(8,128)(2,1)} %bitcast.30, ...), custom_call_target="tpu_custom_call" | custom-call | flops 1000000 | bytes 65536 | tf_op jit(solution)/shard_map/sum_x_first/away_x/pallas_call | solution.py:102
  142.4 0.8 copy-done
  143.2 1.5 collective-permute-start.6
  144.7 1.7 collective-permute-start.7
  146.5 1.8 collective-permute-start.8
  148.3 0.0 copy-done.2
  148.3 0.7 fusion
  149.0 9.9 %cand_project.1 = (bf16[512,1024]{1,0:T(8,128)(2,1)}, bf16[512,1024]{1,0:T(8,128)(2,1)}, bf16[512,1024]{1,0:T(8,128)(2,1)}, f32[512,1024]{1,0:T(8,128)}) custom-call(s32[1,512]{1,0:T(1,128)S(1)} %bitcast.25, bf16[512,1024]{1,0:T(8,128)(2,1)} %feats_hbm.1, bf16[1024,4096]{1,0:T(8,128)(2,1)} %refs_1_.1), custom_call_target="tpu_custom_call" | custom-call | flops 1000000 | bytes 65536 | tf_op jit(solution)/shard_map/cand_project/pallas_call | solution.py:273
  158.9 2.5 collective-permute-done.1.refs_2_.refs_5_.refs_8_.refs_11_
  161.3 2.2 join_y.1
  163.5 0.0 collective-permute-done.6.refs_1_.refs_5_
  163.5 5.3 %collective-permute-done.7.refs_2_.refs_6_ = bf16[2,128,1024]{2,1,0:T(8,128)(2,1)} collective-permute-done((bf16[2,128,1024]{2,1,0:T(8,128)(2,1)}, bf16[2,128,1024]{2,1,0:T(8,128)(2,1)}, u32[]{:S(2)}, u32[]{:S(2)}) %collective-permute-start.7) | collective-permute-done | bytes 524320 | tf_op jit(solution)/shard_map/sum_x_first/ppermute | solution.py:537
  168.8 1.7 collective-permute-done.8.refs_3_.refs_7_
  170.5 0.0 copy-done.1
  170.5 2.2 join_x.1
  172.7 0.8 collective-permute-start.9
  173.5 1.1 collective-permute-start.3
  174.6 2.1 collective-permute-start.4
  176.7 0.2 collective-permute-start.5
  176.9 2.9 %collective-permute-done.9.refs_1_ = bf16[128,1024]{1,0:T(8,128)(2,1)S(1)} collective-permute-done((bf16[128,1024]{1,0:T(8,128)(2,1)S(1)}, bf16[128,1024]{1,0:T(8,128)(2,1)S(1)}, u32[]{:S(2)}, u32[]{:S(2)}) %collective-permute-start.9) | collective-permute-done | bytes 262176 | tf_op jit(solution)/shard_map/sum_x_first/ppermute | solution.py:537
  179.9 1.0 norm_sum.2.refs_8_
  180.9 0.0 copy-start.3
  180.9 3.0 %collective-permute-start.11 = (bf16[128,1024]{1,0:T(8,128)(2,1)S(1)}, bf16[128,1024]{1,0:T(8,128)(2,1)S(1)}, u32[]{:S(2)}, u32[]{:S(2)}) collective-permute-start(bf16[128,1024]{1,0:T(8,128)(2,1)S(1)} %norm_sum.2.refs_8_), channel_id=1, source_target_pairs={{0,1},{1,0},{2,3},{3,2},{4,5},{5,4},{6,7},{7,6},{8,9},{9,8},{10,11... | collective-permute-start | bytes 786440 | tf_op jit(solution)/shard_map/gather/ppermute | solution.py:541
  183.9 3.5 %collective-permute-done.3.refs_1_ = bf16[128,1024]{1,0:T(8,128)(2,1)S(1)} collective-permute-done((bf16[128,1024]{1,0:T(8,128)(2,1)S(1)}, bf16[128,1024]{1,0:T(8,128)(2,1)S(1)}, u32[]{:S(2)}, u32[]{:S(2)}) %collective-permute-start.3) | collective-permute-done | bytes 262176 | tf_op jit(solution)/shard_map/sum_y_second/ppermute | solution.py:537
  187.4 0.0 collective-permute-done.4.refs_2_
  187.4 0.0 collective-permute-done.5.refs_3_
  187.4 1.0 norm_sum.3.refs_10_
  188.4 2.8 %collective-permute-start.10 = (bf16[128,1024]{1,0:T(8,128)(2,1)S(1)}, bf16[128,1024]{1,0:T(8,128)(2,1)S(1)}, u32[]{:S(2)}, u32[]{:S(2)}) collective-permute-start(bf16[128,1024]{1,0:T(8,128)(2,1)S(1)} %norm_sum.3.refs_10_), channel_id=1, source_target_pairs={{0,1},{1,0},{2,3},{3,2},{4,5},{5,4},{6,7},{7,6},{8,9},{9,8},{10,11... | collective-permute-start | bytes 786440 | tf_op jit(solution)/shard_map/gather/ppermute | solution.py:541
  191.2 0.0 collective-permute-done.11
  191.2 0.1 pad_maximum_fusion.refs_0_
  191.3 2.0 collective-permute-start.14
  193.3 2.2 collective-permute-start.15
  195.5 0.9 collective-permute-done.10
  196.4 0.1 pad_maximum_fusion.1.refs_1_
  196.4 2.0 collective-permute-start.12
  198.4 2.4 collective-permute-start.13
  201.5 0.0 copy-done.3
  201.5 0.6 fusion.1
  202.1 0.7 stack.105
  202.8 0.7 stack.107
  203.6 13.3 %own_pairs.1 = (f32[512,1024]{1,0:T(8,128)}, f32[128,1024]{1,0:T(8,128)}, bf16[128,1024]{1,0:T(8,128)(2,1)}, bf16[128,1024]{1,0:T(8,128)(2,1)}, f32[128,1024]{1,...) custom-call(s32[2,12]{1,0:T(2,128)S(1)} %pad_add_fusion.scal_ref, ...), custom_call_target="tpu_custom_call" | custom-call | flops 1000000 | bytes 65536 | tf_op jit(solution)/shard_map/own_pairs/pallas_call | solution.py:496
  216.9 0.0 collective-permute-done.14.refs_0_
  216.9 0.0 collective-permute-done.15.refs_1_
  216.9 0.1 collective-permute-start.17
  217.0 10.3 %side_first.1 = (f32[512,1024]{1,0:T(8,128)}, f32[128,1024]{1,0:T(8,128)}) custom-call(s32[2,12]{1,0:T(2,128)S(1)} %pad_add_fusion.scal_ref, bf16[2,128,1024]{2,1,0:T(8,128)(2,1)S(1)} %collective-permute-done.14.refs_0_, bf16[2,128,1024]{2,1,0:T(8,128)(2,1)S(1)} %collective-permute-done.15.refs_1_, bf16[1024,4096]{1,0:T(8,128)(2,1)} %refs_1_.1, ...), custom_call_target="tpu_custom_call" | custom-call | flops 1000000 | bytes 65536 | tf_op jit(solution)/shard_map/side_first/pallas_call | solution.py:496
  227.4 0.0 collective-permute-done.12.refs_0_
  227.4 0.0 collective-permute-done.13.refs_1_
  227.4 3.5 %collective-permute-start.16 = (bf16[2,128,1024]{2,1,0:T(8,128)(2,1)S(1)}, bf16[2,128,1024]{2,1,0:T(8,128)(2,1)S(1)}, u32[]{:S(2)}, u32[]{:S(2)}) collective-permute-start(bf16[2,128,1024]{2,1,0:T(8,128)(2,1)S(1)} %collective-permute-done.13.refs_1_), channel_id=1, source_target_pairs={{0,6},{1,7},{2,0},{3,1},{4,2},{5,3},{6,4},{7,5},{8,14},{9,15},{10,... | collective-permute-start | bytes 1572872 | tf_op jit(solution)/shard_map/gather/ppermute | solution.py:541
  230.9 0.9 copy.8.refs_14_
  231.8 0.0 collective-permute-done.17.refs_2_
  231.8 14.2 %side_second.1 = (f32[512,1024]{1,0:T(8,128)}, f32[128,1024]{1,0:T(8,128)}, f32[128,1024]{1,0:T(8,128)}) custom-call(s32[2,12]{1,0:T(2,128)S(1)} %pad_add_fusion.scal_ref, bf16[2,128,1024]{2,1,0:T(8,128)(2,1)} %collective-permute-done.12.refs_0_, bf16[2,128,1024]{2,1,0:T(8,128)(2,1)S(1)} %collective-permute-done.13.refs_1_, ...), custom_call_target="tpu_custom_call" | custom-call | flops 1000000 | bytes 65536 | tf_op jit(solution)/shard_map/side_second/pallas_call | solution.py:496
  246.0 0.0 collective-permute-done.16.refs_0_
  246.0 13.3 %far_finish.1 = (bf16[2,128,1024]{2,1,0:T(8,128)(2,1)}, bf16[512,1024]{1,0:T(8,128)(2,1)}) custom-call(s32[2,12]{1,0:T(2,128)S(1)} %pad_add_fusion.scal_ref, bf16[2,128,1024]{2,1,0:T(8,128)(2,1)S(1)} %collective-permute-done.16.refs_0_, bf16[1024,4096]{1,0:T(8,128)(2,1)} %refs_1_.1, bf16[512,1024]{1,0:T(8,128)(2,1)} %get-tuple-element.69.refs_3_.refs_4_.refs_2_, ...), custom_call_target="tpu_custom_call" | custom-call | flops 1000000 | bytes 65536 | tf_op jit(solution)/shard_map/far_finish/pallas_call | solution.py:496
  (4 shorter events, 0.0 us)
Async XLA Ops:
  66.0 66.1 %collective-permute-start = (bf16[4,2,128,1024]{3,2,1,0:T(8,128)(2,1)}, bf16[4,2,128,1024]{3,2,1,0:T(8,128)(2,1)S(1)}, u32[]{:S(2)}, u32[]{:S(2)}) collective-permute-start(bf16[4,2,128,1024]{3,2,1,0:T(8,128)(2,1)} %pack.2), channel_id=1, source_target_pairs={{0,8},{8,0},{16,24},{24,16},{32,40},{40,32},{48,56},{56,48},{64,72... | collective-permute-start | bytes 6291464 | tf_op jit(solution)/shard_map/sum_core/ppermute | solution.py:537
  131.4 6.3 %collective-permute-start.2 = (bf16[4,2,128,1024]{3,2,1,0:T(8,128)(2,1)}, bf16[4,2,128,1024]{3,2,1,0:T(8,128)(2,1)}, u32[]{:S(2)}, u32[]{:S(2)}) collective-permute-start(bf16[4,2,128,1024]{3,2,1,0:T(8,128)(2,1)} %pack.3), channel_id=1, source_target_pairs={{0,8},{8,0},{16,24},{24,16},{32,40},{40,32},{48,56},{56,48},{64,72... | collective-permute-start | bytes 6291464 | tf_op jit(solution)/shard_map/sum_core/ppermute | solution.py:537
  136.0 12.2 %copy-start.2 = (s32[512]{0:T(512)S(1)}, s32[512]{0:T(512)}, u32[]{:S(2)}) copy-start(s32[512]{0:T(512)} %param.9) | copy-start | bytes 6148
  136.0 25.3 %collective-permute-start.1 = (bf16[4,128,1024]{2,1,0:T(8,128)(2,1)}, bf16[4,128,1024]{2,1,0:T(8,128)(2,1)S(1)}, u32[]{:S(2)}, u32[]{:S(2)}) collective-permute-start(bf16[4,128,1024]{2,1,0:T(8,128)(2,1)} %over_y.1), channel_id=1, source_target_pairs={{0,16},{8,24},{16,0},{24,8},{32,48},{40,56},{48,32},{56,40},{64,80... | collective-permute-start | bytes 3145736 | tf_op jit(solution)/shard_map/sum_y_second/ppermute | solution.py:537
  142.4 0.8 copy-start
  143.2 20.3 %collective-permute-start.6 = (bf16[2,128,1024]{2,1,0:T(8,128)(2,1)}, bf16[2,128,1024]{2,1,0:T(8,128)(2,1)}, u32[]{:S(2)}, u32[]{:S(2)}) collective-permute-start(bf16[2,128,1024]{2,1,0:T(8,128)(2,1)} %get-tuple-element.49), channel_id=1, source_target_pairs={{0,32},{8,40},{16,48},{24,56},{32,64},{40,72},{48,80},{56,88},{64,... | collective-permute-start | bytes 1572872 | tf_op jit(solution)/shard_map/sum_x_first/ppermute | solution.py:537
  144.7 24.1 %collective-permute-start.7 = (bf16[2,128,1024]{2,1,0:T(8,128)(2,1)}, bf16[2,128,1024]{2,1,0:T(8,128)(2,1)}, u32[]{:S(2)}, u32[]{:S(2)}) collective-permute-start(bf16[2,128,1024]{2,1,0:T(8,128)(2,1)} %get-tuple-element.51), channel_id=1, source_target_pairs={{0,96},{8,104},{16,112},{24,120},{32,0},{40,8},{48,16},{56,24},{64... | collective-permute-start | bytes 1572872 | tf_op jit(solution)/shard_map/sum_x_first/ppermute | solution.py:537
  146.5 24.1 %collective-permute-start.8 = (bf16[2,128,1024]{2,1,0:T(8,128)(2,1)}, bf16[2,128,1024]{2,1,0:T(8,128)(2,1)}, u32[]{:S(2)}, u32[]{:S(2)}) collective-permute-start(bf16[2,128,1024]{2,1,0:T(8,128)(2,1)} %get-tuple-element.50), channel_id=1, source_target_pairs={{0,64},{8,72},{16,80},{24,88},{32,96},{40,104},{48,112},{56,120},{... | collective-permute-start | bytes 1572872 | tf_op jit(solution)/shard_map/sum_x_first/ppermute | solution.py:537
  161.3 9.2 %copy-start.1 = (bf16[2,128,1024]{2,1,0:T(8,128)(2,1)S(1)}, bf16[2,128,1024]{2,1,0:T(8,128)(2,1)}, u32[]{:S(2)}) copy-start(bf16[2,128,1024]{2,1,0:T(8,128)(2,1)} %copy-done) | copy-start | bytes 1572868
  172.7 7.1 %collective-permute-start.9 = (bf16[128,1024]{1,0:T(8,128)(2,1)S(1)}, bf16[128,1024]{1,0:T(8,128)(2,1)S(1)}, u32[]{:S(2)}, u32[]{:S(2)}) collective-permute-start(bf16[128,1024]{1,0:T(8,128)(2,1)S(1)} %get-tuple-element.63), channel_id=1, source_target_pairs={{0,16},{8,24},{16,0},{24,8},{32,48},{40,56},{48,32},{56,40},{64,80... | collective-permute-start | bytes 786440 | tf_op jit(solution)/shard_map/sum_x_first/ppermute | solution.py:537
  173.5 13.9 %collective-permute-start.3 = (bf16[128,1024]{1,0:T(8,128)(2,1)S(1)}, bf16[128,1024]{1,0:T(8,128)(2,1)S(1)}, u32[]{:S(2)}, u32[]{:S(2)}) collective-permute-start(bf16[128,1024]{1,0:T(8,128)(2,1)S(1)} %get-tuple-element.56), channel_id=1, source_target_pairs={{0,32},{8,40},{16,48},{24,56},{32,64},{40,72},{48,80},{56,88},{64,... | collective-permute-start | bytes 786440 | tf_op jit(solution)/shard_map/sum_y_second/ppermute | solution.py:537
  174.6 12.7 %collective-permute-start.4 = (bf16[128,1024]{1,0:T(8,128)(2,1)S(1)}, bf16[128,1024]{1,0:T(8,128)(2,1)S(1)}, u32[]{:S(2)}, u32[]{:S(2)}) collective-permute-start(bf16[128,1024]{1,0:T(8,128)(2,1)S(1)} %get-tuple-element.57), channel_id=1, source_target_pairs={{0,96},{8,104},{16,112},{24,120},{32,0},{40,8},{48,16},{56,24},{64... | collective-permute-start | bytes 786440 | tf_op jit(solution)/shard_map/sum_y_second/ppermute | solution.py:537
  176.7 10.6 %collective-permute-start.5 = (bf16[128,1024]{1,0:T(8,128)(2,1)S(1)}, bf16[128,1024]{1,0:T(8,128)(2,1)S(1)}, u32[]{:S(2)}, u32[]{:S(2)}) collective-permute-start(bf16[128,1024]{1,0:T(8,128)(2,1)S(1)} %get-tuple-element.58), channel_id=1, source_target_pairs={{0,64},{8,72},{16,80},{24,88},{32,96},{40,104},{48,112},{56,120},{... | collective-permute-start | bytes 786440 | tf_op jit(solution)/shard_map/sum_y_second/ppermute | solution.py:537
  180.9 20.6 %copy-start.3 = (s32[2]{0:T(128)S(1)}, s32[2]{0:T(128)}, u32[]{:S(2)}) copy-start(s32[2]{0:T(128)} %param.8) | copy-start | bytes 28
  180.9 10.3 %collective-permute-start.11 = (bf16[128,1024]{1,0:T(8,128)(2,1)S(1)}, bf16[128,1024]{1,0:T(8,128)(2,1)S(1)}, u32[]{:S(2)}, u32[]{:S(2)}) collective-permute-start(bf16[128,1024]{1,0:T(8,128)(2,1)S(1)} %norm_sum.2.refs_8_), channel_id=1, source_target_pairs={{0,1},{1,0},{2,3},{3,2},{4,5},{5,4},{6,7},{7,6},{8,9},{9,8},{10,11... | collective-permute-start | bytes 786440 | tf_op jit(solution)/shard_map/gather/ppermute | solution.py:541
  188.4 8.0 %collective-permute-start.10 = (bf16[128,1024]{1,0:T(8,128)(2,1)S(1)}, bf16[128,1024]{1,0:T(8,128)(2,1)S(1)}, u32[]{:S(2)}, u32[]{:S(2)}) collective-permute-start(bf16[128,1024]{1,0:T(8,128)(2,1)S(1)} %norm_sum.3.refs_10_), channel_id=1, source_target_pairs={{0,1},{1,0},{2,3},{3,2},{4,5},{5,4},{6,7},{7,6},{8,9},{9,8},{10,11... | collective-permute-start | bytes 786440 | tf_op jit(solution)/shard_map/gather/ppermute | solution.py:541
  191.3 25.6 %collective-permute-start.14 = (bf16[2,128,1024]{2,1,0:T(8,128)(2,1)S(1)}, bf16[2,128,1024]{2,1,0:T(8,128)(2,1)S(1)}, u32[]{:S(2)}, u32[]{:S(2)}) collective-permute-start(bf16[2,128,1024]{2,1,0:T(8,128)(2,1)S(1)} %pad_maximum_fusion.refs_0_), channel_id=1, source_target_pairs={{0,2},{1,3},{2,4},{3,5},{4,6},{5,7},{6,0},{7,1},{8,10},{9,11},{10,... | collective-permute-start | bytes 1572872 | tf_op jit(solution)/shard_map/gather/ppermute | solution.py:541
  193.3 23.7 %collective-permute-start.15 = (bf16[2,128,1024]{2,1,0:T(8,128)(2,1)S(1)}, bf16[2,128,1024]{2,1,0:T(8,128)(2,1)S(1)}, u32[]{:S(2)}, u32[]{:S(2)}) collective-permute-start(bf16[2,128,1024]{2,1,0:T(8,128)(2,1)S(1)} %pad_maximum_fusion.refs_0_), channel_id=1, source_target_pairs={{0,6},{1,7},{2,0},{3,1},{4,2},{5,3},{6,4},{7,5},{8,14},{9,15},{10,... | collective-permute-start | bytes 1572872 | tf_op jit(solution)/shard_map/gather/ppermute | solution.py:541
  196.4 30.9 %collective-permute-start.12 = (bf16[2,128,1024]{2,1,0:T(8,128)(2,1)S(1)}, bf16[2,128,1024]{2,1,0:T(8,128)(2,1)}, u32[]{:S(2)}, u32[]{:S(2)}) collective-permute-start(bf16[2,128,1024]{2,1,0:T(8,128)(2,1)S(1)} %pad_maximum_fusion.1.refs_1_), channel_id=1, source_target_pairs={{0,2},{1,3},{2,4},{3,5},{4,6},{5,7},{6,0},{7,1},{8,10},{9,11},{10,... | collective-permute-start | bytes 1572872 | tf_op jit(solution)/shard_map/gather/ppermute | solution.py:541
  198.4 29.0 %collective-permute-start.13 = (bf16[2,128,1024]{2,1,0:T(8,128)(2,1)S(1)}, bf16[2,128,1024]{2,1,0:T(8,128)(2,1)S(1)}, u32[]{:S(2)}, u32[]{:S(2)}) collective-permute-start(bf16[2,128,1024]{2,1,0:T(8,128)(2,1)S(1)} %pad_maximum_fusion.1.refs_1_), channel_id=1, source_target_pairs={{0,6},{1,7},{2,0},{3,1},{4,2},{5,3},{6,4},{7,5},{8,14},{9,15},{10,... | collective-permute-start | bytes 1572872 | tf_op jit(solution)/shard_map/gather/ppermute | solution.py:541
  216.9 14.9 %collective-permute-start.17 = (bf16[2,128,1024]{2,1,0:T(8,128)(2,1)S(1)}, bf16[2,128,1024]{2,1,0:T(8,128)(2,1)S(1)}, u32[]{:S(2)}, u32[]{:S(2)}) collective-permute-start(bf16[2,128,1024]{2,1,0:T(8,128)(2,1)S(1)} %collective-permute-done.14.refs_0_), channel_id=1, source_target_pairs={{0,2},{1,3},{2,4},{3,5},{4,6},{5,7},{6,0},{7,1},{8,10},{9,11},{10,... | collective-permute-start | bytes 1572872 | tf_op jit(solution)/shard_map/gather/ppermute | solution.py:541
  227.4 18.6 %collective-permute-start.16 = (bf16[2,128,1024]{2,1,0:T(8,128)(2,1)S(1)}, bf16[2,128,1024]{2,1,0:T(8,128)(2,1)S(1)}, u32[]{:S(2)}, u32[]{:S(2)}) collective-permute-start(bf16[2,128,1024]{2,1,0:T(8,128)(2,1)S(1)} %collective-permute-done.13.refs_1_), channel_id=1, source_target_pairs={{0,6},{1,7},{2,0},{3,1},{4,2},{5,3},{6,4},{7,5},{8,14},{9,15},{10,... | collective-permute-start | bytes 1572872 | tf_op jit(solution)/shard_map/gather/ppermute | solution.py:541

commit v2 on v0

--- a/solution.py
+++ b/solution.py
@@ -42,6 +42,131 @@
     s = lax.dot_general(queries, keys, (((1,), (1,)), ((), ())), preferred_element_type=F32)
     half = s * HALF_SCALE
     return half + half * jnp.tanh(half)
+
+
+def after(value, *others):
+    return lax.optimization_barrier((value, others))[0]
+
+
+def in_hbm(array):
+    return pltpu.with_memory_space_constraint(array, pltpu.HBM)
+
+
+def cost():
+    return pl.CostEstimate(flops=10**6, bytes_accessed=1 << 16, transcendentals=0)
+
+
+def block_sums(name, scal, arrays, shapes, sums, hbm=True):
+    loads = [part for _, _, parts, _ in sums for part in parts]
+
+    def body(scal_ref, *refs):
+        ins, refs = refs[: len(arrays)], refs[len(arrays) :]
+        outs, refs = refs[: len(shapes)], refs[len(shapes) :]
+        bufs, refs = refs[: len(loads)], refs[len(loads) :]
+        res, (in_sems, out_sems) = refs[: len(sums)], refs[len(sums) :]
+        copies = []
+        for n, (at, index) in enumerate(loads):
+            lead = index(scal_ref)
+            src = ins[at].at[lead] if lead else ins[at]
+            copies.append(pltpu.make_async_copy(src, bufs[n], in_sems.at[n]))
+            copies[-1].start()
+        stores, used = [], 0
+        for n, (out, lead, parts, norm) in enumerate(sums):
+            total = None
+            for k in range(used, used + len(parts)):
+                copies[k].wait()
+                value = bufs[k][...].astype(F32)
+                total = value if total is None else total + value
+            used += len(parts)
+            res[n][...] = (layer_norm(total) if norm else total).astype(res[n].dtype)
+            dst = outs[out].at[lead] if lead else outs[out]
+            stores.append(pltpu.make_async_copy(res[n], dst, out_sems.at[n]))
+            stores[-1].start()
+        for store in stores:
+            store.wait()
+
+    spec = pl.BlockSpec(memory_space=pltpu.HBM)
+    return pl.pallas_call(
+        body,
+        in_specs=[pl.BlockSpec(memory_space=pltpu.SMEM)]
+        + [spec if a.ndim == 6 else pl.BlockSpec(memory_space=pl.ANY) for a in arrays],
+        out_specs=[spec if hbm else pl.BlockSpec(memory_space=pl.ANY)] * len(shapes),
+        out_shape=[(pltpu.HBM if hbm else jax.ShapeDtypeStruct)(shape, dtype) for shape, dtype in shapes],
+        scratch_shapes=[pltpu.VMEM((SLOTS, D), arrays[at].dtype) for at, _ in loads]
+        + [pltpu.VMEM((SLOTS, D), shapes[out][1]) for out, _, _, _ in sums]
+        + [pltpu.SemaphoreType.DMA((len(loads),)), pltpu.SemaphoreType.DMA((len(sums),))],
+        compiler_params=pltpu.CompilerParams(vmem_limit_bytes=VMEM),
+        cost_estimate=cost(),
+        name=name,
+    )(scal, *(in_hbm(a) if a.ndim == 6 else a for a in arrays))
+
+
+def pack(place, tables, j):
+    sums = [
+        (0, (x, y), [(0, lambda s, x=x, y=y: (x, y, 1 - s[2], j))], False)
+        for x in range(NX)
+        for y in range(2)
+    ]
+    return block_sums("pack", place, [tables], [((NX, 2, SLOTS, D), BF16)], sums)[0]
+
+
+def over_y(place, tables, got):
+    sums = [
+        (
+            0,
+            (x,),
+            [(0, lambda s, x=x: (x, 1 - s[1], s[2], 1)), (1, lambda s, x=x: (x, 1 - s[1]))],
+            False,
+        )
+        for x in range(NX)
+    ]
+    return block_sums("over_y", place, [tables, got], [((NX, SLOTS, D), BF16)], sums)[0]
+
+
+def away_x(place, tables, got):
+    sums = []
+    for d in (1, 3, 2, 0):
+        for y in range(2):
+            at = lambda s, d=d: lax.rem(s[0] + d, NX)
+            parts = [
+                (0, lambda s, at=at, y=y: (at(s), y, s[2], 0)),
+                (1, lambda s, at=at, y=y: (at(s), y)),
+            ]
+            sums.append((d, (y,), parts, False))
+    return block_sums("away_x", place, [tables, got], [((2, SLOTS, D), BF16)] * NX, sums)
+
+
+def join_x(place, away, arrived):
+    arrays = [away] + list(arrived)
+    sums = [
+        (1, (), [(n, lambda s: (1 - s[1],)) for n in range(NX)], False),
+        (0, (), [(n, lambda s: (s[1],)) for n in range(NX)], False),
+    ]
+    return block_sums("join_x", place, arrays, [((SLOTS, D), F32), ((SLOTS, D), BF16)], sums, False)
+
+
+def join_y(place, tables, got, arrived):
+    sums = []
+    for d in (1, 3, 2, 0):
+        at = lambda s, d=d: lax.rem(s[0] + d, NX)
+        parts = [
+            (0, lambda s, at=at: (at(s), s[1], s[2], 1)),
+            (1, lambda s, at=at: (at(s), s[1])),
+            (2, lambda s, at=at: (at(s),)),
+        ]
+        sums.append((d, (), parts, False))
+    shapes = [((SLOTS, D), F32 if d == 0 else BF16) for d in range(NX)]
+    return block_sums("join_y", place, [tables, got, arrived], shapes, sums)
+
+
+def norm_sum(place, arrays):
+    parts = [(n, lambda s: ()) for n in range(len(arrays))]
+    return block_sums("norm_sum", place, arrays, [((SLOTS, D), BF16)], [(0, (), parts, True)], False)[0]
+
+
+def join_pair(place, own, near):
+    sums = [(0, (n,), [(n, lambda s: ())], False) for n in range(2)]
+    return block_sums("join_pair", place, [own, near], [((2, SLOTS, D), BF16)], sums, False)[0]
 
 
 def in_vmem(array):
@@ -62,12 +187,12 @@
         scratch_shapes=scratch,
         input_output_aliases=aliases or {},
         compiler_params=pltpu.CompilerParams(vmem_limit_bytes=VMEM),
-        cost_estimate=pl.CostEstimate(flops=10**6, bytes_accessed=1 << 16, transcendentals=0),
+        cost_estimate=cost(),
         name=name,
     )(*args)
 
 
-def cand_kernel(owner_ref, feats_ref, w_ref, xs_ref, u_ref, q_ref, a_ref):
+def cand_kernel(owner_ref, feats_ref, w_ref, xs_ref, u_ref, q_ref, back_ref, a_ref):
     second = owner_ref[...].astype(F32)
     r_from = lax.broadcasted_iota(jnp.int32, (ROWS, ROWS), 0)
     r_to = lax.broadcasted_iota(jnp.int32, (ROWS, ROWS), 1)
@@ -76,7 +201,9 @@
     index = lax.broadcasted_iota(jnp.int32, (1, ROWS), 1).astype(F32)
     n_first = ROWS - jnp.sum(second, axis=1, keepdims=True)
     place = jnp.where(second > 0.5, n_first + ones_before - 1.0, index - ones_before)
-    onehot = jnp.where(r_from == place.astype(jnp.int32), 1.0, 0.0).astype(BF16)
+    onehot = jnp.where(r_from == place.astype(jnp.int32), 1.0, 0.0)
+    back_ref[...] = onehot.T.astype(BF16)
+    onehot = onehot.astype(BF16)
     x = layer_norm(feats_ref[...].astype(F32)).astype(BF16)
     xs_ref[...] = mm(onehot, x).astype(BF16)
 
@@ -97,12 +224,12 @@
 
 def cand_project(owner_row, feats, w_in):
     rows = jax.ShapeDtypeStruct((ROWS, D), BF16)
-    out_shape = [rows, rows, rows, jax.ShapeDtypeStruct((ROWS, D), F32)]
+    out_shape = [rows, rows, rows, jax.ShapeDtypeStruct((ROWS, ROWS), BF16), jax.ShapeDtypeStruct((ROWS, D), F32)]
     return kernel_call(cand_kernel, "cand_project", [owner_row, feats, w_in], out_shape, [])
 
 
 def absorb_kernel(plan, scal_ref, *refs):
-    users, first, final = plan["users"], plan["first"], plan["final"]
+    users, every, first, final = plan["users"], plan["every"], plan["first"], plan["final"]
     refs = list(refs)
     take = lambda n: [refs.pop(0) for _ in range(n)]
     keys = [(user, shift, e, ref) for (user, shift, es), ref in zip(plan["items"], take(len(plan["items"]))) for e in es]
@@ -111,11 +238,11 @@
         own_ref = dict(zip(users, take(len(users))))
     else:
         qh_ref = dict(zip(users, take(len(users))))
-        ah_ref = dict(zip(users, take(len(users))))
+        ah_ref = dict(zip(every, take(len(every))))
     if final:
-        uh_ref = dict(zip(users, take(len(users))))
-        xh_ref = dict(zip(users, take(len(users))))
-        u_ref, xs_ref, owner_ref, wo_ref = take(4)
+        uh_ref = dict(zip(every, take(len(every))))
+        xh_ref = dict(zip(every, take(len(every))))
+        u_ref, xs_ref, back_ref, wo_ref = take(4)
         hist_ref, cand_ref = take(2)
     else:
         take(1)
@@ -191,8 +318,8 @@
                 attend(0, ROWS)
 
     if final:
-        n_hist = SLOTS * len(users)
-        for i, user in enumerate(users):
+        n_hist = SLOTS * len(every)
+        for i, user in enumerate(every):
             y = layer_norm(ah_ref[user][...]) * uh_ref[user][...].astype(F32)
             y_scr[i * SLOTS : (i + 1) * SLOTS, :] = y.astype(BF16)
 
@@ -202,31 +329,22 @@
             y = layer_norm(a_ref[rows, :]) * u_ref[rows, :].astype(F32)
             y_scr[pl.ds(pl.multiple_of(n_hist + n * SLOTS, SLOTS), SLOTS), :] = y.astype(BF16)
 
-        r_row = lax.broadcasted_iota(jnp.int32, (ROWS, ROWS), 0)
-        r_col = lax.broadcasted_iota(jnp.int32, (ROWS, ROWS), 1)
-        second = owner_ref[...].astype(F32)
-        lower = jnp.where(r_col <= r_row, 1.0, 0.0).astype(BF16)
-        ones_before = mm(lower, jnp.broadcast_to(second, (ROWS, HD)).astype(BF16))[:, :1]
-        index = lax.broadcasted_iota(jnp.int32, (ROWS, 1), 0).astype(F32)
-        n_first = ROWS - jnp.sum(second, axis=0, keepdims=True)
-        place = jnp.where(second > 0.5, n_first + ones_before - 1.0, index - ones_before)
-        back = jnp.where(r_col == place.astype(jnp.int32), 1.0, 0.0).astype(BF16)
-
         @pl.loop(0, D // GROUP)
         def _(g):
             cols = pl.ds(pl.multiple_of(g * GROUP, GROUP), GROUP)
             res = mm(y_scr[...], wo_ref[:, cols])
-            for i, user in enumerate(users):
+            for i, user in enumerate(every):
                 out = res[i * SLOTS : (i + 1) * SLOTS] + xh_ref[user][:, cols].astype(F32)
                 keep = scal_ref[user, 3] + row_iota < scal_ref[user, 0]
                 hist_ref[user, :, cols] = jnp.where(keep, out, 0.0).astype(BF16)
             done = (res[n_hist:] + xs_ref[:, cols].astype(F32)).astype(BF16)
-            cand_ref[:, cols] = mm(back, done).astype(BF16)
+            cand_ref[:, cols] = mm(back_ref[...], done).astype(BF16)
 
 
 def absorb(name, scal, items, w_in, q_cand, a_cand, first=None, state=None, final=None):
     users = tuple(sorted({item[0] for item in items}))
-    plan = dict(items=tuple(item[:3] for item in items), users=users, first=first is not None, final=final is not None)
+    every = (0, 1) if final is not None else users
+    plan = dict(items=tuple(item[:3] for item in items), users=users, every=every, first=first is not None, final=final is not None)
     arrays = [item[3] for item in items] + [w_in, q_cand, a_cand]
     n = len(users)
     a_at = len(arrays)
@@ -242,21 +360,21 @@
     else:
         arrays += [state[user][0] for user in users]
         aliases.update({len(arrays) + 1 + i: 1 + i for i in range(n)})
-        arrays += [state[user][2] for user in users]
+        arrays += [state[user][2] for user in every]
         out_shape += [sums] * n
     if final is not None:
-        arrays += [state[user][1] for user in users]
-        arrays += [final["own"][user] for user in users]
-        arrays += [final["u"], final["xs"], final["owner"], final["w_out"]]
-        out_shape = [jax.ShapeDtypeStruct((n, SLOTS, D), BF16), jax.ShapeDtypeStruct((ROWS, D), BF16)]
+        arrays += [state[user][1] for user in every]
+        arrays += [final["own"][user] for user in every]
+        arrays += [final["u"], final["xs"], final["back"], final["w_out"]]
+        out_shape = [jax.ShapeDtypeStruct((2, SLOTS, D), BF16), jax.ShapeDtypeStruct((ROWS, D), BF16)]
         aliases = {}
-        scratch.append(pltpu.VMEM((n * SLOTS + ROWS, D), BF16))
+        scratch.append(pltpu.VMEM((2 * SLOTS + ROWS, D), BF16))
     outs = kernel_call(
         functools.partial(absorb_kernel, plan), name, arrays, out_shape, scratch, scal, aliases
     )
     if final is not None:
         return outs
-    new = {}
+    new = dict(state or {})
     for i, user in enumerate(users):
         if first is not None:
             new[user] = (outs[1 + n + i], outs[1 + 2 * n + i], outs[1 + i])
@@ -283,10 +401,6 @@
 
 def to_cand(array, dz, dy):
     return lax.ppermute(array, "cand", cand_perm(dz, dy))
-
-
-def after(value, *others):
-    return lax.optimization_barrier((value, others))[0]
 
 
 def local(pooled, cand_feats, hist_len, cand_user, w_in, w_out):
@@ -305,98 +419,67 @@
     ).astype(jnp.int32)
 
     tables = pooled.reshape(NX, 2, 2, 2, SLOTS, D)
-
-    def block(j, core_at, x_at=None, y_at=None):
-        at = (0 if x_at is None else x_at, 0 if y_at is None else y_at, core_at, j, 0, 0)
-        size = (NX if x_at is None else 1, 2 if y_at is None else 1, 1, 1, SLOTS, D)
-        return lax.dynamic_slice(tables, at, size).reshape(size[0], size[1], SLOTS, D)
-
-    def share(got, x_at=None, y_at=None):
-        at = (0 if x_at is None else x_at, 0 if y_at is None else y_at, 0, 0)
-        size = (NX if x_at is None else 1, 2 if y_at is None else 1, SLOTS, D)
-        return lax.dynamic_slice(got, at, size)
-
-    hop = [lax.rem(x + d, NX) for d in range(NX)]
+    place = jnp.stack([x, y, core]).astype(jnp.int32)
     with jax.named_scope("sum_core"):
-        pack0 = block(0, 1 - core)
+        pack1 = pack(place, tables, 1)
+        got1 = to_user(pack1, 0, 0, 1)
+        pack0 = pack(place, after(tables, pack1), 0)
         got0 = to_user(pack0, 0, 0, 1)
-        tables = after(tables, pack0)
-        got1 = to_user(block(1, 1 - core), 0, 0, 1)
+    with jax.named_scope("sum_y_second"):
+        over1 = over_y(place, tables, after(got1, pack0))
+        y1 = to_user(over1, 0, 1, 0)
     with jax.named_scope("sum_x_first"):
-        away = [
-            (block(0, core, x_at=hop[d]).astype(F32) + share(got0, x_at=hop[d]).astype(F32)).astype(BF16)[0]
-            for d in range(NX)
-        ]
-        x0 = [to_user(away[d], d, 0, 0) for d in (1, 3, 2)]
+        away0 = away_x(place, tables, after(got0, over1))
+        x0 = [to_user(away0[d], d, 0, 0) for d in (1, 3, 2)]
+    owner_row, scal = after((owner.reshape(1, ROWS), scal), away0)
+    xs, u_cand, q_cand, back, a_cand = cand_project(owner_row, cand_feats, w_in)
     with jax.named_scope("sum_y_second"):
-        got1 = after(got1, away)
-        over = (block(1, core, y_at=1 - y).astype(F32) + share(got1, y_at=1 - y).astype(F32)).astype(BF16)
-        y1 = to_user(over, 0, 1, 0)
-    owner_row = after(owner.reshape(1, ROWS), over)
-    xs, u_cand, q_cand, a_cand = cand_project(owner_row, cand_feats, w_in)
+        away1 = join_y(place, tables, got1, after(y1, xs, scal))
+        x1 = [to_user(away1[d], d, 0, 0) for d in (1, 3, 2)]
     with jax.named_scope("sum_x_first"):
-        x0 = after(x0, xs)
-        total0 = away[0].astype(F32)
-        for got in x0:
-            total0 = total0 + got.astype(F32)
-        y0 = to_user(lax.dynamic_index_in_dim(total0, 1 - y, 0, False).astype(BF16), 0, 1, 0)
-        mine0 = lax.dynamic_index_in_dim(total0, y, 0, False)
-    with jax.named_scope("sum_y_second"):
-        y1 = after(y1, mine0)
-        away1 = []
-        for d in range(NX):
-            part = (
-                block(1, core, x_at=hop[d], y_at=y).astype(F32)
-                + share(got1, x_at=hop[d], y_at=y).astype(F32)
-            )[0, 0]
-            part = part + share(y1, x_at=hop[d], y_at=0).astype(F32)[0, 0]
-            away1.append(part if d == 0 else part.astype(BF16))
-        x1 = [to_user(away1[d], d, 0, 0) for d in (1, 3, 2)]
+        mine0, over0 = join_x(place, away0[0], after(x0, away1))
+        y0 = to_user(over0, 0, 1, 0)
     with jax.named_scope("gather"):
-        y0 = after(y0, away1)
-        own0 = layer_norm(mine0 + y0.astype(F32)).astype(BF16)
-        pair0 = jnp.stack([own0, to_cand(own0, 0, 1)])
+        own1 = norm_sum(place, [away1[0]] + after(x1, mine0))
+        near1 = to_cand(own1, 0, 1)
+        own0 = norm_sum(place, [mine0, after(y0, own1)])
+        near0 = to_cand(own0, 0, 1)
+        pair1 = join_pair(place, own1, after(near1, own0))
+        z1 = {-1: to_cand(pair1, 1, 0), 1: to_cand(pair1, -1, 0)}
+        pair0 = join_pair(place, own0, after(near0, pair1))
         z0 = {-1: to_cand(pair0, 1, 0), 1: to_cand(pair0, -1, 0)}
     both = (0, 1)
     put = functools.partial(absorb, scal=scal, w_in=w_in, q_cand=q_cand)
-    a_cand, state0 = put("own_first", items=[(0, 0, both, pair0)], a_cand=a_cand, first={0: own0})
-    with jax.named_scope("gather"):
-        x1 = after(x1, a_cand)
-        total1 = away1[0]
-        for got in x1:
-            total1 = total1 + got.astype(F32)
-        own1 = layer_norm(total1).astype(BF16)
-        near1 = to_cand(own1, 0, 1)
-        z0 = after(z0, own1)
-        ends0 = [z0[-1][:1], z0[1][1:]]
-        far0 = [to_cand(ends0[0], 1, 0), to_cand(ends0[1], -1, 0)]
-        pair1 = jnp.stack([own1, after(near1, ends0)])
-        z1 = {-1: to_cand(pair1, 1, 0), 1: to_cand(pair1, -1, 0)}
-    a_cand, state0 = put(
-        "side_first",
-        items=[(0, -1, both, z0[-1]), (0, 1, both, z0[1])],
-        a_cand=after(a_cand, pair1),
-        state=state0,
-    )
-    a_cand, state1 = put("own_second", items=[(1, 0, both, pair1)], a_cand=a_cand, first={1: own1})
+    a_cand, state = put(
+        "own_pairs",
+        items=[(1, 0, both, pair1), (0, 0, both, pair0)],
+        a_cand=a_cand,
+        first={0: own0, 1: own1},
+    )
     with jax.named_scope("gather"):
         z1 = after(z1, a_cand)
-        ends1 = [z1[-1][:1], z1[1][1:]]
-        far1 = [to_cand(ends1[0], 1, 0), to_cand(ends1[1], -1, 0)]
-    a_cand, state1 = put(
+        far1 = to_cand(z1[1], -1, 0)
+    a_cand, state = put(
         "side_second",
         items=[(1, -1, both, z1[-1]), (1, 1, both, z1[1])],
-        a_cand=after(a_cand, ends1),
-        state=state1,
+        a_cand=a_cand,
+        state=state,
+    )
+    with jax.named_scope("gather"):
+        z0 = after(z0, a_cand)
+        far0 = to_cand(z0[-1], 1, 0)
+    a_cand, state = put(
+        "side_first",
+        items=[(0, -1, both, z0[-1]), (0, 1, both, z0[1]), (1, 2, both, far1)],
+        a_cand=a_cand,
+        state=state,
     )
     return put(
         "far_finish",
-        items=[(0, 2, (0,), far0[0]), (0, 2, (1,), far0[1]), (1, 2, (0,), far1[0]), (1, 2, (1,), far1[1])],
+        items=[(0, 2, both, far0)],
         a_cand=a_cand,
-        state={**state0, **state1},
-        final=dict(
-            own={0: own0, 1: own1}, u=u_cand, xs=xs, owner=owner.reshape(ROWS, 1), w_out=w_out
-        ),
+        state=state,
+        final=dict(own={0: own0, 1: own1}, u=u_cand, xs=xs, back=back, w_out=w_out),
     )
 
 

time: 138 us -> 120 us (0.87)
  local copies, waits for them, and re-layouts: 30.8 us -> 5.46 us
  Pallas kernels: 42.1 us -> 60.9 us
  other arithmetic: 16.3 us -> 0.74 us
  waiting for transfers between devices: 14.3 us -> 20.4 us
  starting transfers between devices: 32.2 us -> 30.3 us
    pallas_call x0 -> x10, Pallas kernels: none -> 20.4 us  [block_sums(): pl.pallas_call(body, in_specs=[pl.BlockSpec(memory_space=pltpu.SMEM)] + [...]
    unnamed x68 -> x18, local copies, waits for them, and re-layouts: 18.6 us -> 3.42 us
    ppermute x10 -> x8, waiting for transfers between devices: 4.22 us -> 11.7 us  [to_cand(): return lax.ppermute(array, 'cand', cand_perm(dz, dy))]
    reshape x3 -> x0, local copies, waits for them, and re-layouts: 7.08 us -> none  [the longest x2 6.22 us: block(): lax.dynamic_slice(tables, at, size).reshape(size[0], size[1], SLOTS, D)]
    convert_element_type x4 -> x0, other arithmetic: 6.52 us -> none  [the longest x1 3.26 us: local(): (block(1, core, y_at=1 - y).astype(F32) + share(got1, y_at=1 - y).astype(...]
    squeeze x1 -> x0, other arithmetic: 4.23 us -> none  [local(): (block(0, core, x_at=hop[d]).astype(F32) + share(got0, x_at=hop[d]).astyp...]
    ppermute x10 -> x8, starting transfers between devices: 19.6 us -> 15.9 us  [to_cand(): return lax.ppermute(array, 'cand', cand_perm(dz, dy))]
    slice x4 -> x0, local copies, waits for them, and re-layouts: 3.01 us -> none  [the longest x2 1.54 us: local(): ends1 = [z1[-1][:1], z1[1][1:]]]
  transfers between devices with their start and end apart: 20 -> 18, of which waited for: 5 -> 8; matrix products, arithmetic and copies ran while one was open for 18% -> 2% of each run, Pallas kernels for 21% -> 41%
where the time goes in v2:
time: 120 us; the launch traced here: 119 us
  Pallas kernels  60.9 us (51%)
  starting transfers between devices  30.3 us (25%)
  waiting for transfers between devices  20.4 us (17%)
  local copies, waits for them, and re-layouts  5.46 us (5%)
  between operations  1.52 us (1%)
    pallas_call x5, Pallas kernels, kernel_call(): pl.pallas_call(body, in_specs=in_specs, out_specs=[vmem] * len(out_shape)...  40.5 us
    pallas_call x10, Pallas kernels, block_sums(): pl.pallas_call(body, in_specs=[pl.BlockSpec(memory_space=pltpu.SMEM)] + [...  20.4 us
    ppermute x8, starting transfers between devices, to_cand(): return lax.ppermute(array, 'cand', cand_perm(dz, dy))  15.9 us
    ppermute x10, starting transfers between devices, to_user(): return lax.ppermute(array, 'user', user_perm(dx, dy, dcore))  14.4 us
    ppermute x8, waiting for transfers between devices, to_cand(): return lax.ppermute(array, 'cand', cand_perm(dz, dy))  11.7 us
    ppermute x10, waiting for transfers between devices, to_user(): return lax.ppermute(array, 'user', user_perm(dx, dy, dcore))  8.68 us
    unnamed x18, local copies, waits for them, and re-layouts  3.42 us
  transfers between devices with their start and end apart: 18, of which 8 were waited for; matrix products, arithmetic and copies ran while one was open for 2% of the time, Pallas kernels for 41%

profile of v2, /device:TPU:0, one launch (start us, length us, event | category | flops | bytes accessed | tf_op | source)
XLA Modules:
  0.0 119.3 jit_solution(15186250255583781230)
XLA Ops:
  0.6 0.1 pad_add_fusion.1.scal_ref
  0.7 3.0 %pack.2 = bf16[4,2,128,1024]{3,2,1,0:T(8,128)(2,1)} custom-call(s32[3]{0:T(128)S(1)} %pad_add_fusion.1.scal_ref, bf16[4,2,2,2,128,1024]{5,4,3,2,1,0:T(8,128)(2,1)} %bitcast.20), custom_call_target="tpu_custom_call" | custom-call | flops 1000000 | bytes 65536 | tf_op jit(solution)/shard_map/sum_core/pack/pallas_call | solution.py:89
  3.7 0.1 collective-permute-start.1
  3.8 3.0 %pack.3 = bf16[4,2,128,1024]{3,2,1,0:T(8,128)(2,1)} custom-call(s32[3]{0:T(128)S(1)} %pad_add_fusion.1.scal_ref, bf16[4,2,2,2,128,1024]{5,4,3,2,1,0:T(8,128)(2,1)} %bitcast.21), custom_call_target="tpu_custom_call" | custom-call | flops 1000000 | bytes 65536 | tf_op jit(solution)/shard_map/sum_core/pack/pallas_call | solution.py:89
  6.8 0.6 collective-permute-start
  7.4 0.8 collective-permute-done.1.refs_1_
  8.2 2.6 %over_y.1 = bf16[4,128,1024]{2,1,0:T(8,128)(2,1)} custom-call(s32[3]{0:T(128)S(1)} %pad_add_fusion.1.scal_ref, bf16[4,2,2,2,128,1024]{5,4,3,2,1,0:T(8,128)(2,1)} %bitcast.22, bf16[4,2,128,1024]{3,2,1,0:T(8,128)(2,1)S(1)} %collective-permute-done.1.refs_1_), custom_call_target="tpu_custom_call" | custom-call | flops 1000000 | bytes 65536 | tf_op jit(solution)/shard_map/sum_y_second/over_y/pallas_call | solution.py:89
  10.8 0.0 copy-start.5
  10.8 0.0 copy-start.6
  10.8 0.0 copy-start.2
  10.8 1.7 %collective-permute-start.5 = (bf16[4,128,1024]{2,1,0:T(8,128)(2,1)}, bf16[4,128,1024]{2,1,0:T(8,128)(2,1)}, u32[]{:S(2)}, u32[]{:S(2)}) collective-permute-start(bf16[4,128,1024]{2,1,0:T(8,128)(2,1)} %over_y.1), channel_id=1, source_target_pairs={{0,16},{8,24},{16,0},{24,8},{32,48},{40,56},{48,32},{56,40},{64,80... | collective-permute-start | bytes 3145736 | tf_op jit(solution)/shard_map/sum_y_second/ppermute | solution.py:399
  12.6 0.0 collective-permute-done.refs_1_
  12.6 3.1 %away_x.1 = (bf16[2,128,1024]{2,1,0:T(8,128)(2,1)}, bf16[2,128,1024]{2,1,0:T(8,128)(2,1)}, bf16[2,128,1024]{2,1,0:T(8,128)(2,1)}, bf16[2,128,1024]{2,1,0:T(8,128)(2,1)}) custom-call(s32[3]{0:T(128)S(1)} %pad_add_fusion.1.scal_ref, bf16[4,2,2,2,128,1024]{5,4,3,2,1,0:T(8,128)(2,1)} %bitcast.23, bf16[4,2,128,1024]{3,2,1,0:T(8,128)(2,1)S(1)} %collective-permute-done.refs_1_), custom_call_target="tpu_custom_call" | custom-call | flops 1000000 | bytes 65536 | tf_op jit(solution)/shard_map/sum_x_first/away_x/pallas_call | solution.py:89
  15.7 1.6 %collective-permute-start.2 = (bf16[2,128,1024]{2,1,0:T(8,128)(2,1)}, bf16[2,128,1024]{2,1,0:T(8,128)(2,1)}, u32[]{:S(2)}, u32[]{:S(2)}) collective-permute-start(bf16[2,128,1024]{2,1,0:T(8,128)(2,1)} %get-tuple-element.52), channel_id=1, source_target_pairs={{0,32},{8,40},{16,48},{24,56},{32,64},{40,72},{48,80},{56,88},{64,... | collective-permute-start | bytes 1572872 | tf_op jit(solution)/shard_map/sum_x_first/ppermute | solution.py:399
  17.2 1.7 %collective-permute-start.3 = (bf16[2,128,1024]{2,1,0:T(8,128)(2,1)}, bf16[2,128,1024]{2,1,0:T(8,128)(2,1)}, u32[]{:S(2)}, u32[]{:S(2)}) collective-permute-start(bf16[2,128,1024]{2,1,0:T(8,128)(2,1)} %get-tuple-element.54), channel_id=1, source_target_pairs={{0,96},{8,104},{16,112},{24,120},{32,0},{40,8},{48,16},{56,24},{64... | collective-permute-start | bytes 1572872 | tf_op jit(solution)/shard_map/sum_x_first/ppermute | solution.py:399
  19.0 1.8 %collective-permute-start.4 = (bf16[2,128,1024]{2,1,0:T(8,128)(2,1)}, bf16[2,128,1024]{2,1,0:T(8,128)(2,1)}, u32[]{:S(2)}, u32[]{:S(2)}) collective-permute-start(bf16[2,128,1024]{2,1,0:T(8,128)(2,1)} %get-tuple-element.53), channel_id=1, source_target_pairs={{0,64},{8,72},{16,80},{24,88},{32,96},{40,104},{48,112},{56,120},{... | collective-permute-start | bytes 1572872 | tf_op jit(solution)/shard_map/sum_x_first/ppermute | solution.py:399
  20.8 0.7 fusion
  22.1 0.6 fusion.1
  22.7 0.7 stack.77
  23.4 0.7 stack.79
  24.2 0.0 copy-done.2
  24.2 0.0 copy-start
  24.2 3.4 %copy-done = bf16[1024,4096]{1,0:T(8,128)(2,1)S(1)} copy-done((bf16[1024,4096]{1,0:T(8,128)(2,1)S(1)}, bf16[1024,4096]{1,0:T(8,128)(2,1)}, u32[]{:S(2)}) %copy-start) | copy-done | bytes 8388632
  27.6 7.7 %cand_project.1 = (bf16[512,1024]{1,0:T(8,128)(2,1)S(1)}, bf16[512,1024]{1,0:T(8,128)(2,1)S(1)}, bf16[512,1024]{1,0:T(8,128)(2,1)S(1)}, bf16[512,512]{1,0:T(8,128)(2,1)S(1)}, f32[512,1024]{1,0:T(8,128)S(1)}) custom-call(s32[1,512]{1,0:T(1,128)S(1)} %bitcast.19, bf16[512,1024]{1,0:T(8,128)(2,1)S(1)} %copy-done.2, bf16[1024,4096]{1,0:T(8,128)(2,1)S(1)} %copy-done), custom_call_target="tpu_custom_call" | custom-call | flops 1000000 | bytes 65536 | tf_op jit(solution)/shard_map/cand_project/pallas_call | solution.py:182
  35.3 1.2 collective-permute-done.5.refs_2_
  36.4 3.2 %join_y.1 = (f32[128,1024]{1,0:T(8,128)}, bf16[128,1024]{1,0:T(8,128)(2,1)}, bf16[128,1024]{1,0:T(8,128)(2,1)}, bf16[128,1024]{1,0:T(8,128)(2,1)}) custom-call(s32[3]{0:T(128)S(1)} %pad_add_fusion.1.scal_ref, bf16[4,2,2,2,128,1024]{5,4,3,2,1,0:T(8,128)(2,1)} %bitcast.24, bf16[4,2,128,1024]{3,2,1,0:T(8,128)(2,1)S(1)} %collective-permute-done.1.refs_1_, ...), custom_call_target="tpu_custom_call" | custom-call | flops 1000000 | bytes 65536 | tf_op jit(solution)/shard_map/sum_y_second/join_y/pallas_call | solution.py:89
  39.7 0.0 copy-start.4
  39.7 1.6 %collective-permute-start.7 = (bf16[128,1024]{1,0:T(8,128)(2,1)}, bf16[128,1024]{1,0:T(8,128)(2,1)S(1)}, u32[]{:S(2)}, u32[]{:S(2)}) collective-permute-start(bf16[128,1024]{1,0:T(8,128)(2,1)} %get-tuple-element.60), channel_id=1, source_target_pairs={{0,32},{8,40},{16,48},{24,56},{32,64},{40,72},{48,80},{56,88},{64,... | collective-permute-start | bytes 786440 | tf_op jit(solution)/shard_map/sum_y_second/ppermute | solution.py:399
  41.3 1.7 %collective-permute-start.8 = (bf16[128,1024]{1,0:T(8,128)(2,1)}, bf16[128,1024]{1,0:T(8,128)(2,1)S(1)}, u32[]{:S(2)}, u32[]{:S(2)}) collective-permute-start(bf16[128,1024]{1,0:T(8,128)(2,1)} %get-tuple-element.62), channel_id=1, source_target_pairs={{0,96},{8,104},{16,112},{24,120},{32,0},{40,8},{48,16},{56,24},{64... | collective-permute-start | bytes 786440 | tf_op jit(solution)/shard_map/sum_y_second/ppermute | solution.py:399
  43.0 0.0 collective-permute-done.2.refs_1_
  43.0 1.9 %collective-permute-start.9 = (bf16[128,1024]{1,0:T(8,128)(2,1)}, bf16[128,1024]{1,0:T(8,128)(2,1)S(1)}, u32[]{:S(2)}, u32[]{:S(2)}) collective-permute-start(bf16[128,1024]{1,0:T(8,128)(2,1)} %get-tuple-element.61), channel_id=1, source_target_pairs={{0,64},{8,72},{16,80},{24,88},{32,96},{40,104},{48,112},{56,120},{... | collective-permute-start | bytes 786440 | tf_op jit(solution)/shard_map/sum_y_second/ppermute | solution.py:399
  44.9 0.0 collective-permute-done.3.refs_2_
  44.9 0.0 collective-permute-done.4.refs_3_
  44.9 2.1 %join_x.1 = (f32[128,1024]{1,0:T(8,128)S(1)}, bf16[128,1024]{1,0:T(8,128)(2,1)S(1)}) custom-call(s32[3]{0:T(128)S(1)} %pad_add_fusion.1.scal_ref, bf16[2,128,1024]{2,1,0:T(8,128)(2,1)S(1)} %copy-done.3, bf16[2,128,1024]{2,1,0:T(8,128)(2,1)} %collective-permute-done.2.refs_1_, bf16[2,128,1024]{2,1,0:T(8,128)(2,1)} %collective-permute-done.3.refs_2_, ...), custom_call_target="tpu_custom_call" | custom-call | flops 1000000 | bytes 65536 | tf_op jit(solution)/shard_map/sum_x_first/join_x/pallas_call | solution.py:89
  47.0 1.7 %collective-permute-start.6 = (bf16[128,1024]{1,0:T(8,128)(2,1)S(1)}, bf16[128,1024]{1,0:T(8,128)(2,1)S(1)}, u32[]{:S(2)}, u32[]{:S(2)}) collective-permute-start(bf16[128,1024]{1,0:T(8,128)(2,1)S(1)} %get-tuple-element.67), channel_id=1, source_target_pairs={{0,16},{8,24},{16,0},{24,8},{32,48},{40,56},{48,32},{56,40},{64,80... | collective-permute-start | bytes 786440 | tf_op jit(solution)/shard_map/sum_x_first/ppermute | solution.py:399
  48.7 0.7 collective-permute-done.7.refs_1_
  49.4 1.4 %collective-permute-done.8.refs_2_ = bf16[128,1024]{1,0:T(8,128)(2,1)S(1)} collective-permute-done((bf16[128,1024]{1,0:T(8,128)(2,1)}, bf16[128,1024]{1,0:T(8,128)(2,1)S(1)}, u32[]{:S(2)}, u32[]{:S(2)}) %collective-permute-start.8) | collective-permute-done | bytes 262176 | tf_op jit(solution)/shard_map/sum_y_second/ppermute | solution.py:399
  50.8 4.6 %collective-permute-done.9.refs_3_ = bf16[128,1024]{1,0:T(8,128)(2,1)S(1)} collective-permute-done((bf16[128,1024]{1,0:T(8,128)(2,1)}, bf16[128,1024]{1,0:T(8,128)(2,1)S(1)}, u32[]{:S(2)}, u32[]{:S(2)}) %collective-permute-start.9) | collective-permute-done | bytes 262176 | tf_op jit(solution)/shard_map/sum_y_second/ppermute | solution.py:399
  55.4 1.1 norm_sum.2.refs_0_.refs_6_.refs_10_
  56.5 3.3 %collective-permute-start.11 = (bf16[128,1024]{1,0:T(8,128)(2,1)S(1)}, bf16[128,1024]{1,0:T(8,128)(2,1)S(1)}, u32[]{:S(2)}, u32[]{:S(2)}) collective-permute-start(bf16[128,1024]{1,0:T(8,128)(2,1)S(1)} %norm_sum.2.refs_0_.refs_6_.refs_10_), channel_id=1, source_target_pairs={{0,1},{1,0},{2,3},{3,2},{4,5},{5,4},{6,7},{7,6},{8,9},{9,8},{10,11... | collective-permute-start | bytes 786440 | tf_op jit(solution)/shard_map/gather/ppermute | solution.py:403
  59.8 0.0 collective-permute-done.6.refs_1_
  59.8 0.9 norm_sum.3.refs_0_.refs_5_.refs_9_
  60.7 0.6 collective-permute-start.10
  61.3 5.2 %collective-permute-done.11.refs_1_ = bf16[128,1024]{1,0:T(8,128)(2,1)S(1)} collective-permute-done((bf16[128,1024]{1,0:T(8,128)(2,1)S(1)}, bf16[128,1024]{1,0:T(8,128)(2,1)S(1)}, u32[]{:S(2)}, u32[]{:S(2)}) %collective-permute-start.11) | collective-permute-done | bytes 262176 | tf_op jit(solution)/shard_map/gather/ppermute | solution.py:403
  66.5 0.7 join_pair.2.refs_0_
  67.2 2.0 %collective-permute-start.14 = (bf16[2,128,1024]{2,1,0:T(8,128)(2,1)S(1)}, bf16[2,128,1024]{2,1,0:T(8,128)(2,1)S(1)}, u32[]{:S(2)}, u32[]{:S(2)}) collective-permute-start(bf16[2,128,1024]{2,1,0:T(8,128)(2,1)S(1)} %join_pair.2.refs_0_), channel_id=1, source_target_pairs={{0,2},{1,3},{2,4},{3,5},{4,6},{5,7},{6,0},{7,1},{8,10},{9,11},{10,... | collective-permute-start | bytes 1572872 | tf_op jit(solution)/shard_map/gather/ppermute | solution.py:403
  69.2 2.2 %collective-permute-start.15 = (bf16[2,128,1024]{2,1,0:T(8,128)(2,1)S(1)}, bf16[2,128,1024]{2,1,0:T(8,128)(2,1)S(1)}, u32[]{:S(2)}, u32[]{:S(2)}) collective-permute-start(bf16[2,128,1024]{2,1,0:T(8,128)(2,1)S(1)} %join_pair.2.refs_0_), channel_id=1, source_target_pairs={{0,6},{1,7},{2,0},{3,1},{4,2},{5,3},{6,4},{7,5},{8,14},{9,15},{10,... | collective-permute-start | bytes 1572872 | tf_op jit(solution)/shard_map/gather/ppermute | solution.py:403
  71.4 0.0 collective-permute-done.10.refs_1_
  71.4 0.7 join_pair.3.refs_1_
  72.1 0.9 collective-permute-start.12
  73.0 2.4 %collective-permute-start.13 = (bf16[2,128,1024]{2,1,0:T(8,128)(2,1)S(1)}, bf16[2,128,1024]{2,1,0:T(8,128)(2,1)S(1)}, u32[]{:S(2)}, u32[]{:S(2)}) collective-permute-start(bf16[2,128,1024]{2,1,0:T(8,128)(2,1)S(1)} %join_pair.3.refs_1_), channel_id=1, source_target_pairs={{0,6},{1,7},{2,0},{3,1},{4,2},{5,3},{6,4},{7,5},{8,14},{9,15},{10,... | collective-permute-start | bytes 1572872 | tf_op jit(solution)/shard_map/gather/ppermute | solution.py:403
  75.4 0.0 slice-done
  75.4 8.3 %own_pairs.1 = (f32[512,1024]{1,0:T(8,128)S(1)}, f32[128,1024]{1,0:T(8,128)S(1)}, f32[128,1024]{1,0:T(8,128)S(1)}, bf16[128,1024]{1,0:T(8,128)(2,1)S(1)}, bf16[1...) custom-call(s32[2,12]{1,0:T(2,128)S(1)} %pad_add_fusion.scal_ref, ...), custom_call_target="tpu_custom_call", output_to_operand_aliasing={{0}: (5, {})} | custom-call | flops 1000000 | bytes 65536 | tf_op jit(solution)/shard_map/own_pairs/pallas_call | solution.py:182
  83.7 0.0 collective-permute-done.14.refs_0_
  83.7 0.0 collective-permute-done.15.refs_1_
  83.7 2.7 %collective-permute-start.17 = (bf16[2,128,1024]{2,1,0:T(8,128)(2,1)S(1)}, bf16[2,128,1024]{2,1,0:T(8,128)(2,1)S(1)}, u32[]{:S(2)}, u32[]{:S(2)}) collective-permute-start(bf16[2,128,1024]{2,1,0:T(8,128)(2,1)S(1)} %collective-permute-done.15.refs_1_), channel_id=1, source_target_pairs={{0,6},{1,7},{2,0},{3,1},{4,2},{5,3},{6,4},{7,5},{8,14},{9,15},{10,... | collective-permute-start | bytes 1572872 | tf_op jit(solution)/shard_map/gather/ppermute | solution.py:403
  86.5 6.3 %side_second.1 = (f32[512,1024]{1,0:T(8,128)S(1)}, f32[128,1024]{1,0:T(8,128)S(1)}) custom-call(s32[2,12]{1,0:T(2,128)S(1)} %pad_add_fusion.scal_ref, bf16[2,128,1024]{2,1,0:T(8,128)(2,1)S(1)} %collective-permute-done.14.refs_0_, bf16[2,128,1024]{2,1,0:T(8,128)(2,1)S(1)} %collective-permute-done.15.refs_1_, ...), custom_call_target="tpu_custom_call", output_to_operand_aliasing={{0}: (5, {}), {1}: (7, {})} | custom-call | flops 1000000 | bytes 65536 | tf_op jit(solution)/shard_map/side_second/pallas_call | solution.py:182
  92.7 0.0 collective-permute-done.12.refs_0_
  92.8 1.4 %collective-permute-done.13.refs_1_ = bf16[2,128,1024]{2,1,0:T(8,128)(2,1)S(1)} collective-permute-done((bf16[2,128,1024]{2,1,0:T(8,128)(2,1)S(1)}, bf16[2,128,1024]{2,1,0:T(8,128)(2,1)S(1)}, u32[]{:S(2)}, u32[]{:S(2)}) %collective-permute-start.13) | collective-permute-done | bytes 524320 | tf_op jit(solution)/shard_map/gather/ppermute | solution.py:403
  94.2 1.8 %collective-permute-start.16 = (bf16[2,128,1024]{2,1,0:T(8,128)(2,1)S(1)}, bf16[2,128,1024]{2,1,0:T(8,128)(2,1)S(1)}, u32[]{:S(2)}, u32[]{:S(2)}) collective-permute-start(bf16[2,128,1024]{2,1,0:T(8,128)(2,1)S(1)} %collective-permute-done.12.refs_0_), channel_id=1, source_target_pairs={{0,2},{1,3},{2,4},{3,5},{4,6},{5,7},{6,0},{7,1},{8,10},{9,11},{10,... | collective-permute-start | bytes 1572872 | tf_op jit(solution)/shard_map/gather/ppermute | solution.py:403
  96.0 5.0 %collective-permute-done.17.refs_2_ = bf16[2,128,1024]{2,1,0:T(8,128)(2,1)S(1)} collective-permute-done((bf16[2,128,1024]{2,1,0:T(8,128)(2,1)S(1)}, bf16[2,128,1024]{2,1,0:T(8,128)(2,1)S(1)}, u32[]{:S(2)}, u32[]{:S(2)}) %collective-permute-start.17) | collective-permute-done | bytes 524320 | tf_op jit(solution)/shard_map/gather/ppermute | solution.py:403
  101.0 9.5 %side_first.1 = (f32[512,1024]{1,0:T(8,128)S(1)}, f32[128,1024]{1,0:T(8,128)S(1)}, f32[128,1024]{1,0:T(8,128)S(1)}) custom-call(s32[2,12]{1,0:T(2,128)S(1)} %pad_add_fusion.scal_ref, bf16[2,128,1024]{2,1,0:T(8,128)(2,1)S(1)} %collective-permute-done.12.refs_0_, ...), custom_call_target="tpu_custom_call", output_to_operand_aliasing={{0}: (6, {}), {1}: (9, {}), {2}: (10, {})} | custom-call | flops 1000000 | bytes 65536 | tf_op jit(solution)/shard_map/side_first/pallas_call | solution.py:182
  110.5 0.0 collective-permute-done.16.refs_0_
  110.5 8.7 %far_finish.1 = (bf16[2,128,1024]{2,1,0:T(8,128)(2,1)}, bf16[512,1024]{1,0:T(8,128)(2,1)}) custom-call(s32[2,12]{1,0:T(2,128)S(1)} %pad_add_fusion.scal_ref, bf16[2,128,1024]{2,1,0:T(8,128)(2,1)S(1)} %collective-permute-done.16.refs_0_, bf16[1024,4096]{1,0:T(8,128)(2,1)S(1)} %bitcast.18, bf16[512,1024]{1,0:T(8,128)(2,1)S(1)} %get-tuple-element.74.refs_3_.refs_4_.refs_2_, ...), custom_call_target="tpu_custom_call" | custom-call | flops 1000000 | bytes 65536 | tf_op jit(solution)/shard_map/far_finish/pallas_call | solution.py:182
  (12 shorter events, 0.0 us)
Async XLA Ops:
  3.7 4.5 %collective-permute-start.1 = (bf16[4,2,128,1024]{3,2,1,0:T(8,128)(2,1)}, bf16[4,2,128,1024]{3,2,1,0:T(8,128)(2,1)S(1)}, u32[]{:S(2)}, u32[]{:S(2)}) collective-permute-start(bf16[4,2,128,1024]{3,2,1,0:T(8,128)(2,1)} %pack.2), channel_id=1, source_target_pairs={{0,8},{8,0},{16,24},{24,16},{32,40},{40,32},{48,56},{56,48},{64,72... | collective-permute-start | bytes 6291464 | tf_op jit(solution)/shard_map/sum_core/ppermute | solution.py:399
  6.8 5.8 %collective-permute-start = (bf16[4,2,128,1024]{3,2,1,0:T(8,128)(2,1)}, bf16[4,2,128,1024]{3,2,1,0:T(8,128)(2,1)S(1)}, u32[]{:S(2)}, u32[]{:S(2)}) collective-permute-start(bf16[4,2,128,1024]{3,2,1,0:T(8,128)(2,1)} %pack.3), channel_id=1, source_target_pairs={{0,8},{8,0},{16,24},{24,16},{32,40},{40,32},{48,56},{56,48},{64,72... | collective-permute-start | bytes 6291464 | tf_op jit(solution)/shard_map/sum_core/ppermute | solution.py:399
  10.8 10.0 %copy-start.5 = (s32[512]{0:T(512)S(1)}, s32[512]{0:T(512)}, u32[]{:S(2)}) copy-start(s32[512]{0:T(512)} %param.9) | copy-start | bytes 6148
  10.8 11.3 %copy-start.6 = (s32[2]{0:T(128)S(1)}, s32[2]{0:T(128)}, u32[]{:S(2)}) copy-start(s32[2]{0:T(128)} %param.8) | copy-start | bytes 28
  10.8 13.3 %copy-start.2 = (bf16[512,1024]{1,0:T(8,128)(2,1)S(1)}, bf16[512,1024]{1,0:T(8,128)(2,1)}, u32[]{:S(2)}) copy-start(bf16[512,1024]{1,0:T(8,128)(2,1)} %feats_ref.1) | copy-start | bytes 3145732
  10.8 25.6 %collective-permute-start.5 = (bf16[4,128,1024]{2,1,0:T(8,128)(2,1)}, bf16[4,128,1024]{2,1,0:T(8,128)(2,1)}, u32[]{:S(2)}, u32[]{:S(2)}) collective-permute-start(bf16[4,128,1024]{2,1,0:T(8,128)(2,1)} %over_y.1), channel_id=1, source_target_pairs={{0,16},{8,24},{16,0},{24,8},{32,48},{40,56},{48,32},{56,40},{64,80... | collective-permute-start | bytes 3145736 | tf_op jit(solution)/shard_map/sum_y_second/ppermute | solution.py:399
  15.7 27.3 %collective-permute-start.2 = (bf16[2,128,1024]{2,1,0:T(8,128)(2,1)}, bf16[2,128,1024]{2,1,0:T(8,128)(2,1)}, u32[]{:S(2)}, u32[]{:S(2)}) collective-permute-start(bf16[2,128,1024]{2,1,0:T(8,128)(2,1)} %get-tuple-element.52), channel_id=1, source_target_pairs={{0,32},{8,40},{16,48},{24,56},{32,64},{40,72},{48,80},{56,88},{64,... | collective-permute-start | bytes 1572872 | tf_op jit(solution)/shard_map/sum_x_first/ppermute | solution.py:399
  17.2 27.7 %collective-permute-start.3 = (bf16[2,128,1024]{2,1,0:T(8,128)(2,1)}, bf16[2,128,1024]{2,1,0:T(8,128)(2,1)}, u32[]{:S(2)}, u32[]{:S(2)}) collective-permute-start(bf16[2,128,1024]{2,1,0:T(8,128)(2,1)} %get-tuple-element.54), channel_id=1, source_target_pairs={{0,96},{8,104},{16,112},{24,120},{32,0},{40,8},{48,16},{56,24},{64... | collective-permute-start | bytes 1572872 | tf_op jit(solution)/shard_map/sum_x_first/ppermute | solution.py:399
  19.0 25.9 %collective-permute-start.4 = (bf16[2,128,1024]{2,1,0:T(8,128)(2,1)}, bf16[2,128,1024]{2,1,0:T(8,128)(2,1)}, u32[]{:S(2)}, u32[]{:S(2)}) collective-permute-start(bf16[2,128,1024]{2,1,0:T(8,128)(2,1)} %get-tuple-element.53), channel_id=1, source_target_pairs={{0,64},{8,72},{16,80},{24,88},{32,96},{40,104},{48,112},{56,120},{... | collective-permute-start | bytes 1572872 | tf_op jit(solution)/shard_map/sum_x_first/ppermute | solution.py:399
  24.2 3.4 %copy-start = (bf16[1024,4096]{1,0:T(8,128)(2,1)S(1)}, bf16[1024,4096]{1,0:T(8,128)(2,1)}, u32[]{:S(2)}) copy-start(bf16[1024,4096]{1,0:T(8,128)(2,1)} %refs_1_.1) | copy-start | bytes 25165828
  27.6 47.9 %slice-start = ((s8[8388608]{0:T(1024)(128)(4,1)}), s8[4194304]{0:T(1024)(128)(4,1)S(1)}, s32[]{:S(2)}) async-start(s8[8388608]{0:T(1024)(128)(4,1)} %bitcast.17), calls=%async_computation | async-start | bytes 8388608
  36.4 8.5 %copy-start.3 = (bf16[2,128,1024]{2,1,0:T(8,128)(2,1)S(1)}, bf16[2,128,1024]{2,1,0:T(8,128)(2,1)}, u32[]{:S(2)}) copy-start(bf16[2,128,1024]{2,1,0:T(8,128)(2,1)} %get-tuple-element.51.refs_0_) | copy-start | bytes 1572868
  36.4 39.0 %slice-start.1 = ((s8[8388608]{0:T(1024)(128)(4,1)}), s8[4194304]{0:T(1024)(128)(4,1)S(1)}, s32[]{:S(2)}) async-start(s8[8388608]{0:T(1024)(128)(4,1)} %bitcast.17), calls=%async_computation.1 | async-start | bytes 8388608
  39.7 15.7 %copy-start.4 = (f32[128,1024]{1,0:T(8,128)S(1)}, f32[128,1024]{1,0:T(8,128)}, u32[]{:S(2)}) copy-start(f32[128,1024]{1,0:T(8,128)} %get-tuple-element.59.refs_0_) | copy-start | bytes 1572868
  39.7 9.7 %collective-permute-start.7 = (bf16[128,1024]{1,0:T(8,128)(2,1)}, bf16[128,1024]{1,0:T(8,128)(2,1)S(1)}, u32[]{:S(2)}, u32[]{:S(2)}) collective-permute-start(bf16[128,1024]{1,0:T(8,128)(2,1)} %get-tuple-element.60), channel_id=1, source_target_pairs={{0,32},{8,40},{16,48},{24,56},{32,64},{40,72},{48,80},{56,88},{64,... | collective-permute-start | bytes 786440 | tf_op jit(solution)/shard_map/sum_y_second/ppermute | solution.py:399
  41.3 9.5 %collective-permute-start.8 = (bf16[128,1024]{1,0:T(8,128)(2,1)}, bf16[128,1024]{1,0:T(8,128)(2,1)S(1)}, u32[]{:S(2)}, u32[]{:S(2)}) collective-permute-start(bf16[128,1024]{1,0:T(8,128)(2,1)} %get-tuple-element.62), channel_id=1, source_target_pairs={{0,96},{8,104},{16,112},{24,120},{32,0},{40,8},{48,16},{56,24},{64... | collective-permute-start | bytes 786440 | tf_op jit(solution)/shard_map/sum_y_second/ppermute | solution.py:399
  43.0 12.4 %collective-permute-start.9 = (bf16[128,1024]{1,0:T(8,128)(2,1)}, bf16[128,1024]{1,0:T(8,128)(2,1)S(1)}, u32[]{:S(2)}, u32[]{:S(2)}) collective-permute-start(bf16[128,1024]{1,0:T(8,128)(2,1)} %get-tuple-element.61), channel_id=1, source_target_pairs={{0,64},{8,72},{16,80},{24,88},{32,96},{40,104},{48,112},{56,120},{... | collective-permute-start | bytes 786440 | tf_op jit(solution)/shard_map/sum_y_second/ppermute | solution.py:399
  47.0 12.8 %collective-permute-start.6 = (bf16[128,1024]{1,0:T(8,128)(2,1)S(1)}, bf16[128,1024]{1,0:T(8,128)(2,1)S(1)}, u32[]{:S(2)}, u32[]{:S(2)}) collective-permute-start(bf16[128,1024]{1,0:T(8,128)(2,1)S(1)} %get-tuple-element.67), channel_id=1, source_target_pairs={{0,16},{8,24},{16,0},{24,8},{32,48},{40,56},{48,32},{56,40},{64,80... | collective-permute-start | bytes 786440 | tf_op jit(solution)/shard_map/sum_x_first/ppermute | solution.py:399
  56.5 10.0 %collective-permute-start.11 = (bf16[128,1024]{1,0:T(8,128)(2,1)S(1)}, bf16[128,1024]{1,0:T(8,128)(2,1)S(1)}, u32[]{:S(2)}, u32[]{:S(2)}) collective-permute-start(bf16[128,1024]{1,0:T(8,128)(2,1)S(1)} %norm_sum.2.refs_0_.refs_6_.refs_10_), channel_id=1, source_target_pairs={{0,1},{1,0},{2,3},{3,2},{4,5},{5,4},{6,7},{7,6},{8,9},{9,8},{10,11... | collective-permute-start | bytes 786440 | tf_op jit(solution)/shard_map/gather/ppermute | solution.py:403
  60.7 10.7 %collective-permute-start.10 = (bf16[128,1024]{1,0:T(8,128)(2,1)S(1)}, bf16[128,1024]{1,0:T(8,128)(2,1)S(1)}, u32[]{:S(2)}, u32[]{:S(2)}) collective-permute-start(bf16[128,1024]{1,0:T(8,128)(2,1)S(1)} %norm_sum.3.refs_0_.refs_5_.refs_9_), channel_id=1, source_target_pairs={{0,1},{1,0},{2,3},{3,2},{4,5},{5,4},{6,7},{7,6},{8,9},{9,8},{10,11... | collective-permute-start | bytes 786440 | tf_op jit(solution)/shard_map/gather/ppermute | solution.py:403
  67.2 16.5 %collective-permute-start.14 = (bf16[2,128,1024]{2,1,0:T(8,128)(2,1)S(1)}, bf16[2,128,1024]{2,1,0:T(8,128)(2,1)S(1)}, u32[]{:S(2)}, u32[]{:S(2)}) collective-permute-start(bf16[2,128,1024]{2,1,0:T(8,128)(2,1)S(1)} %join_pair.2.refs_0_), channel_id=1, source_target_pairs={{0,2},{1,3},{2,4},{3,5},{4,6},{5,7},{6,0},{7,1},{8,10},{9,11},{10,... | collective-permute-start | bytes 1572872 | tf_op jit(solution)/shard_map/gather/ppermute | solution.py:403
  69.2 14.5 %collective-permute-start.15 = (bf16[2,128,1024]{2,1,0:T(8,128)(2,1)S(1)}, bf16[2,128,1024]{2,1,0:T(8,128)(2,1)S(1)}, u32[]{:S(2)}, u32[]{:S(2)}) collective-permute-start(bf16[2,128,1024]{2,1,0:T(8,128)(2,1)S(1)} %join_pair.2.refs_0_), channel_id=1, source_target_pairs={{0,6},{1,7},{2,0},{3,1},{4,2},{5,3},{6,4},{7,5},{8,14},{9,15},{10,... | collective-permute-start | bytes 1572872 | tf_op jit(solution)/shard_map/gather/ppermute | solution.py:403
  72.1 20.6 %collective-permute-start.12 = (bf16[2,128,1024]{2,1,0:T(8,128)(2,1)S(1)}, bf16[2,128,1024]{2,1,0:T(8,128)(2,1)S(1)}, u32[]{:S(2)}, u32[]{:S(2)}) collective-permute-start(bf16[2,128,1024]{2,1,0:T(8,128)(2,1)S(1)} %join_pair.3.refs_1_), channel_id=1, source_target_pairs={{0,2},{1,3},{2,4},{3,5},{4,6},{5,7},{6,0},{7,1},{8,10},{9,11},{10,... | collective-permute-start | bytes 1572872 | tf_op jit(solution)/shard_map/gather/ppermute | solution.py:403
  73.0 21.2 %collective-permute-start.13 = (bf16[2,128,1024]{2,1,0:T(8,128)(2,1)S(1)}, bf16[2,128,1024]{2,1,0:T(8,128)(2,1)S(1)}, u32[]{:S(2)}, u32[]{:S(2)}) collective-permute-start(bf16[2,128,1024]{2,1,0:T(8,128)(2,1)S(1)} %join_pair.3.refs_1_), channel_id=1, source_target_pairs={{0,6},{1,7},{2,0},{3,1},{4,2},{5,3},{6,4},{7,5},{8,14},{9,15},{10,... | collective-permute-start | bytes 1572872 | tf_op jit(solution)/shard_map/gather/ppermute | solution.py:403
  83.7 17.3 %collective-permute-start.17 = (bf16[2,128,1024]{2,1,0:T(8,128)(2,1)S(1)}, bf16[2,128,1024]{2,1,0:T(8,128)(2,1)S(1)}, u32[]{:S(2)}, u32[]{:S(2)}) collective-permute-start(bf16[2,128,1024]{2,1,0:T(8,128)(2,1)S(1)} %collective-permute-done.15.refs_1_), channel_id=1, source_target_pairs={{0,6},{1,7},{2,0},{3,1},{4,2},{5,3},{6,4},{7,5},{8,14},{9,15},{10,... | collective-permute-start | bytes 1572872 | tf_op jit(solution)/shard_map/gather/ppermute | solution.py:403
  94.2 16.3 %collective-permute-start.16 = (bf16[2,128,1024]{2,1,0:T(8,128)(2,1)S(1)}, bf16[2,128,1024]{2,1,0:T(8,128)(2,1)S(1)}, u32[]{:S(2)}, u32[]{:S(2)}) collective-permute-start(bf16[2,128,1024]{2,1,0:T(8,128)(2,1)S(1)} %collective-permute-done.12.refs_0_), channel_id=1, source_target_pairs={{0,2},{1,3},{2,4},{3,5},{4,6},{5,7},{6,0},{7,1},{8,10},{9,11},{10,... | collective-permute-start | bytes 1572872 | tf_op jit(solution)/shard_map/gather/ppermute | solution.py:403
  101.0 9.5 %copy-start.1 = (bf16[1024,1024]{1,0:T(8,128)(2,1)S(1)}, bf16[1024,1024]{1,0:T(8,128)(2,1)}, u32[]{:S(2)}) copy-start(bf16[1024,1024]{1,0:T(8,128)(2,1)} %refs_14_.1) | copy-start | bytes 6291460

commit v3 on v2

--- a/solution.py
+++ b/solution.py
@@ -164,9 +164,10 @@
     return block_sums("norm_sum", place, arrays, [((SLOTS, D), BF16)], [(0, (), parts, True)], False)[0]
 
 
-def join_pair(place, own, near):
-    sums = [(0, (n,), [(n, lambda s: ())], False) for n in range(2)]
-    return block_sums("join_pair", place, [own, near], [((2, SLOTS, D), BF16)], sums, False)[0]
+def norm_both(place, first, second):
+    parts = [(n, lambda s: ()) for n in range(len(first) + 1)]
+    sums = [(0, (1,), parts[-1:], False), (0, (0,), parts[:-1], True)]
+    return block_sums("norm_both", place, list(first) + [second], [((2, SLOTS, D), BF16)], sums, False)[0]
 
 
 def in_vmem(array):
@@ -229,82 +230,70 @@
 
 
 def absorb_kernel(plan, scal_ref, *refs):
-    users, every, first, final = plan["users"], plan["every"], plan["first"], plan["final"]
+    pieces, first, final = plan
+    count = len(pieces)
     refs = list(refs)
     take = lambda n: [refs.pop(0) for _ in range(n)]
-    keys = [(user, shift, e, ref) for (user, shift, es), ref in zip(plan["items"], take(len(plan["items"]))) for e in es]
+    x_refs = take(count)
     w_ref, q_ref, a_ref = take(3)
-    if first:
-        own_ref = dict(zip(users, take(len(users))))
+    if not first:
+        qh_ref, ah_ref = take(2)
+    if final:
+        uh_ref, own_ref, u_ref, xs_ref, back_ref, wo_ref, hist_ref, cand_ref = take(8)
+    elif first:
+        _, ah_ref, qh_ref, uh_ref = take(4)
     else:
-        qh_ref = dict(zip(users, take(len(users))))
-        ah_ref = dict(zip(every, take(len(every))))
-    if final:
-        uh_ref = dict(zip(every, take(len(every))))
-        xh_ref = dict(zip(every, take(len(every))))
-        u_ref, xs_ref, back_ref, wo_ref = take(4)
-        hist_ref, cand_ref = take(2)
-    else:
-        take(1)
-        if first:
-            ah_ref = dict(zip(users, take(len(users))))
-            qh_ref = dict(zip(users, take(len(users))))
-            uh_ref = dict(zip(users, take(len(users))))
-        else:
-            take(len(users))
+        take(2)
     k_scr, v_scr = take(2)
-    if final:
-        (y_scr,) = take(1)
     row_iota = lax.broadcasted_iota(jnp.int32, (SLOTS, 1), 0)
     ahead = lax.broadcasted_iota(jnp.int32, (SLOTS, SLOTS), 0) - lax.broadcasted_iota(
         jnp.int32, (SLOTS, SLOTS), 1
     )
-    for user in users:
-        length = scal_ref[user, 0]
-        row_lo = scal_ref[user, 1]
-        row_hi = scal_ref[user, 2]
-        my_off = scal_ref[user, 3]
-        mine_keys = [(shift, e, ref) for (u, shift, e, ref) in keys if u == user]
-        offs = [scal_ref[user, 4 + 2 * SHIFTS.index(shift) + e] for shift, e, _ in mine_keys]
-        n_keys = SLOTS * len(offs)
-
-        @pl.loop(0, D // GROUP)
-        def _(g):
-            cols = lambda n: pl.ds(pl.multiple_of(n * D + g * GROUP, GROUP), GROUP)
-            if first:
-                x_own = own_ref[user][...]
-                qh_ref[user][:, cols(0)] = silu(mm(x_own, w_ref[:, cols(2)])).astype(BF16)
-                uh_ref[user][:, cols(0)] = silu(mm(x_own, w_ref[:, cols(0)])).astype(BF16)
-                ah_ref[user][:, cols(0)] = jnp.zeros((SLOTS, GROUP), F32)
-            x = jnp.concatenate([ref[min(e, ref.shape[0] - 1)] for _, e, ref in mine_keys], axis=0)
-            k_scr[:n_keys, :] = silu(mm(x, w_ref[:, cols(3)])).astype(BF16)
-            v = silu(mm(x, w_ref[:, cols(1)])).astype(BF16)
-            for i, off in enumerate(offs):
-                piece = v[i * SLOTS : (i + 1) * SLOTS]
-                piece = jnp.where(row_iota < length - off, piece, jnp.zeros_like(piece))
-                v_scr[i * SLOTS : (i + 1) * SLOTS, :] = piece
-
-            def attend(start, count):
-                rows = pl.ds(start, count)
-                index = start + lax.broadcasted_iota(jnp.int32, (count, 1), 0)
+    offs = [scal_ref[0, 4 + piece] for piece in pieces]
+    my_off = scal_ref[0, 3]
+
+    @pl.loop(0, D // GROUP)
+    def _(g):
+        cols = lambda n: pl.ds(pl.multiple_of(n * D + g * GROUP, GROUP), GROUP)
+        if first:
+            own = x_refs[0][...].reshape(2 * SLOTS, D)
+            qh_ref[:, cols(0)] = silu(mm(own, w_ref[:, cols(2)])).astype(BF16)
+            uh_ref[:, cols(0)] = silu(mm(own, w_ref[:, cols(0)])).astype(BF16)
+            ah_ref[:, cols(0)] = jnp.zeros((2 * SLOTS, GROUP), F32)
+        x = jnp.concatenate([ref[...].reshape(2 * SLOTS, D) for ref in x_refs], axis=0)
+        k = silu(mm(x, w_ref[:, cols(3)])).astype(BF16)
+        v = silu(mm(x, w_ref[:, cols(1)])).astype(BF16)
+        for n in range(count):
+            to = slice(n * SLOTS, (n + 1) * SLOTS)
+            for user in (0, 1):
+                at = slice((2 * n + user) * SLOTS, (2 * n + user + 1) * SLOTS)
+                live = row_iota < scal_ref[user, 0] - offs[n]
+                k_scr[user, to, :] = k[at]
+                v_scr[user, to, :] = jnp.where(live, v[at], jnp.zeros_like(v[at]))
+
+        for user in (0, 1):
+            row_lo = scal_ref[user, 1]
+            row_hi = scal_ref[user, 2]
+            mine_rows = slice(user * SLOTS, (user + 1) * SLOTS)
+
+            def attend(start, n_rows):
+                rows = pl.ds(start, n_rows)
+                index = start + lax.broadcasted_iota(jnp.int32, (n_rows, 1), 0)
                 mine = (index >= row_lo) & (index < row_hi)
                 for h in range(GROUP // HD):
                     hc = slice(h * HD, (h + 1) * HD)
                     oc = pl.ds(pl.multiple_of(g * GROUP + h * HD, HD), HD)
-                    q = jnp.concatenate([q_ref[rows, oc], qh_ref[user][:, oc]], axis=0)
-                    total = None
-                    for n in range(0, n_keys, 2 * SLOTS):
-                        w = weights_of(q, k_scr[n : n + 2 * SLOTS, hc])
-                        parts = []
-                        for i in range(2):
-                            part = w[count:, i * SLOTS : (i + 1) * SLOTS]
-                            seen = ahead >= offs[n // SLOTS + i] - my_off
-                            parts.append(jnp.where(seen, part, 0.0).astype(BF16))
-                        w = jnp.concatenate([w[:count].astype(BF16), jnp.concatenate(parts, axis=1)], axis=0)
-                        pv = mm(w, v_scr[n : n + 2 * SLOTS, hc])
-                        total = pv if total is None else total + pv
-                    a_ref[rows, oc] += jnp.where(mine, total[:count], 0.0)
-                    ah_ref[user][:, oc] += total[count:]
+                    q = jnp.concatenate([q_ref[rows, oc], qh_ref[mine_rows, oc]], axis=0)
+                    w = weights_of(q, k_scr[user, :, hc])
+                    parts = []
+                    for n in range(count):
+                        part = w[n_rows:, n * SLOTS : (n + 1) * SLOTS]
+                        parts.append(jnp.where(ahead >= offs[n] - my_off, part, 0.0).astype(BF16))
+                    hist_w = jnp.concatenate(parts, axis=1)
+                    w = jnp.concatenate([w[:n_rows].astype(BF16), hist_w], axis=0)
+                    total = mm(w, v_scr[user, :, hc])
+                    a_ref[rows, oc] += jnp.where(mine, total[:n_rows], 0.0)
+                    ah_ref[mine_rows, oc] += total[n_rows:]
 
             start = jnp.minimum((row_lo // 16) * 16, ROWS - WINDOW)
             narrow = row_hi <= start + WINDOW
@@ -318,10 +307,10 @@
                 attend(0, ROWS)
 
     if final:
-        n_hist = SLOTS * len(every)
-        for i, user in enumerate(every):
-            y = layer_norm(ah_ref[user][...]) * uh_ref[user][...].astype(F32)
-            y_scr[i * SLOTS : (i + 1) * SLOTS, :] = y.astype(BF16)
+        (y_scr,) = take(1)
+        n_hist = 2 * SLOTS
+        y = layer_norm(ah_ref[...]) * uh_ref[...].astype(F32)
+        y_scr[:n_hist, :] = y.astype(BF16)
 
         @pl.loop(0, ROWS // SLOTS)
         def _(n):
@@ -333,54 +322,46 @@
         def _(g):
             cols = pl.ds(pl.multiple_of(g * GROUP, GROUP), GROUP)
             res = mm(y_scr[...], wo_ref[:, cols])
-            for i, user in enumerate(every):
-                out = res[i * SLOTS : (i + 1) * SLOTS] + xh_ref[user][:, cols].astype(F32)
-                keep = scal_ref[user, 3] + row_iota < scal_ref[user, 0]
+            for user in (0, 1):
+                out = res[user * SLOTS : (user + 1) * SLOTS] + own_ref[user, :, cols].astype(F32)
+                keep = my_off + row_iota < scal_ref[user, 0]
                 hist_ref[user, :, cols] = jnp.where(keep, out, 0.0).astype(BF16)
             done = (res[n_hist:] + xs_ref[:, cols].astype(F32)).astype(BF16)
             cand_ref[:, cols] = mm(back_ref[...], done).astype(BF16)
 
 
-def absorb(name, scal, items, w_in, q_cand, a_cand, first=None, state=None, final=None):
-    users = tuple(sorted({item[0] for item in items}))
-    every = (0, 1) if final is not None else users
-    plan = dict(items=tuple(item[:3] for item in items), users=users, every=every, first=first is not None, final=final is not None)
-    arrays = [item[3] for item in items] + [w_in, q_cand, a_cand]
-    n = len(users)
+def absorb(name, scal, items, w_in, q_cand, a_cand, state=None, final=None):
+    pieces = tuple(item[0] for item in items)
+    arrays = [item[1] for item in items] + [w_in, q_cand, a_cand]
     a_at = len(arrays)
-    sums = jax.ShapeDtypeStruct((SLOTS, D), F32)
-    rows = jax.ShapeDtypeStruct((SLOTS, D), BF16)
-    most = max(sum(len(item[2]) for item in items if item[0] == user) for user in users)
-    scratch = [pltpu.VMEM((most * SLOTS, GROUP), BF16)] * 2
-    out_shape = [jax.ShapeDtypeStruct((ROWS, D), F32)]
+    scratch = [pltpu.VMEM((2, len(pieces) * SLOTS, GROUP), BF16)] * 2
+    sums = jax.ShapeDtypeStruct((2 * SLOTS, D), F32)
+    rows = jax.ShapeDtypeStruct((2 * SLOTS, D), BF16)
+    out_shape = [jax.ShapeDtypeStruct((ROWS, D), F32), sums]
     aliases = {a_at: 0}
-    if first is not None:
-        arrays += [first[user] for user in users]
-        out_shape += [sums] * n + [rows] * (2 * n)
+    first = state is None
+    if first:
+        out_shape += [rows, rows]
     else:
-        arrays += [state[user][0] for user in users]
-        aliases.update({len(arrays) + 1 + i: 1 + i for i in range(n)})
-        arrays += [state[user][2] for user in every]
-        out_shape += [sums] * n
+        arrays += [state[0], state[2]]
+        aliases[a_at + 2] = 1
     if final is not None:
-        arrays += [state[user][1] for user in every]
-        arrays += [final["own"][user] for user in every]
-        arrays += [final["u"], final["xs"], final["back"], final["w_out"]]
+        arrays += [state[1]] + list(final)
         out_shape = [jax.ShapeDtypeStruct((2, SLOTS, D), BF16), jax.ShapeDtypeStruct((ROWS, D), BF16)]
         aliases = {}
         scratch.append(pltpu.VMEM((2 * SLOTS + ROWS, D), BF16))
     outs = kernel_call(
-        functools.partial(absorb_kernel, plan), name, arrays, out_shape, scratch, scal, aliases
+        functools.partial(absorb_kernel, (pieces, first, final is not None)),
+        name,
+        arrays,
+        out_shape,
+        scratch,
+        scal,
+        aliases,
     )
     if final is not None:
         return outs
-    new = dict(state or {})
-    for i, user in enumerate(users):
-        if first is not None:
-            new[user] = (outs[1 + n + i], outs[1 + 2 * n + i], outs[1 + i])
-        else:
-            new[user] = (state[user][0], state[user][1], outs[1 + i])
-    return outs[0], new
+    return outs[0], (outs[2], outs[3], outs[1]) if first else (state[0], state[1], outs[1])
 
 
 def user_perm(dx, dy, dcore):
@@ -441,45 +422,38 @@
         y0 = to_user(over0, 0, 1, 0)
     with jax.named_scope("gather"):
         own1 = norm_sum(place, [away1[0]] + after(x1, mine0))
-        near1 = to_cand(own1, 0, 1)
-        own0 = norm_sum(place, [mine0, after(y0, own1)])
-        near0 = to_cand(own0, 0, 1)
-        pair1 = join_pair(place, own1, after(near1, own0))
-        z1 = {-1: to_cand(pair1, 1, 0), 1: to_cand(pair1, -1, 0)}
-        pair0 = join_pair(place, own0, after(near0, pair1))
-        z0 = {-1: to_cand(pair0, 1, 0), 1: to_cand(pair0, -1, 0)}
-    both = (0, 1)
+        own = norm_both(place, [mine0, after(y0, own1)], own1)
+        near = to_cand(own, 0, 1)
+        own_left, own_right = to_cand(own, 1, 0), to_cand(own, -1, 0)
     put = functools.partial(absorb, scal=scal, w_in=w_in, q_cand=q_cand)
+    piece = lambda shift, e: 2 * SHIFTS.index(shift) + e
+    a_cand, state = put("own_keys", items=[(piece(0, 0), own)], a_cand=a_cand)
+    with jax.named_scope("gather"):
+        near = after(near, a_cand)
+        near_left, near_right = to_cand(near, 1, 0), to_cand(near, -1, 0)
+        own_left, own_right = after((own_left, own_right), near)
+        own_far = to_cand(own_left, 1, 0)
     a_cand, state = put(
-        "own_pairs",
-        items=[(1, 0, both, pair1), (0, 0, both, pair0)],
-        a_cand=a_cand,
-        first={0: own0, 1: own1},
-    )
-    with jax.named_scope("gather"):
-        z1 = after(z1, a_cand)
-        far1 = to_cand(z1[1], -1, 0)
-    a_cand, state = put(
-        "side_second",
-        items=[(1, -1, both, z1[-1]), (1, 1, both, z1[1])],
+        "own_sides",
+        items=[(piece(-1, 0), own_left), (piece(1, 0), own_right), (piece(0, 1), near)],
         a_cand=a_cand,
         state=state,
     )
     with jax.named_scope("gather"):
-        z0 = after(z0, a_cand)
-        far0 = to_cand(z0[-1], 1, 0)
+        near_left, near_right = after((near_left, near_right), a_cand)
+        near_far = to_cand(near_right, -1, 0)
     a_cand, state = put(
-        "side_first",
-        items=[(0, -1, both, z0[-1]), (0, 1, both, z0[1]), (1, 2, both, far1)],
+        "near_sides",
+        items=[(piece(-1, 1), near_left), (piece(1, 1), near_right), (piece(2, 0), own_far)],
         a_cand=a_cand,
         state=state,
     )
     return put(
         "far_finish",
-        items=[(0, 2, both, far0)],
+        items=[(piece(2, 1), near_far)],
         a_cand=a_cand,
         state=state,
-        final=dict(own={0: own0, 1: own1}, u=u_cand, xs=xs, back=back, w_out=w_out),
+        final=(own, u_cand, xs, back, w_out),
     )
 
 

time: 120 us -> 121 us (level)
  starting transfers between devices: 30.3 us -> 27.4 us
  waiting for transfers between devices: 20.4 us -> 22.6 us
    ppermute x8 -> x7, starting transfers between devices: 15.9 us -> 11.8 us  [to_cand(): return lax.ppermute(array, 'cand', cand_perm(dz, dy))]
    ppermute x8 -> x7, waiting for transfers between devices: 11.7 us -> 15.3 us  [to_cand(): return lax.ppermute(array, 'cand', cand_perm(dz, dy))]
    pallas_call x5, Pallas kernels: 40.5 us -> 42.7 us  [kernel_call(): pl.pallas_call(body, in_specs=in_specs, out_specs=[vmem] * len(out_shape)...]
    ppermute x10, waiting for transfers between devices: 8.68 us -> 7.3 us  [to_user(): return lax.ppermute(array, 'user', user_perm(dx, dy, dcore))]
    pallas_call x10 -> x8, Pallas kernels: 20.4 us -> 19.2 us  [block_sums(): pl.pallas_call(body, in_specs=[pl.BlockSpec(memory_space=pltpu.SMEM)] + [...]
    ppermute x10, starting transfers between devices: 14.4 us -> 15.6 us  [to_user(): return lax.ppermute(array, 'user', user_perm(dx, dy, dcore))]
  transfers between devices with their start and end apart: 18 -> 17, of which waited for: 8 -> 9; matrix products, arithmetic and copies ran while one was open for 2% -> 2% of each run, Pallas kernels for 41% -> 40%
where the time goes in v3:
time: 121 us; the launch traced here: 120 us
  Pallas kernels  61.9 us (51%)
  starting transfers between devices  27.4 us (23%)
  waiting for transfers between devices  22.6 us (19%)
  local copies, waits for them, and re-layouts  5.52 us (5%)
  between operations  1.57 us (1%)
    pallas_call x5, Pallas kernels, kernel_call(): pl.pallas_call(body, in_specs=in_specs, out_specs=[vmem] * len(out_shape)...  42.7 us
    pallas_call x8, Pallas kernels, block_sums(): pl.pallas_call(body, in_specs=[pl.BlockSpec(memory_space=pltpu.SMEM)] + [...  19.2 us
    ppermute x10, starting transfers between devices, to_user(): return lax.ppermute(array, 'user', user_perm(dx, dy, dcore))  15.6 us
    ppermute x7, waiting for transfers between devices, to_cand(): return lax.ppermute(array, 'cand', cand_perm(dz, dy))  15.3 us
    ppermute x7, starting transfers between devices, to_cand(): return lax.ppermute(array, 'cand', cand_perm(dz, dy))  11.8 us
    ppermute x10, waiting for transfers between devices, to_user(): return lax.ppermute(array, 'user', user_perm(dx, dy, dcore))  7.3 us
    unnamed x18, local copies, waits for them, and re-layouts  3.42 us
  transfers between devices with their start and end apart: 17, of which 9 were waited for; matrix products, arithmetic and copies ran while one was open for 2% of the time, Pallas kernels for 40%

profile of v3, /device:TPU:0, one launch (start us, length us, event | category | flops | bytes accessed | tf_op | source)
XLA Modules:
  0.0 119.7 jit_solution(10185647816101539308)
XLA Ops:
  0.6 0.1 pad_add_fusion.1.scal_ref
  0.7 3.0 %pack.2 = bf16[4,2,128,1024]{3,2,1,0:T(8,128)(2,1)} custom-call(s32[3]{0:T(128)S(1)} %pad_add_fusion.1.scal_ref, bf16[4,2,2,2,128,1024]{5,4,3,2,1,0:T(8,128)(2,1)} %bitcast.20), custom_call_target="tpu_custom_call" | custom-call | flops 1000000 | bytes 65536 | tf_op jit(solution)/shard_map/sum_core/pack/pallas_call | solution.py:89
  3.7 0.1 collective-permute-start.1
  3.8 3.0 %pack.3 = bf16[4,2,128,1024]{3,2,1,0:T(8,128)(2,1)} custom-call(s32[3]{0:T(128)S(1)} %pad_add_fusion.1.scal_ref, bf16[4,2,2,2,128,1024]{5,4,3,2,1,0:T(8,128)(2,1)} %bitcast.21), custom_call_target="tpu_custom_call" | custom-call | flops 1000000 | bytes 65536 | tf_op jit(solution)/shard_map/sum_core/pack/pallas_call | solution.py:89
  6.8 0.6 collective-permute-start
  7.4 0.8 collective-permute-done.1.refs_1_
  8.2 2.6 %over_y.1 = bf16[4,128,1024]{2,1,0:T(8,128)(2,1)} custom-call(s32[3]{0:T(128)S(1)} %pad_add_fusion.1.scal_ref, bf16[4,2,2,2,128,1024]{5,4,3,2,1,0:T(8,128)(2,1)} %bitcast.22, bf16[4,2,128,1024]{3,2,1,0:T(8,128)(2,1)S(1)} %collective-permute-done.1.refs_1_), custom_call_target="tpu_custom_call" | custom-call | flops 1000000 | bytes 65536 | tf_op jit(solution)/shard_map/sum_y_second/over_y/pallas_call | solution.py:89
  10.8 0.0 copy-start.5
  10.8 0.0 copy-start.6
  10.8 0.0 copy-start.2
  10.8 1.7 %collective-permute-start.5 = (bf16[4,128,1024]{2,1,0:T(8,128)(2,1)}, bf16[4,128,1024]{2,1,0:T(8,128)(2,1)}, u32[]{:S(2)}, u32[]{:S(2)}) collective-permute-start(bf16[4,128,1024]{2,1,0:T(8,128)(2,1)} %over_y.1), channel_id=1, source_target_pairs={{0,16},{8,24},{16,0},{24,8},{32,48},{40,56},{48,32},{56,40},{64,80... | collective-permute-start | bytes 3145736 | tf_op jit(solution)/shard_map/sum_y_second/ppermute | solution.py:380
  12.6 0.0 collective-permute-done.refs_1_
  12.6 3.1 %away_x.1 = (bf16[2,128,1024]{2,1,0:T(8,128)(2,1)}, bf16[2,128,1024]{2,1,0:T(8,128)(2,1)}, bf16[2,128,1024]{2,1,0:T(8,128)(2,1)}, bf16[2,128,1024]{2,1,0:T(8,128)(2,1)}) custom-call(s32[3]{0:T(128)S(1)} %pad_add_fusion.1.scal_ref, bf16[4,2,2,2,128,1024]{5,4,3,2,1,0:T(8,128)(2,1)} %bitcast.23, bf16[4,2,128,1024]{3,2,1,0:T(8,128)(2,1)S(1)} %collective-permute-done.refs_1_), custom_call_target="tpu_custom_call" | custom-call | flops 1000000 | bytes 65536 | tf_op jit(solution)/shard_map/sum_x_first/away_x/pallas_call | solution.py:89
  15.7 1.6 %collective-permute-start.2 = (bf16[2,128,1024]{2,1,0:T(8,128)(2,1)}, bf16[2,128,1024]{2,1,0:T(8,128)(2,1)}, u32[]{:S(2)}, u32[]{:S(2)}) collective-permute-start(bf16[2,128,1024]{2,1,0:T(8,128)(2,1)} %get-tuple-element.47), channel_id=1, source_target_pairs={{0,32},{8,40},{16,48},{24,56},{32,64},{40,72},{48,80},{56,88},{64,... | collective-permute-start | bytes 1572872 | tf_op jit(solution)/shard_map/sum_x_first/ppermute | solution.py:380
  17.2 2.7 %collective-permute-start.4 = (bf16[2,128,1024]{2,1,0:T(8,128)(2,1)}, bf16[2,128,1024]{2,1,0:T(8,128)(2,1)}, u32[]{:S(2)}, u32[]{:S(2)}) collective-permute-start(bf16[2,128,1024]{2,1,0:T(8,128)(2,1)} %get-tuple-element.48), channel_id=1, source_target_pairs={{0,64},{8,72},{16,80},{24,88},{32,96},{40,104},{48,112},{56,120},{... | collective-permute-start | bytes 1572872 | tf_op jit(solution)/shard_map/sum_x_first/ppermute | solution.py:380
  20.0 1.4 %collective-permute-start.3 = (bf16[2,128,1024]{2,1,0:T(8,128)(2,1)}, bf16[2,128,1024]{2,1,0:T(8,128)(2,1)}, u32[]{:S(2)}, u32[]{:S(2)}) collective-permute-start(bf16[2,128,1024]{2,1,0:T(8,128)(2,1)} %get-tuple-element.49), channel_id=1, source_target_pairs={{0,96},{8,104},{16,112},{24,120},{32,0},{40,8},{48,16},{56,24},{64... | collective-permute-start | bytes 1572872 | tf_op jit(solution)/shard_map/sum_x_first/ppermute | solution.py:380
  21.4 0.0 copy-done.5
  21.4 0.7 fusion
  22.8 0.0 copy-done.6
  22.8 0.6 fusion.1
  23.4 0.7 stack.79
  24.1 0.8 stack.77
  24.9 0.0 copy-done.2
  24.9 0.0 copy-start
  25.0 3.4 %copy-done = bf16[1024,4096]{1,0:T(8,128)(2,1)S(1)} copy-done((bf16[1024,4096]{1,0:T(8,128)(2,1)S(1)}, bf16[1024,4096]{1,0:T(8,128)(2,1)}, u32[]{:S(2)}) %copy-start) | copy-done | bytes 8388632
  28.3 7.7 %cand_project.1 = (bf16[512,1024]{1,0:T(8,128)(2,1)S(1)}, bf16[512,1024]{1,0:T(8,128)(2,1)S(1)}, bf16[512,1024]{1,0:T(8,128)(2,1)S(1)}, bf16[512,512]{1,0:T(8,128)(2,1)S(1)}, f32[512,1024]{1,0:T(8,128)S(1)}) custom-call(s32[1,512]{1,0:T(1,128)S(1)} %bitcast.19, bf16[512,1024]{1,0:T(8,128)(2,1)S(1)} %copy-done.2, bf16[1024,4096]{1,0:T(8,128)(2,1)S(1)} %copy-done), custom_call_target="tpu_custom_call" | custom-call | flops 1000000 | bytes 65536 | tf_op jit(solution)/shard_map/cand_project/pallas_call | solution.py:183
  36.0 0.4 collective-permute-done.5.refs_2_
  36.4 3.3 %join_y.1 = (f32[128,1024]{1,0:T(8,128)}, bf16[128,1024]{1,0:T(8,128)(2,1)}, bf16[128,1024]{1,0:T(8,128)(2,1)}, bf16[128,1024]{1,0:T(8,128)(2,1)}) custom-call(s32[3]{0:T(128)S(1)} %pad_add_fusion.1.scal_ref, bf16[4,2,2,2,128,1024]{5,4,3,2,1,0:T(8,128)(2,1)} %bitcast.24, bf16[4,2,128,1024]{3,2,1,0:T(8,128)(2,1)S(1)} %collective-permute-done.1.refs_1_, ...), custom_call_target="tpu_custom_call" | custom-call | flops 1000000 | bytes 65536 | tf_op jit(solution)/shard_map/sum_y_second/join_y/pallas_call | solution.py:89
  39.8 0.0 copy-start.4
  39.8 1.6 %collective-permute-start.7 = (bf16[128,1024]{1,0:T(8,128)(2,1)}, bf16[128,1024]{1,0:T(8,128)(2,1)S(1)}, u32[]{:S(2)}, u32[]{:S(2)}) collective-permute-start(bf16[128,1024]{1,0:T(8,128)(2,1)} %get-tuple-element.55), channel_id=1, source_target_pairs={{0,32},{8,40},{16,48},{24,56},{32,64},{40,72},{48,80},{56,88},{64,... | collective-permute-start | bytes 786440 | tf_op jit(solution)/shard_map/sum_y_second/ppermute | solution.py:380
  41.4 2.7 %collective-permute-start.9 = (bf16[128,1024]{1,0:T(8,128)(2,1)}, bf16[128,1024]{1,0:T(8,128)(2,1)S(1)}, u32[]{:S(2)}, u32[]{:S(2)}) collective-permute-start(bf16[128,1024]{1,0:T(8,128)(2,1)} %get-tuple-element.56), channel_id=1, source_target_pairs={{0,64},{8,72},{16,80},{24,88},{32,96},{40,104},{48,112},{56,120},{... | collective-permute-start | bytes 786440 | tf_op jit(solution)/shard_map/sum_y_second/ppermute | solution.py:380
  44.1 0.0 collective-permute-done.2.refs_1_
  44.1 1.4 %collective-permute-start.8 = (bf16[128,1024]{1,0:T(8,128)(2,1)}, bf16[128,1024]{1,0:T(8,128)(2,1)S(1)}, u32[]{:S(2)}, u32[]{:S(2)}) collective-permute-start(bf16[128,1024]{1,0:T(8,128)(2,1)} %get-tuple-element.57), channel_id=1, source_target_pairs={{0,96},{8,104},{16,112},{24,120},{32,0},{40,8},{48,16},{56,24},{64... | collective-permute-start | bytes 786440 | tf_op jit(solution)/shard_map/sum_y_second/ppermute | solution.py:380
  45.6 0.0 collective-permute-done.4.refs_3_
  45.6 0.0 collective-permute-done.3.refs_2_
  45.6 0.0 copy-done.3
  45.6 2.1 %join_x.1 = (f32[128,1024]{1,0:T(8,128)S(1)}, bf16[128,1024]{1,0:T(8,128)(2,1)S(1)}) custom-call(s32[3]{0:T(128)S(1)} %pad_add_fusion.1.scal_ref, bf16[2,128,1024]{2,1,0:T(8,128)(2,1)S(1)} %copy-done.3, bf16[2,128,1024]{2,1,0:T(8,128)(2,1)} %collective-permute-done.2.refs_1_, bf16[2,128,1024]{2,1,0:T(8,128)(2,1)} %collective-permute-done.3.refs_2_, ...), custom_call_target="tpu_custom_call" | custom-call | flops 1000000 | bytes 65536 | tf_op jit(solution)/shard_map/sum_x_first/join_x/pallas_call | solution.py:89
  47.7 1.7 %collective-permute-start.6 = (bf16[128,1024]{1,0:T(8,128)(2,1)S(1)}, bf16[128,1024]{1,0:T(8,128)(2,1)S(1)}, u32[]{:S(2)}, u32[]{:S(2)}) collective-permute-start(bf16[128,1024]{1,0:T(8,128)(2,1)S(1)} %get-tuple-element.62), channel_id=1, source_target_pairs={{0,16},{8,24},{16,0},{24,8},{32,48},{40,56},{48,32},{56,40},{64,80... | collective-permute-start | bytes 786440 | tf_op jit(solution)/shard_map/sum_x_first/ppermute | solution.py:380
  49.3 0.1 collective-permute-done.7.refs_1_
  49.4 6.0 %collective-permute-done.9.refs_3_ = bf16[128,1024]{1,0:T(8,128)(2,1)S(1)} collective-permute-done((bf16[128,1024]{1,0:T(8,128)(2,1)}, bf16[128,1024]{1,0:T(8,128)(2,1)S(1)}, u32[]{:S(2)}, u32[]{:S(2)}) %collective-permute-start.9) | collective-permute-done | bytes 262176 | tf_op jit(solution)/shard_map/sum_y_second/ppermute | solution.py:380
  55.5 0.0 collective-permute-done.8.refs_2_
  55.5 0.0 copy-done.4
  55.5 1.1 norm_sum.1.refs_2_
  56.6 0.0 collective-permute-done.6.refs_1_
  56.6 1.0 norm_both.1.refs_0_.refs_7_
  57.6 3.3 %collective-permute-start.10 = (bf16[2,128,1024]{2,1,0:T(8,128)(2,1)S(1)}, bf16[2,128,1024]{2,1,0:T(8,128)(2,1)S(1)}, u32[]{:S(2)}, u32[]{:S(2)}) collective-permute-start(bf16[2,128,1024]{2,1,0:T(8,128)(2,1)S(1)} %norm_both.1.refs_0_.refs_7_), channel_id=1, source_target_pairs={{0,1},{1,0},{2,3},{3,2},{4,5},{5,4},{6,7},{7,6},{8,9},{9,8},{10,11... | collective-permute-start | bytes 1572872 | tf_op jit(solution)/shard_map/gather/ppermute | solution.py:384
  60.9 4.0 %collective-permute-start.14 = (bf16[2,128,1024]{2,1,0:T(8,128)(2,1)S(1)}, bf16[2,128,1024]{2,1,0:T(8,128)(2,1)S(1)}, u32[]{:S(2)}, u32[]{:S(2)}) collective-permute-start(bf16[2,128,1024]{2,1,0:T(8,128)(2,1)S(1)} %norm_both.1.refs_0_.refs_7_), channel_id=1, source_target_pairs={{0,6},{1,7},{2,0},{3,1},{4,2},{5,3},{6,4},{7,5},{8,14},{9,15},{10,... | collective-permute-start | bytes 1572872 | tf_op jit(solution)/shard_map/gather/ppermute | solution.py:384
  64.9 0.0 collective-permute-start.13
  64.9 0.0 slice-done
  64.9 6.2 %own_keys.1 = (f32[512,1024]{1,0:T(8,128)S(1)}, f32[256,1024]{1,0:T(8,128)S(1)}, bf16[256,1024]{1,0:T(8,128)(2,1)S(1)}, bf16[256,1024]{1,0:T(8,128)(2,1)S(1)}) custom-call(s32[2,12]{1,0:T(2,128)S(1)} %pad_add_fusion.scal_ref, bf16[2,128,1024]{2,1,0:T(8,128)(2,1)S(1)} %norm_both.1.refs_0_.refs_7_, ...), custom_call_target="tpu_custom_call", output_to_operand_aliasing={{0}: (4, {})} | custom-call | flops 1000000 | bytes 65536 | tf_op jit(solution)/shard_map/own_keys/pallas_call | solution.py:183
  71.1 0.4 collective-permute-done.10.refs_2_
  71.5 4.1 %collective-permute-start.12 = (bf16[2,128,1024]{2,1,0:T(8,128)(2,1)S(1)}, bf16[2,128,1024]{2,1,0:T(8,128)(2,1)S(1)}, u32[]{:S(2)}, u32[]{:S(2)}) collective-permute-start(bf16[2,128,1024]{2,1,0:T(8,128)(2,1)S(1)} %collective-permute-done.10.refs_2_), channel_id=1, source_target_pairs={{0,6},{1,7},{2,0},{3,1},{4,2},{5,3},{6,4},{7,5},{8,14},{9,15},{10,... | collective-permute-start | bytes 1572872 | tf_op jit(solution)/shard_map/gather/ppermute | solution.py:384
  75.6 0.0 collective-permute-start.11
  75.6 0.1 collective-permute-done.14.refs_1_
  75.6 3.4 %collective-permute-done.13.refs_0_ = bf16[2,128,1024]{2,1,0:T(8,128)(2,1)S(1)} collective-permute-done((bf16[2,128,1024]{2,1,0:T(8,128)(2,1)S(1)}, bf16[2,128,1024]{2,1,0:T(8,128)(2,1)S(1)}, u32[]{:S(2)}, u32[]{:S(2)}) %collective-permute-start.13) | collective-permute-done | bytes 524320 | tf_op jit(solution)/shard_map/gather/ppermute | solution.py:384
  79.1 0.0 collective-permute-start.16
  79.1 9.5 %own_sides.1 = (f32[512,1024]{1,0:T(8,128)S(1)}, f32[256,1024]{1,0:T(8,128)S(1)}) custom-call(s32[2,12]{1,0:T(2,128)S(1)} %pad_add_fusion.scal_ref, bf16[2,128,1024]{2,1,0:T(8,128)(2,1)S(1)} %collective-permute-done.13.refs_0_, bf16[2,128,1024]{2,1,0:T(8,128)(2,1)S(1)} %collective-permute-done.14.refs_1_, ...), custom_call_target="tpu_custom_call", output_to_operand_aliasing={{0}: (6, {}), {1}: (8, {})} | custom-call | flops 1000000 | bytes 65536 | tf_op jit(solution)/shard_map/own_sides/pallas_call | solution.py:183
  88.5 0.0 collective-permute-done.12.refs_1_
  88.5 3.1 %collective-permute-done.11.refs_0_ = bf16[2,128,1024]{2,1,0:T(8,128)(2,1)S(1)} collective-permute-done((bf16[2,128,1024]{2,1,0:T(8,128)(2,1)S(1)}, bf16[2,128,1024]{2,1,0:T(8,128)(2,1)S(1)}, u32[]{:S(2)}, u32[]{:S(2)}) %collective-permute-start.11) | collective-permute-done | bytes 524320 | tf_op jit(solution)/shard_map/gather/ppermute | solution.py:384
  91.7 0.4 collective-permute-start.15
  92.1 8.3 %collective-permute-done.16.refs_2_ = bf16[2,128,1024]{2,1,0:T(8,128)(2,1)S(1)} collective-permute-done((bf16[2,128,1024]{2,1,0:T(8,128)(2,1)S(1)}, bf16[2,128,1024]{2,1,0:T(8,128)(2,1)S(1)}, u32[]{:S(2)}, u32[]{:S(2)}) %collective-permute-start.16) | collective-permute-done | bytes 524320 | tf_op jit(solution)/shard_map/gather/ppermute | solution.py:384
  100.4 9.5 %near_sides.1 = (f32[512,1024]{1,0:T(8,128)S(1)}, f32[256,1024]{1,0:T(8,128)S(1)}) custom-call(s32[2,12]{1,0:T(2,128)S(1)} %pad_add_fusion.scal_ref, bf16[2,128,1024]{2,1,0:T(8,128)(2,1)S(1)} %collective-permute-done.11.refs_0_, bf16[2,128,1024]{2,1,0:T(8,128)(2,1)S(1)} %collective-permute-done.12.refs_1_, ...), custom_call_target="tpu_custom_call", output_to_operand_aliasing={{0}: (6, {}), {1}: (8, {})} | custom-call | flops 1000000 | bytes 65536 | tf_op jit(solution)/shard_map/near_sides/pallas_call | solution.py:183
  109.9 0.0 collective-permute-done.15.refs_0_
  109.9 9.8 %far_finish.1 = (bf16[2,128,1024]{2,1,0:T(8,128)(2,1)}, bf16[512,1024]{1,0:T(8,128)(2,1)}) custom-call(s32[2,12]{1,0:T(2,128)S(1)} %pad_add_fusion.scal_ref, bf16[2,128,1024]{2,1,0:T(8,128)(2,1)S(1)} %collective-permute-done.15.refs_0_, bf16[1024,4096]{1,0:T(8,128)(2,1)S(1)} %bitcast.18, bf16[512,1024]{1,0:T(8,128)(2,1)S(1)} %get-tuple-element.67.refs_2_.refs_4_, ...), custom_call_target="tpu_custom_call" | custom-call | flops 1000000 | bytes 65536 | tf_op jit(solution)/shard_map/far_finish/pallas_call | solution.py:183
  (8 shorter events, 0.0 us)
Async XLA Ops:
  3.7 4.5 %collective-permute-start.1 = (bf16[4,2,128,1024]{3,2,1,0:T(8,128)(2,1)}, bf16[4,2,128,1024]{3,2,1,0:T(8,128)(2,1)S(1)}, u32[]{:S(2)}, u32[]{:S(2)}) collective-permute-start(bf16[4,2,128,1024]{3,2,1,0:T(8,128)(2,1)} %pack.2), channel_id=1, source_target_pairs={{0,8},{8,0},{16,24},{24,16},{32,40},{40,32},{48,56},{56,48},{64,72... | collective-permute-start | bytes 6291464 | tf_op jit(solution)/shard_map/sum_core/ppermute | solution.py:380
  6.8 5.8 %collective-permute-start = (bf16[4,2,128,1024]{3,2,1,0:T(8,128)(2,1)}, bf16[4,2,128,1024]{3,2,1,0:T(8,128)(2,1)S(1)}, u32[]{:S(2)}, u32[]{:S(2)}) collective-permute-start(bf16[4,2,128,1024]{3,2,1,0:T(8,128)(2,1)} %pack.3), channel_id=1, source_target_pairs={{0,8},{8,0},{16,24},{24,16},{32,40},{40,32},{48,56},{56,48},{64,72... | collective-permute-start | bytes 6291464 | tf_op jit(solution)/shard_map/sum_core/ppermute | solution.py:380
  10.8 10.6 %copy-start.5 = (s32[512]{0:T(512)S(1)}, s32[512]{0:T(512)}, u32[]{:S(2)}) copy-start(s32[512]{0:T(512)} %param.9) | copy-start | bytes 6148
  10.8 12.0 %copy-start.6 = (s32[2]{0:T(128)S(1)}, s32[2]{0:T(128)}, u32[]{:S(2)}) copy-start(s32[2]{0:T(128)} %param.8) | copy-start | bytes 28
  10.8 14.1 %copy-start.2 = (bf16[512,1024]{1,0:T(8,128)(2,1)S(1)}, bf16[512,1024]{1,0:T(8,128)(2,1)}, u32[]{:S(2)}) copy-start(bf16[512,1024]{1,0:T(8,128)(2,1)} %feats_ref.1) | copy-start | bytes 3145732
  10.8 25.6 %collective-permute-start.5 = (bf16[4,128,1024]{2,1,0:T(8,128)(2,1)}, bf16[4,128,1024]{2,1,0:T(8,128)(2,1)}, u32[]{:S(2)}, u32[]{:S(2)}) collective-permute-start(bf16[4,128,1024]{2,1,0:T(8,128)(2,1)} %over_y.1), channel_id=1, source_target_pairs={{0,16},{8,24},{16,0},{24,8},{32,48},{40,56},{48,32},{56,40},{64,80... | collective-permute-start | bytes 3145736 | tf_op jit(solution)/shard_map/sum_y_second/ppermute | solution.py:380
  15.7 28.5 %collective-permute-start.2 = (bf16[2,128,1024]{2,1,0:T(8,128)(2,1)}, bf16[2,128,1024]{2,1,0:T(8,128)(2,1)}, u32[]{:S(2)}, u32[]{:S(2)}) collective-permute-start(bf16[2,128,1024]{2,1,0:T(8,128)(2,1)} %get-tuple-element.47), channel_id=1, source_target_pairs={{0,32},{8,40},{16,48},{24,56},{32,64},{40,72},{48,80},{56,88},{64,... | collective-permute-start | bytes 1572872 | tf_op jit(solution)/shard_map/sum_x_first/ppermute | solution.py:380
  17.2 28.4 %collective-permute-start.4 = (bf16[2,128,1024]{2,1,0:T(8,128)(2,1)}, bf16[2,128,1024]{2,1,0:T(8,128)(2,1)}, u32[]{:S(2)}, u32[]{:S(2)}) collective-permute-start(bf16[2,128,1024]{2,1,0:T(8,128)(2,1)} %get-tuple-element.48), channel_id=1, source_target_pairs={{0,64},{8,72},{16,80},{24,88},{32,96},{40,104},{48,112},{56,120},{... | collective-permute-start | bytes 1572872 | tf_op jit(solution)/shard_map/sum_x_first/ppermute | solution.py:380
  20.0 25.6 %collective-permute-start.3 = (bf16[2,128,1024]{2,1,0:T(8,128)(2,1)}, bf16[2,128,1024]{2,1,0:T(8,128)(2,1)}, u32[]{:S(2)}, u32[]{:S(2)}) collective-permute-start(bf16[2,128,1024]{2,1,0:T(8,128)(2,1)} %get-tuple-element.49), channel_id=1, source_target_pairs={{0,96},{8,104},{16,112},{24,120},{32,0},{40,8},{48,16},{56,24},{64... | collective-permute-start | bytes 1572872 | tf_op jit(solution)/shard_map/sum_x_first/ppermute | solution.py:380
  24.9 3.4 %copy-start = (bf16[1024,4096]{1,0:T(8,128)(2,1)S(1)}, bf16[1024,4096]{1,0:T(8,128)(2,1)}, u32[]{:S(2)}) copy-start(bf16[1024,4096]{1,0:T(8,128)(2,1)} %refs_1_.3) | copy-start | bytes 25165828
  36.4 28.5 %slice-start = ((s8[8388608]{0:T(1024)(128)(4,1)}), s8[4194304]{0:T(1024)(128)(4,1)S(1)}, s32[]{:S(2)}) async-start(s8[8388608]{0:T(1024)(128)(4,1)} %bitcast.17), calls=%async_computation | async-start | bytes 8388608
  36.4 9.2 %copy-start.3 = (bf16[2,128,1024]{2,1,0:T(8,128)(2,1)S(1)}, bf16[2,128,1024]{2,1,0:T(8,128)(2,1)}, u32[]{:S(2)}) copy-start(bf16[2,128,1024]{2,1,0:T(8,128)(2,1)} %get-tuple-element.46.refs_0_) | copy-start | bytes 1572868
  36.4 28.5 %slice-start.1 = ((s8[8388608]{0:T(1024)(128)(4,1)}), s8[4194304]{0:T(1024)(128)(4,1)S(1)}, s32[]{:S(2)}) async-start(s8[8388608]{0:T(1024)(128)(4,1)} %bitcast.17), calls=%async_computation.1 | async-start | bytes 8388608
  39.8 15.7 %copy-start.4 = (f32[128,1024]{1,0:T(8,128)S(1)}, f32[128,1024]{1,0:T(8,128)}, u32[]{:S(2)}) copy-start(f32[128,1024]{1,0:T(8,128)} %get-tuple-element.54.refs_0_) | copy-start | bytes 1572868
  39.8 9.7 %collective-permute-start.7 = (bf16[128,1024]{1,0:T(8,128)(2,1)}, bf16[128,1024]{1,0:T(8,128)(2,1)S(1)}, u32[]{:S(2)}, u32[]{:S(2)}) collective-permute-start(bf16[128,1024]{1,0:T(8,128)(2,1)} %get-tuple-element.55), channel_id=1, source_target_pairs={{0,32},{8,40},{16,48},{24,56},{32,64},{40,72},{48,80},{56,88},{64,... | collective-permute-start | bytes 786440 | tf_op jit(solution)/shard_map/sum_y_second/ppermute | solution.py:380
  41.4 14.1 %collective-permute-start.9 = (bf16[128,1024]{1,0:T(8,128)(2,1)}, bf16[128,1024]{1,0:T(8,128)(2,1)S(1)}, u32[]{:S(2)}, u32[]{:S(2)}) collective-permute-start(bf16[128,1024]{1,0:T(8,128)(2,1)} %get-tuple-element.56), channel_id=1, source_target_pairs={{0,64},{8,72},{16,80},{24,88},{32,96},{40,104},{48,112},{56,120},{... | collective-permute-start | bytes 786440 | tf_op jit(solution)/shard_map/sum_y_second/ppermute | solution.py:380
  44.1 11.3 %collective-permute-start.8 = (bf16[128,1024]{1,0:T(8,128)(2,1)}, bf16[128,1024]{1,0:T(8,128)(2,1)S(1)}, u32[]{:S(2)}, u32[]{:S(2)}) collective-permute-start(bf16[128,1024]{1,0:T(8,128)(2,1)} %get-tuple-element.57), channel_id=1, source_target_pairs={{0,96},{8,104},{16,112},{24,120},{32,0},{40,8},{48,16},{56,24},{64... | collective-permute-start | bytes 786440 | tf_op jit(solution)/shard_map/sum_y_second/ppermute | solution.py:380
  47.7 8.9 %collective-permute-start.6 = (bf16[128,1024]{1,0:T(8,128)(2,1)S(1)}, bf16[128,1024]{1,0:T(8,128)(2,1)S(1)}, u32[]{:S(2)}, u32[]{:S(2)}) collective-permute-start(bf16[128,1024]{1,0:T(8,128)(2,1)S(1)} %get-tuple-element.62), channel_id=1, source_target_pairs={{0,16},{8,24},{16,0},{24,8},{32,48},{40,56},{48,32},{56,40},{64,80... | collective-permute-start | bytes 786440 | tf_op jit(solution)/shard_map/sum_x_first/ppermute | solution.py:380
  57.6 13.9 %collective-permute-start.10 = (bf16[2,128,1024]{2,1,0:T(8,128)(2,1)S(1)}, bf16[2,128,1024]{2,1,0:T(8,128)(2,1)S(1)}, u32[]{:S(2)}, u32[]{:S(2)}) collective-permute-start(bf16[2,128,1024]{2,1,0:T(8,128)(2,1)S(1)} %norm_both.1.refs_0_.refs_7_), channel_id=1, source_target_pairs={{0,1},{1,0},{2,3},{3,2},{4,5},{5,4},{6,7},{7,6},{8,9},{9,8},{10,11... | collective-permute-start | bytes 1572872 | tf_op jit(solution)/shard_map/gather/ppermute | solution.py:384
  60.9 14.8 %collective-permute-start.14 = (bf16[2,128,1024]{2,1,0:T(8,128)(2,1)S(1)}, bf16[2,128,1024]{2,1,0:T(8,128)(2,1)S(1)}, u32[]{:S(2)}, u32[]{:S(2)}) collective-permute-start(bf16[2,128,1024]{2,1,0:T(8,128)(2,1)S(1)} %norm_both.1.refs_0_.refs_7_), channel_id=1, source_target_pairs={{0,6},{1,7},{2,0},{3,1},{4,2},{5,3},{6,4},{7,5},{8,14},{9,15},{10,... | collective-permute-start | bytes 1572872 | tf_op jit(solution)/shard_map/gather/ppermute | solution.py:384
  64.9 14.2 %collective-permute-start.13 = (bf16[2,128,1024]{2,1,0:T(8,128)(2,1)S(1)}, bf16[2,128,1024]{2,1,0:T(8,128)(2,1)S(1)}, u32[]{:S(2)}, u32[]{:S(2)}) collective-permute-start(bf16[2,128,1024]{2,1,0:T(8,128)(2,1)S(1)} %norm_both.1.refs_0_.refs_7_), channel_id=1, source_target_pairs={{0,2},{1,3},{2,4},{3,5},{4,6},{5,7},{6,0},{7,1},{8,10},{9,11},{10,... | collective-permute-start | bytes 1572872 | tf_op jit(solution)/shard_map/gather/ppermute | solution.py:384
  71.5 17.0 %collective-permute-start.12 = (bf16[2,128,1024]{2,1,0:T(8,128)(2,1)S(1)}, bf16[2,128,1024]{2,1,0:T(8,128)(2,1)S(1)}, u32[]{:S(2)}, u32[]{:S(2)}) collective-permute-start(bf16[2,128,1024]{2,1,0:T(8,128)(2,1)S(1)} %collective-permute-done.10.refs_2_), channel_id=1, source_target_pairs={{0,6},{1,7},{2,0},{3,1},{4,2},{5,3},{6,4},{7,5},{8,14},{9,15},{10,... | collective-permute-start | bytes 1572872 | tf_op jit(solution)/shard_map/gather/ppermute | solution.py:384
  75.6 16.1 %collective-permute-start.11 = (bf16[2,128,1024]{2,1,0:T(8,128)(2,1)S(1)}, bf16[2,128,1024]{2,1,0:T(8,128)(2,1)S(1)}, u32[]{:S(2)}, u32[]{:S(2)}) collective-permute-start(bf16[2,128,1024]{2,1,0:T(8,128)(2,1)S(1)} %collective-permute-done.10.refs_2_), channel_id=1, source_target_pairs={{0,2},{1,3},{2,4},{3,5},{4,6},{5,7},{6,0},{7,1},{8,10},{9,11},{10,... | collective-permute-start | bytes 1572872 | tf_op jit(solution)/shard_map/gather/ppermute | solution.py:384
  79.1 21.3 %collective-permute-start.16 = (bf16[2,128,1024]{2,1,0:T(8,128)(2,1)S(1)}, bf16[2,128,1024]{2,1,0:T(8,128)(2,1)S(1)}, u32[]{:S(2)}, u32[]{:S(2)}) collective-permute-start(bf16[2,128,1024]{2,1,0:T(8,128)(2,1)S(1)} %collective-permute-done.13.refs_0_), channel_id=1, source_target_pairs={{0,2},{1,3},{2,4},{3,5},{4,6},{5,7},{6,0},{7,1},{8,10},{9,11},{10,... | collective-permute-start | bytes 1572872 | tf_op jit(solution)/shard_map/gather/ppermute | solution.py:384
  91.7 18.2 %collective-permute-start.15 = (bf16[2,128,1024]{2,1,0:T(8,128)(2,1)S(1)}, bf16[2,128,1024]{2,1,0:T(8,128)(2,1)S(1)}, u32[]{:S(2)}, u32[]{:S(2)}) collective-permute-start(bf16[2,128,1024]{2,1,0:T(8,128)(2,1)S(1)} %collective-permute-done.12.refs_1_), channel_id=1, source_target_pairs={{0,6},{1,7},{2,0},{3,1},{4,2},{5,3},{6,4},{7,5},{8,14},{9,15},{10,... | collective-permute-start | bytes 1572872 | tf_op jit(solution)/shard_map/gather/ppermute | solution.py:384
  100.4 9.5 %copy-start.1 = (bf16[1024,1024]{1,0:T(8,128)(2,1)S(1)}, bf16[1024,1024]{1,0:T(8,128)(2,1)}, u32[]{:S(2)}) copy-start(bf16[1024,1024]{1,0:T(8,128)(2,1)} %refs_11_.1) | copy-start | bytes 6291460
